TPU v7x, 256 devices: a whole 4x4x8 slice. The times are simulated.
256 devices in a mesh: wide: 64 (over z, x_hi, y), narrow: 4 (over x_lo, core).
Axes of the slice: x: 4 (x_hi: 2, x_lo: 2; x = x_hi * 2 + x_lo), y: 4, z: 8, core: 2. Of those that a mesh axis runs over, the one named last changes fastest.
Arguments:
- amplitudes: float32 [1536, 32768], P('narrow', 'wide'), may hold values from -6 to 6
- integrals: float32 [512, 64, 64, 64], P('wide', 'narrow'), may hold values from -0.09375 to 0.09375
- send_tiles: int32 [64, 64], P('wide'), may hold values from 0 to 7
- task_slots: int32 [512, 64], P('wide'), may hold values from 0 to 63, as said below
- row_gap: float32 [32768], P('wide'), may hold values from 0.5 to 4
- column_gap: float32 [1536], P('narrow'), may hold values from 0.5 to 4
Outputs:
- residual: float32 [1536, 32768], P('narrow', 'wide')
- new_amplitudes: float32 [1536, 32768], P('narrow', 'wide')
Inputs may be any that keep to these rules, and one draw needn't show every extreme that they name: `task_slots`: within each row tile the 64 entries are distinct; among the 8 row tiles of one owner every wide index is named exactly 8 times.
All inputs are finite; a program needn't handle non-finite values.
Results may differ from a plain program's by a relative error of at most 0.0003.
Values sent between devices are 32-bit elements; how exact they have to be, the bound alone decides.
No kernel may reach another device: no remote copies, remote signals or barrier semaphores. Data moves between devices by JAX's collectives and lax.ppermute only.
A program may use at most 128 MiB of HBM per device.

v0:
```python
import jax
import jax.numpy as jnp
from jax import lax
from jax.sharding import PartitionSpec as P


def contract_tiles(source_tiles, slot_rows, integral_rows):

    def one_tile(inputs):
        slots, tile_integrals = inputs
        picked = jnp.take(source_tiles, slots, axis=1)
        return jnp.einsum("ckv,kuv->cu", picked, tile_integrals, precision=lax.Precision.HIGHEST)

    mapped = lax.map(one_tile, (slot_rows, integral_rows))
    return jnp.transpose(mapped, (1, 0, 2))


def body(amplitudes, integrals, send_tiles, task_slots, row_gap, column_gap):
    col_count = amplitudes.shape[0]
    tile_count = integrals.shape[0]
    tile_width = integrals.shape[2]
    local_terms = integrals.shape[1]
    owned = amplitudes.reshape(col_count, tile_count, tile_width)
    outgoing = jnp.take(owned, send_tiles[0], axis=1)
    received = lax.all_to_all(outgoing, "wide", split_axis=1, concat_axis=1, tiled=True)
    first_term = lax.axis_index("narrow") * local_terms
    my_slots = lax.dynamic_slice_in_dim(task_slots, first_term, local_terms, 1)
    piece = lax.all_gather(received, "narrow", axis=0, tiled=True)
    rows_here = piece.shape[0]
    summed = contract_tiles(piece, my_slots, integrals)
    partial_value = summed.reshape(rows_here, tile_count * tile_width)
    cycle = lax.psum_scatter(partial_value, "narrow", scatter_dimension=0, tiled=True)
    gap = column_gap[:, None] + row_gap[None, :]
    residual = cycle - gap * amplitudes
    new_amplitudes = amplitudes + residual / gap
    return (residual, new_amplitudes)


def solution(mesh):
    placed = (
        P("narrow", "wide"),
        P("wide", "narrow", None, None),
        P("wide", None),
        P("wide", None),
        P("wide"),
        P("narrow"),
    )
    return jax.shard_map(
        body,
        mesh=mesh,
        in_specs=placed,
        out_specs=(P("narrow", "wide"), P("narrow", "wide")),
        check_vma=False,
    )
```

profile of v0, /device:TPU:8, one launch (start us, length us, event | category | flops | bytes accessed | tf_op | source)
XLA Modules:
  0.0 598.6 jit_solution(15647367757949063025)
XLA Ops:
  7.2 0.0 copy-start
  7.2 0.0 all-gather.2.cloned.1.call-start
  7.2 0.7 fusion.18
  7.9 0.7 compare_and_fusion.1
  8.5 1.4 copy.10
  10.0 3.6 gather_fusion.1
  13.6 3.6 select_bitcast_fusion
  17.2 155.4 %all_to_all.5 = f32[384,64,64]{0,2,1:T(8,128)} all-to-all(f32[384,64,64]{0,2,1:T(8,128)S(1)} %select_bitcast_fusion), channel_id=1, replica_groups=mesh['wide'=64,'narrow'=4] {'wide'}, dimensions={1} | all-to-all | bytes 12582912 | tf_op jit(solution)/shard_map/all_to_all | solution.py:25
  172.5 0.0 all-gather.2.cloned.1.call-update
  172.5 0.0 reduce-scatter.2.cloned.1.call-start
  172.6 0.0 copy-done
  172.6 0.1 constant_dynamic-slice_fusion.1
  172.7 219.7 %all-gather.2.cloned.1.call-done = f32[1536,64,64]{0,2,1:T(8,128)} async-done(((f32[384,64,64]{0,2,1:T(8,128)}), f32[1536,64,64]{0,2,1:T(8,128)}) %all-gather.2.cloned.1.call-update) | async-done | bytes 25165840 | tf_op jit(solution)/shard_map/all_gather | solution.py:28
  392.4 0.0 copy-start.1
  392.4 0.0 copy-start.2
  392.4 154.3 %while.10 = (s32[]{:T(128)}, f32[8,1536,64]{1,2,0:T(8,128)}, s32[8,16]{1,0:T(8,128)S(1)}, f32[1536,64,64]{0,2,1:T(8,128)}, f32[8,16,64,64]{3,2,1,0:T(8,128)}, /*index=5*/s32[]{:T(128)}) while((s32[]{:T(128)}, f32[8,1536,64]{1,2,0:T(8,128)}, s32[8,16]{1,0:T(8,128)S(1)}, f32[1536,64,64]{0,2,1:T(8,128)}, f32[8,16,64,64]{3,2,1,0:T(8,128)}, ...), condition=%wide.region_1.2_spmd, body=%wide.region_0.1_spmd.sunk | while | flops 1209533568 | bytes 19797420 | solution.py:14
  392.4 11.8 %gather_fusion = f32[16,1536,64]{1,2,0:T(8,128)} fusion(f32[1536,64,64]{0,2,1:T(8,128)} %get-tuple-element.90, s32[1024]{0:T(1024)S(1)} %pad_clamp_fusion.3), kind=kCustom, calls=%fused_computation.clone.1 | custom fusion | bytes 12582976 | tf_op jit(solution)/shard_map/while/body/eval_jaxpr/jit(_take)/gather | solution.py:11
  404.2 7.5 %fusion.26 = f32[8,1536,64]{1,2,0:T(8,128)} fusion(f32[8,1536,64]{1,2,0:T(8,128)} %get-tuple-element.82, s32[]{:T(128)} %get-tuple-element.81, f32[16,1536,64]{1,2,0:T(8,128)} %gather_fusion, pred[16]{0:T(512)(128)(4,1)S(1)} %compare_and_fusion.3, f32[8,16,64,64]{3,2,1,0:T(8,128)} %get-tuple-element.91), kind=kOutput, calls=%fused_computation.8.clone.1 | convolution fusion | flops 1209532416 | bytes 7210000 | tf_op jit(solution)/shard_map/while/body/eval_jaxpr/ckv,kuv->cu/dot_general | solution.py:12
  411.7 11.8 %gather_fusion = f32[16,1536,64]{1,2,0:T(8,128)} fusion(f32[1536,64,64]{0,2,1:T(8,128)} %get-tuple-element.90, s32[1024]{0:T(1024)S(1)} %pad_clamp_fusion.3), kind=kCustom, calls=%fused_computation.clone.1 | custom fusion | bytes 12582976 | tf_op jit(solution)/shard_map/while/body/eval_jaxpr/jit(_take)/gather | solution.py:11
  423.5 7.4 %fusion.26 = f32[8,1536,64]{1,2,0:T(8,128)} fusion(f32[8,1536,64]{1,2,0:T(8,128)} %get-tuple-element.82, s32[]{:T(128)} %get-tuple-element.81, f32[16,1536,64]{1,2,0:T(8,128)} %gather_fusion, pred[16]{0:T(512)(128)(4,1)S(1)} %compare_and_fusion.3, f32[8,16,64,64]{3,2,1,0:T(8,128)} %get-tuple-element.91), kind=kOutput, calls=%fused_computation.8.clone.1 | convolution fusion | flops 1209532416 | bytes 7210000 | tf_op jit(solution)/shard_map/while/body/eval_jaxpr/ckv,kuv->cu/dot_general | solution.py:12
  431.0 11.8 %gather_fusion = f32[16,1536,64]{1,2,0:T(8,128)} fusion(f32[1536,64,64]{0,2,1:T(8,128)} %get-tuple-element.90, s32[1024]{0:T(1024)S(1)} %pad_clamp_fusion.3), kind=kCustom, calls=%fused_computation.clone.1 | custom fusion | bytes 12582976 | tf_op jit(solution)/shard_map/while/body/eval_jaxpr/jit(_take)/gather | solution.py:11
  442.8 7.5 %fusion.26 = f32[8,1536,64]{1,2,0:T(8,128)} fusion(f32[8,1536,64]{1,2,0:T(8,128)} %get-tuple-element.82, s32[]{:T(128)} %get-tuple-element.81, f32[16,1536,64]{1,2,0:T(8,128)} %gather_fusion, pred[16]{0:T(512)(128)(4,1)S(1)} %compare_and_fusion.3, f32[8,16,64,64]{3,2,1,0:T(8,128)} %get-tuple-element.91), kind=kOutput, calls=%fused_computation.8.clone.1 | convolution fusion | flops 1209532416 | bytes 7210000 | tf_op jit(solution)/shard_map/while/body/eval_jaxpr/ckv,kuv->cu/dot_general | solution.py:12
  450.3 11.8 %gather_fusion = f32[16,1536,64]{1,2,0:T(8,128)} fusion(f32[1536,64,64]{0,2,1:T(8,128)} %get-tuple-element.90, s32[1024]{0:T(1024)S(1)} %pad_clamp_fusion.3), kind=kCustom, calls=%fused_computation.clone.1 | custom fusion | bytes 12582976 | tf_op jit(solution)/shard_map/while/body/eval_jaxpr/jit(_take)/gather | solution.py:11
  462.1 7.5 %fusion.26 = f32[8,1536,64]{1,2,0:T(8,128)} fusion(f32[8,1536,64]{1,2,0:T(8,128)} %get-tuple-element.82, s32[]{:T(128)} %get-tuple-element.81, f32[16,1536,64]{1,2,0:T(8,128)} %gather_fusion, pred[16]{0:T(512)(128)(4,1)S(1)} %compare_and_fusion.3, f32[8,16,64,64]{3,2,1,0:T(8,128)} %get-tuple-element.91), kind=kOutput, calls=%fused_computation.8.clone.1 | convolution fusion | flops 1209532416 | bytes 7210000 | tf_op jit(solution)/shard_map/while/body/eval_jaxpr/ckv,kuv->cu/dot_general | solution.py:12
  469.6 11.8 %gather_fusion = f32[16,1536,64]{1,2,0:T(8,128)} fusion(f32[1536,64,64]{0,2,1:T(8,128)} %get-tuple-element.90, s32[1024]{0:T(1024)S(1)} %pad_clamp_fusion.3), kind=kCustom, calls=%fused_computation.clone.1 | custom fusion | bytes 12582976 | tf_op jit(solution)/shard_map/while/body/eval_jaxpr/jit(_take)/gather | solution.py:11
  481.4 7.4 %fusion.26 = f32[8,1536,64]{1,2,0:T(8,128)} fusion(f32[8,1536,64]{1,2,0:T(8,128)} %get-tuple-element.82, s32[]{:T(128)} %get-tuple-element.81, f32[16,1536,64]{1,2,0:T(8,128)} %gather_fusion, pred[16]{0:T(512)(128)(4,1)S(1)} %compare_and_fusion.3, f32[8,16,64,64]{3,2,1,0:T(8,128)} %get-tuple-element.91), kind=kOutput, calls=%fused_computation.8.clone.1 | convolution fusion | flops 1209532416 | bytes 7210000 | tf_op jit(solution)/shard_map/while/body/eval_jaxpr/ckv,kuv->cu/dot_general | solution.py:12
  488.8 11.8 %gather_fusion = f32[16,1536,64]{1,2,0:T(8,128)} fusion(f32[1536,64,64]{0,2,1:T(8,128)} %get-tuple-element.90, s32[1024]{0:T(1024)S(1)} %pad_clamp_fusion.3), kind=kCustom, calls=%fused_computation.clone.1 | custom fusion | bytes 12582976 | tf_op jit(solution)/shard_map/while/body/eval_jaxpr/jit(_take)/gather | solution.py:11
  500.6 7.5 %fusion.26 = f32[8,1536,64]{1,2,0:T(8,128)} fusion(f32[8,1536,64]{1,2,0:T(8,128)} %get-tuple-element.82, s32[]{:T(128)} %get-tuple-element.81, f32[16,1536,64]{1,2,0:T(8,128)} %gather_fusion, pred[16]{0:T(512)(128)(4,1)S(1)} %compare_and_fusion.3, f32[8,16,64,64]{3,2,1,0:T(8,128)} %get-tuple-element.91), kind=kOutput, calls=%fused_computation.8.clone.1 | convolution fusion | flops 1209532416 | bytes 7210000 | tf_op jit(solution)/shard_map/while/body/eval_jaxpr/ckv,kuv->cu/dot_general | solution.py:12
  508.1 11.8 %gather_fusion = f32[16,1536,64]{1,2,0:T(8,128)} fusion(f32[1536,64,64]{0,2,1:T(8,128)} %get-tuple-element.90, s32[1024]{0:T(1024)S(1)} %pad_clamp_fusion.3), kind=kCustom, calls=%fused_computation.clone.1 | custom fusion | bytes 12582976 | tf_op jit(solution)/shard_map/while/body/eval_jaxpr/jit(_take)/gather | solution.py:11
  519.9 7.4 %fusion.26 = f32[8,1536,64]{1,2,0:T(8,128)} fusion(f32[8,1536,64]{1,2,0:T(8,128)} %get-tuple-element.82, s32[]{:T(128)} %get-tuple-element.81, f32[16,1536,64]{1,2,0:T(8,128)} %gather_fusion, pred[16]{0:T(512)(128)(4,1)S(1)} %compare_and_fusion.3, f32[8,16,64,64]{3,2,1,0:T(8,128)} %get-tuple-element.91), kind=kOutput, calls=%fused_computation.8.clone.1 | convolution fusion | flops 1209532416 | bytes 7210000 | tf_op jit(solution)/shard_map/while/body/eval_jaxpr/ckv,kuv->cu/dot_general | solution.py:12
  527.4 11.8 %gather_fusion = f32[16,1536,64]{1,2,0:T(8,128)} fusion(f32[1536,64,64]{0,2,1:T(8,128)} %get-tuple-element.90, s32[1024]{0:T(1024)S(1)} %pad_clamp_fusion.3), kind=kCustom, calls=%fused_computation.clone.1 | custom fusion | bytes 12582976 | tf_op jit(solution)/shard_map/while/body/eval_jaxpr/jit(_take)/gather | solution.py:11
  539.2 7.5 %fusion.26 = f32[8,1536,64]{1,2,0:T(8,128)} fusion(f32[8,1536,64]{1,2,0:T(8,128)} %get-tuple-element.82, s32[]{:T(128)} %get-tuple-element.81, f32[16,1536,64]{1,2,0:T(8,128)} %gather_fusion, pred[16]{0:T(512)(128)(4,1)S(1)} %compare_and_fusion.3, f32[8,16,64,64]{3,2,1,0:T(8,128)} %get-tuple-element.91), kind=kOutput, calls=%fused_computation.8.clone.1 | convolution fusion | flops 1209532416 | bytes 7210000 | tf_op jit(solution)/shard_map/while/body/eval_jaxpr/ckv,kuv->cu/dot_general | solution.py:12
  546.6 0.0 reduce-scatter.2.cloned.1.call-update
  546.7 41.4 %reduce-scatter.2.cloned.1.call-done = f32[384,512]{0,1:T(8,128)} async-done(((f32[1536,512]{0,1:T(8,128)}), f32[384,512]{0,1:T(8,128)}) %reduce-scatter.2.cloned.1.call-update) | async-done | bytes 786448 | tf_op jit(solution)/shard_map/reduce_scatter | solution.py:32
  588.1 0.0 copy-done.1
  588.1 0.0 copy-done.2
  588.1 1.4 fusion.17
  589.5 1.1 copy.13
  590.6 1.1 copy.14
  (26 shorter events, 0.2 us)
Async XLA Ops:
  7.2 165.4 %copy-start = (s32[8,64]{1,0:T(8,128)S(1)}, s32[8,64]{1,0:T(8,128)}, u32[]{:S(2)}) copy-start(s32[8,64]{1,0:T(8,128)} %param.11) | copy-start | bytes 6148
  7.2 385.2 %all-gather.2.cloned.1.call-start = ((), (), s32[]{:S(2)}) async-start(), calls=%async_computation.2 | async-start | bytes 31457280 | tf_op jit(solution)/shard_map/all_gather | solution.py:28
  172.5 415.5 %reduce-scatter.2.cloned.1.call-start = ((), (), s32[]{:S(2)}) async-start(), calls=%async_computation.3 | async-start | bytes 3932160 | tf_op jit(solution)/shard_map/reduce_scatter | solution.py:32
  392.4 195.7 %copy-start.1 = (f32[512]{0:T(512)S(1)}, f32[512]{0:T(512)}, u32[]{:S(2)}) copy-start(f32[512]{0:T(512)} %param.12) | copy-start | bytes 6148
  392.4 195.7 %copy-start.2 = (f32[384]{0:T(512)S(1)}, f32[384]{0:T(512)}, u32[]{:S(2)}) copy-start(f32[384]{0:T(512)} %param.13) | copy-start | bytes 4612
Sparse Core Ops, SparseCore 0:
  172.7 219.6 all-gather.1
  546.8 41.2 reduce-scatter.1
where the time goes:
time: 600 us; the launch traced here: 599 us
  waiting for transfers between devices  261 us (44%)
  blocking collectives  155 us (26%)
  local copies, waits for them, and re-layouts  102 us (17%)
  matrix products  59.6 us (10%)
  between operations  14.1 us (2%)
  other arithmetic  6.47 us (1%)
    all_gather x1, waiting for transfers between devices, body(): piece = lax.all_gather(received, 'narrow', axis=0, tiled=True)  220 us
    all_to_all x1, blocking collectives, body(): lax.all_to_all(outgoing, 'wide', split_axis=1, concat_axis=1, tiled=True)  155 us
    gather x8, local copies, waits for them, and re-layouts, one_tile(): picked = jnp.take(source_tiles, slots, axis=1)  94.4 us
    dot_general x8, matrix products, one_tile(): jnp.einsum('ckv,kuv->cu', picked, tile_integrals, precision=lax.Precision...  59.6 us
    reduce_scatter x1, waiting for transfers between devices, body(): lax.psum_scatter(partial_value, 'narrow', scatter_dimension=0, tiled=True)  41.4 us
  transfers between devices with their start and end apart: 2, of which 2 were waited for; matrix products, arithmetic and copies ran while one was open for 0% of the time, Pallas kernels for 0%

commit v1 on v0

v1 whole, which is shorter than its diff:
```python
import jax
import jax.numpy as jnp
from jax import lax
from jax.experimental import pallas as pl
from jax.experimental.pallas import tpu as pltpu
from jax.sharding import Mesh, PartitionSpec as P

OWNERS = 64
TILE = 64
ROW_TILES = 8
TERM_SHARE = 16
GROUP = 4


def split(x):
    hi = x.astype(jnp.bfloat16)
    lo = (x - hi.astype(jnp.float32)).astype(jnp.bfloat16)
    return hi, lo


def contract_kernel(spot, tiles, i0, i1, i2, i3, amp, row_gap, col_gap, res, new, held, src, acc, lhs_hi, lhs_lo, isem, asem):
    pieces = (i0, i1, i2, i3)
    per = ROW_TILES * TERM_SHARE
    icopies = [pltpu.make_async_copy(p, held.at[pl.ds(n * per, per)], isem.at[n]) for n, p in enumerate(pieces)]
    acopy = pltpu.make_async_copy(tiles, src, asem)
    for c in icopies:
        c.start()
    acopy.start()
    acc[...] = jnp.zeros_like(acc)
    low = lax.broadcasted_iota(jnp.int32, (TILE // 2, 2 * TILE), 1) < TILE
    for c in icopies:
        c.wait()
    acopy.wait()

    def step(g, carry):
        for x in range(ROW_TILES):
            for pair in range(GROUP // 2):
                s = g * GROUP + 2 * pair
                first = held[spot[x, s]]
                second = held[spot[x, s + 1]]
                top = jnp.where(low, first, pltpu.roll(second, TILE, 1))
                bottom = jnp.where(low, pltpu.roll(first, TILE, 1), second)
                for half, value in enumerate((top, bottom)):
                    hi, lo = split(value)
                    rows = pl.ds(x * TILE + half * (TILE // 2), TILE // 2)
                    cols = pl.ds(pair * 2 * TILE, 2 * TILE)
                    lhs_hi[rows, cols] = hi
                    lhs_lo[rows, cols] = lo
        block = src[pl.ds(g * GROUP, GROUP)].reshape(GROUP * TILE, src.shape[2])
        hi, lo = split(block)
        left_hi, left_lo = lhs_hi[...], lhs_lo[...]
        total = jnp.dot(left_hi, lo, preferred_element_type=jnp.float32)
        total += jnp.dot(left_lo, hi, preferred_element_type=jnp.float32)
        total += jnp.dot(left_hi, hi, preferred_element_type=jnp.float32)
        acc[...] += total
        return carry

    lax.fori_loop(0, OWNERS // GROUP, step, 0)
    cycle = acc[...].T
    column = jnp.broadcast_to(col_gap[...], (8, col_gap.shape[1])).T[:, :1]
    gap = column + row_gap[...]
    amplitudes = amp[...]
    residual = cycle - gap * amplitudes
    res[...] = residual
    new[...] = amplitudes + residual / gap


def contract(spot, tiles, pieces, amp, row_gap, col_gap):
    cols, rows = amp.shape
    shape = jax.ShapeDtypeStruct((cols, rows), jnp.float32)
    anywhere = pl.BlockSpec(memory_space=pl.ANY)
    inside = pl.BlockSpec(memory_space=pltpu.VMEM)
    return pl.pallas_call(
        contract_kernel,
        out_shape=(shape, shape),
        in_specs=[pl.BlockSpec(memory_space=pltpu.SMEM)] + [anywhere] * 5 + [inside] * 3,
        out_specs=(inside, inside),
        scratch_shapes=[
            pltpu.VMEM((4 * ROW_TILES * TERM_SHARE, TILE // 2, 2 * TILE), jnp.float32),
            pltpu.VMEM((OWNERS, TILE, cols), jnp.float32),
            pltpu.VMEM((rows, cols), jnp.float32),
            pltpu.VMEM((rows, GROUP * TILE), jnp.bfloat16),
            pltpu.VMEM((rows, GROUP * TILE), jnp.bfloat16),
            pltpu.SemaphoreType.DMA((4,)),
            pltpu.SemaphoreType.DMA,
        ],
        compiler_params=pltpu.CompilerParams(vmem_limit_bytes=48 * 1024 * 1024),
    )(spot, tiles, *pieces, amp, row_gap, col_gap)


def swap(x, axis):
    return lax.ppermute(x, axis, [(0, 1), (1, 0)])


def body(amplitudes, integrals, send_tiles, task_slots, row_gap, column_gap):
    cols, rows = amplitudes.shape
    packed = jnp.concatenate([integrals[:, :, : TILE // 2], integrals[:, :, TILE // 2 :]], axis=3)
    packed = packed.reshape(ROW_TILES * TERM_SHARE, TILE // 2, 2 * TILE)
    across = swap(packed, "xl")
    beside = swap(packed, "co")
    diagonal = swap(across, "co")
    owned = amplitudes.T.reshape(ROW_TILES, TILE, cols)
    outgoing = owned.at[send_tiles[0]].get(mode="promise_in_bounds")
    received = lax.all_to_all(outgoing, ("z", "xh", "y"), 0, 0, tiled=True)
    mine = lax.axis_index("xl") * 2 + lax.axis_index("co")
    names = jnp.arange(OWNERS, dtype=jnp.int32)
    term = jnp.sum(jnp.where(task_slots[:, None, :] == names[None, :, None], names[None, None, :], 0), axis=2)
    relative = (term // TERM_SHARE) ^ mine
    spot = (relative * ROW_TILES + jnp.arange(ROW_TILES, dtype=jnp.int32)[:, None]) * TERM_SHARE + term % TERM_SHARE
    return contract(spot, received, (packed, beside, across, diagonal), amplitudes, row_gap[None, :], column_gap[None, :])


def solution(mesh):
    fine = Mesh(mesh.devices.reshape(8, 2, 4, 2, 2), ("z", "xh", "y", "xl", "co"))
    wide, narrow = ("z", "xh", "y"), ("xl", "co")
    return jax.shard_map(
        body,
        mesh=fine,
        in_specs=(P(narrow, wide), P(wide, narrow, None, None), P(wide, None), P(wide, None), P(wide), P(narrow)),
        out_specs=(P(narrow, wide), P(narrow, wide)),
        check_vma=False,
    )
```

time: 600 us -> 179 us (0.30)
  blocking collectives: 155 us -> 0 us
  waiting for transfers between devices: 261 us -> 135 us
  local copies, waits for them, and re-layouts: 102 us -> 7.96 us
  matrix products: 59.6 us -> 0 us
  Pallas kernels: 0 us -> 17.9 us
  starting transfers between devices: 0.08 us -> 15.4 us
  between operations: 14.1 us -> 0.73 us
    all_gather x1 -> x0, waiting for transfers between devices: 220 us -> none  [body(): piece = lax.all_gather(received, 'narrow', axis=0, tiled=True)]
    all_to_all x1 -> x0, blocking collectives: 155 us -> none  [body(): lax.all_to_all(outgoing, 'wide', split_axis=1, concat_axis=1, tiled=True)]
    ppermute x0 -> x3, waiting for transfers between devices: none -> 101 us  [swap(): return lax.ppermute(x, axis, [(0, 1), (1, 0)])]
    gather x9 -> x1, local copies, waits for them, and re-layouts: 98 us -> 3.58 us  [body(): outgoing = owned.at[send_tiles[0]].get(mode='promise_in_bounds')]
    dot_general x8 -> x0, matrix products: 59.6 us -> none  [one_tile(): jnp.einsum('ckv,kuv->cu', picked, tile_integrals, precision=lax.Precision...]
    reduce_scatter x1 -> x0, waiting for transfers between devices: 41.4 us -> none  [body(): lax.psum_scatter(partial_value, 'narrow', scatter_dimension=0, tiled=True)]
    all_to_all x0 -> x1, waiting for transfers between devices: none -> 33.9 us  [body(): received = lax.all_to_all(outgoing, ('z', 'xh', 'y'), 0, 0, tiled=True)]
    pallas_call x0 -> x1, Pallas kernels: none -> 17.9 us  [contract(): pl.pallas_call(contract_kernel, out_shape=(shape, shape), in_specs=[pl.Bl...]
  transfers between devices with their start and end apart: 2 -> 4, of which waited for: 2 -> 3; matrix products, arithmetic and copies ran while one was open for 0% -> 2% of each run, Pallas kernels for 0% -> 0%
where the time goes in v1:
time: 179 us; the launch traced here: 178 us
  waiting for transfers between devices  135 us (75%)
  Pallas kernels  17.9 us (10%)
  starting transfers between devices  15.4 us (9%)
  local copies, waits for them, and re-layouts  7.96 us (4%)
    ppermute x3, waiting for transfers between devices, swap(): return lax.ppermute(x, axis, [(0, 1), (1, 0)])  101 us
    all_to_all x1, waiting for transfers between devices, body(): received = lax.all_to_all(outgoing, ('z', 'xh', 'y'), 0, 0, tiled=True)  33.9 us
    pallas_call x1, Pallas kernels, contract(): pl.pallas_call(contract_kernel, out_shape=(shape, shape), in_specs=[pl.Bl...  17.9 us
    all_to_all x1, starting transfers between devices, body(): received = lax.all_to_all(outgoing, ('z', 'xh', 'y'), 0, 0, tiled=True)  14.7 us
    gather x1, local copies, waits for them, and re-layouts, body(): outgoing = owned.at[send_tiles[0]].get(mode='promise_in_bounds')  3.58 us
  transfers between devices with their start and end apart: 4, of which 3 were waited for; matrix products, arithmetic and copies ran while one was open for 2% of the time, Pallas kernels for 0%

profile of v1, /device:TPU:8, one launch (start us, length us, event | category | flops | bytes accessed | tf_op | source)
XLA Modules:
  0.0 178.0 jit_solution(11735654077468399564)
XLA Ops:
  0.6 1.4 copy.9
  2.0 0.7 fusion.9
  2.7 3.6 %gather_fusion = f32[64,64,384]{2,1,0:T(8,128)} fusion(f32[8,64,384]{2,1,0:T(8,128)S(1)} %bitcast.13, s32[1024]{0:T(1024)S(1)} %pad_clamp_fusion), kind=kCustom, calls=%fused_computation | custom fusion | bytes 12583168 | tf_op jit(solution)/shard_map/gather | solution.py:103
  6.3 14.7 %all-to-all-start = ((f32[64,64,384]{2,1,0:T(8,128)}), f32[64,64,384]{2,1,0:T(8,128)}, u32[]{:S(2)}, u32[]{:S(2)}) async-start(f32[64,64,384]{2,1,0:T(8,128)} %gather_fusion), calls=%async_computation | async-start | bytes 12582912 | tf_op jit(solution)/shard_map/all_to_all | solution.py:104
  21.0 3.0 %fusion.10 = (f32[8,16,32,64]{3,2,1,0:T(8,128)S(1)}, f32[8,16,32,64]{3,2,1,0:T(8,128)S(1)}) fusion(f32[8,16,64,64]{3,2,1,0:T(8,128)} %param.7), kind=kLoop, calls=%fused_computation.22 | loop fusion | bytes 4194304 | tf_op jit(solution)/shard_map/slice | solution.py:97
  24.0 0.0 copy-start.3
  24.0 0.0 copy-start.2
  24.0 0.0 copy-start
  24.0 0.0 copy-start.1
  24.0 0.6 pad_maximum_fusion
  24.6 0.7 collective-permute-start.1
  25.3 0.0 collective-permute-start
  25.3 96.4 %collective-permute-done.1.i2 = f32[128,32,128]{2,1,0:T(8,128)} collective-permute-done((f32[128,32,128]{2,1,0:T(8,128)S(1)}, f32[128,32,128]{2,1,0:T(8,128)}, u32[]{:S(2)}, u32[]{:S(2)}) %collective-permute-start.1) | collective-permute-done | bytes 2097184 | tf_op jit(solution)/shard_map/ppermute | solution.py:92
  121.8 0.0 collective-permute-start.2
  121.8 0.0 copy-done.3
  121.8 0.0 copy-done.2
  121.8 0.2 select_reduce_fusion
  122.0 0.0 collective-permute-done.i1
  122.0 4.2 %collective-permute-done.2.i3 = f32[128,32,128]{2,1,0:T(8,128)} collective-permute-done((f32[128,32,128]{2,1,0:T(8,128)}, f32[128,32,128]{2,1,0:T(8,128)}, u32[]{:S(2)}, u32[]{:S(2)}) %collective-permute-start.2) | collective-permute-done | bytes 2097184 | tf_op jit(solution)/shard_map/ppermute | solution.py:92
  126.3 33.9 %all-to-all-done.tiles = f32[64,64,384]{2,1,0:T(8,128)} async-done(((f32[64,64,384]{2,1,0:T(8,128)}), f32[64,64,384]{2,1,0:T(8,128)}, u32[]{:S(2)}, u32[]{:S(2)}) %all-to-all-start) | async-done | bytes 6291488 | tf_op jit(solution)/shard_map/all_to_all | solution.py:104
  160.2 0.0 copy-done
  160.2 0.0 copy-done.1
  160.2 17.9 %shard_map.77 = (f32[384,512]{1,0:T(8,128)}, f32[384,512]{1,0:T(8,128)}) custom-call(s32[8,64]{1,0:T(8,128)S(1)} %fusion.4.spot, f32[64,64,384]{2,1,0:T(8,128)} %all-to-all-done.tiles, f32[128,32,128]{2,1,0:T(8,128)S(1)} %bitcast.11, f32[128,32,128]{2,1,0:T(8,128)} %collective-permute-done.i1, f32[128,32,128]{2,1,0:T(8,128)} %collective-permute-done.1.i2, ...), custom_call_target="tpu_custom_call" | custom-call | tf_op jit(solution)/shard_map/pallas_call | solution.py:73
  (3 shorter events, 0.0 us)
Async XLA Ops:
  6.3 153.9 %all-to-all-start = ((f32[64,64,384]{2,1,0:T(8,128)}), f32[64,64,384]{2,1,0:T(8,128)}, u32[]{:S(2)}, u32[]{:S(2)}) async-start(f32[64,64,384]{2,1,0:T(8,128)} %gather_fusion), calls=%async_computation | async-start | bytes 12582912 | tf_op jit(solution)/shard_map/all_to_all | solution.py:104
  24.0 97.8 %copy-start.3 = (f32[384]{0:T(512)S(1)}, f32[384]{0:T(512)}, u32[]{:S(2)}) copy-start(f32[384]{0:T(512)} %param.11) | copy-start | bytes 4612
  24.0 97.8 %copy-start.2 = (s32[8,64]{1,0:T(8,128)S(1)}, s32[8,64]{1,0:T(8,128)}, u32[]{:S(2)}) copy-start(s32[8,64]{1,0:T(8,128)} %param.9) | copy-start | bytes 6148
  24.0 136.2 %copy-start = (f32[384,512]{1,0:T(8,128)S(1)}, f32[384,512]{1,0:T(8,128)}, u32[]{:S(2)}) copy-start(f32[384,512]{1,0:T(8,128)} %amp.1) | copy-start | bytes 2359300
  24.0 136.2 %copy-start.1 = (f32[512]{0:T(512)S(1)}, f32[512]{0:T(512)}, u32[]{:S(2)}) copy-start(f32[512]{0:T(512)} %param.10) | copy-start | bytes 6148
  24.6 97.1 %collective-permute-start.1 = (f32[128,32,128]{2,1,0:T(8,128)S(1)}, f32[128,32,128]{2,1,0:T(8,128)}, u32[]{:S(2)}, u32[]{:S(2)}) collective-permute-start(f32[128,32,128]{2,1,0:T(8,128)S(1)} %bitcast.9), channel_id=1, source_target_pairs={{0,2},{2,0},{1,3},{3,1},{4,6},{6,4},{5,7},{7,5},{8,10},{10,8},{9,1... | collective-permute-start | bytes 6291464 | tf_op jit(solution)/shard_map/ppermute | solution.py:92
  25.3 96.7 %collective-permute-start = (f32[128,32,128]{2,1,0:T(8,128)S(1)}, f32[128,32,128]{2,1,0:T(8,128)}, u32[]{:S(2)}, u32[]{:S(2)}) collective-permute-start(f32[128,32,128]{2,1,0:T(8,128)S(1)} %bitcast.10), channel_id=1, source_target_pairs={{0,1},{1,0},{2,3},{3,2},{4,5},{5,4},{6,7},{7,6},{8,9},{9,8},{10,11... | collective-permute-start | bytes 6291464 | tf_op jit(solution)/shard_map/ppermute | solution.py:92
  121.8 4.5 %collective-permute-start.2 = (f32[128,32,128]{2,1,0:T(8,128)}, f32[128,32,128]{2,1,0:T(8,128)}, u32[]{:S(2)}, u32[]{:S(2)}) collective-permute-start(f32[128,32,128]{2,1,0:T(8,128)} %collective-permute-done.1.i2), channel_id=1, source_target_pairs={{0,1},{1,0},{2,3},{3,2},{4,5},{5,4},{6,7},{7,6},{8,9},{9,8},{10,11... | collective-permute-start | bytes 6291464 | tf_op jit(solution)/shard_map/ppermute | solution.py:92

commit v2 on v1

v2 whole, which is shorter than its diff:
```python
import functools

import jax
import jax.numpy as jnp
from jax import lax
from jax.experimental import pallas as pl
from jax.experimental.pallas import tpu as pltpu
from jax.sharding import Mesh, PartitionSpec as P

Z, XH, Y, XL, CO = 8, 2, 4, 2, 2
PLANE = XH * Y
OWNERS = Z * PLANE
TILE = 64
ROW_TILES = 8
TERM_SHARE = 16
GROUP = 4
STEPS = ((1, -1), (2, -2), (3, -3), (0,), (4,))
MIRRORED = (True, True, True, True, False)
ANYWHERE = pl.BlockSpec(memory_space=pl.ANY)
INSIDE = pl.BlockSpec(memory_space=pltpu.VMEM)
SCALARS = pl.BlockSpec(memory_space=pltpu.SMEM)
PARAMS = pltpu.CompilerParams(vmem_limit_bytes=40 * 1024 * 1024)


def split(x):
    hi = x.astype(jnp.bfloat16)
    lo = (x - hi.astype(jnp.float32)).astype(jnp.bfloat16)
    return hi, lo


def select_kernel(parts, choice, *refs):
    sources, out, sems = refs[:-2], refs[-2], refs[-1]
    held = ROW_TILES // parts
    copies = []
    for dest in range(PLANE):
        for n in range(out.shape[1]):
            tile = choice[n, dest]
            target, sem = out.at[dest, n], sems.at[n * PLANE + dest]
            if parts == 1:
                copy = pltpu.make_async_copy(sources[n].at[tile], target, sem)
                copy.start()
                copies.append(copy)
            else:
                lower = pltpu.make_async_copy(sources[0].at[jnp.minimum(tile, held - 1)], target, sem)
                upper = pltpu.make_async_copy(sources[1].at[jnp.maximum(tile - held, 0)], target, sem)
                pl.when(tile < held)(lower.start)
                pl.when(tile >= held)(upper.start)
                copies.append(lower)
    for copy in copies:
        copy.wait()


def select(choice, sources, parts=1):
    owners = len(sources) // parts
    return pl.pallas_call(
        functools.partial(select_kernel, parts),
        out_shape=jax.ShapeDtypeStruct((PLANE, owners) + sources[0].shape[1:], jnp.float32),
        in_specs=[SCALARS] + [ANYWHERE] * len(sources),
        out_specs=ANYWHERE,
        scratch_shapes=[pltpu.SemaphoreType.DMA((PLANE * owners,))],
    )(choice, *sources)


def prepare_kernel(spot, i0, i1, i2, i3, out_hi, out_lo, held, sems):
    per = ROW_TILES * TERM_SHARE
    g = pl.program_id(0)

    @pl.when(g == 0)
    def _():
        copies = [
            pltpu.make_async_copy(piece, held.at[pl.ds(n * per, per)], sems.at[n])
            for n, piece in enumerate((i0, i1, i2, i3))
        ]
        for copy in copies:
            copy.start()
        for copy in copies:
            copy.wait()

    low = lax.broadcasted_iota(jnp.int32, (TILE // 2, 2 * TILE), 1) < TILE
    for x in range(ROW_TILES):
        for pair in range(GROUP // 2):
            s = g * GROUP + 2 * pair
            first = held[spot[x, s]]
            second = held[spot[x, s + 1]]
            top = jnp.where(low, first, pltpu.roll(second, TILE, 1))
            bottom = jnp.where(low, pltpu.roll(first, TILE, 1), second)
            for half, value in enumerate((top, bottom)):
                hi, lo = split(value)
                rows = pl.ds(x * TILE + half * (TILE // 2), TILE // 2)
                cols = pl.ds(pair * 2 * TILE, 2 * TILE)
                out_hi[rows, cols] = hi
                out_lo[rows, cols] = lo


def prepare(spot, pieces):
    rows, width = ROW_TILES * TILE, GROUP * TILE
    shape = jax.ShapeDtypeStruct((rows, OWNERS * TILE), jnp.bfloat16)
    block = pl.BlockSpec((rows, width), lambda g: (0, g))
    return pl.pallas_call(
        prepare_kernel,
        grid=(OWNERS // GROUP,),
        out_shape=(shape, shape),
        in_specs=[SCALARS] + [ANYWHERE] * 4,
        out_specs=(block, block),
        scratch_shapes=[
            pltpu.VMEM((4 * ROW_TILES * TERM_SHARE, TILE // 2, 2 * TILE), jnp.float32),
            pltpu.SemaphoreType.DMA((4,)),
        ],
        compiler_params=PARAMS,
    )(spot, *pieces)


def product(left_hi, left_lo, right):
    hi, lo = split(right)
    total = jnp.dot(left_hi, lo, preferred_element_type=jnp.float32)
    total += jnp.dot(left_lo, hi, preferred_element_type=jnp.float32)
    return total + jnp.dot(left_hi, hi, preferred_element_type=jnp.float32)


def step_kernel(mirrored, has_total, half, tiles, left_hi, left_lo, *refs):
    out = refs[-1]
    if has_total:
        out[...] = refs[0][...]
    else:
        out[...] = jnp.zeros_like(out)
    depth = left_hi.shape[1] // XH
    values = tiles[...].reshape(XH, depth, tiles.shape[-1])
    for xh in range(XH):
        part = pl.ds(xh * depth, depth)
        which = half[0] ^ xh if mirrored else 0
        out[which] += product(left_hi[:, part], left_lo[:, part], values[xh])


def step(mirrored, index, half, tiles, left, total):
    rows, cols = left[0].shape[0], tiles.shape[-1]
    depth = PLANE * tiles.shape[1] * TILE
    shape = jax.ShapeDtypeStruct((2, rows, cols), jnp.float32)
    block = pl.BlockSpec((rows, depth), lambda g: (0, index))
    whole = pl.BlockSpec((2, rows, cols), lambda g: (0, 0, 0))
    tile_block = pl.BlockSpec(tiles.shape, lambda g: (0, 0, 0, 0))
    has_total = total is not None
    return pl.pallas_call(
        functools.partial(step_kernel, mirrored, has_total),
        grid=(1,),
        out_shape=shape,
        in_specs=[SCALARS, tile_block, block, block] + [whole] * has_total,
        out_specs=whole,
        compiler_params=PARAMS,
    )(half, tiles, *left, *([total] if has_total else []))


def last_kernel(tiles, left_hi, left_lo, total, other, amp, row_gap, col_gap, res, new):
    values = tiles[...].reshape(left_hi.shape[1], tiles.shape[-1])
    cycle = (total[0] + other[...] + product(left_hi[...], left_lo[...], values)).T
    column = jnp.broadcast_to(col_gap[...], (8, col_gap.shape[1])).T[:, :1]
    gap = column + row_gap[...]
    amplitudes = amp[...]
    residual = cycle - gap * amplitudes
    res[...] = residual
    new[...] = amplitudes + residual / gap


def last(index, tiles, left, total, other, amp, row_gap, col_gap):
    rows, cols = left[0].shape[0], tiles.shape[-1]
    depth = PLANE * tiles.shape[1] * TILE
    shape = jax.ShapeDtypeStruct((cols, rows), jnp.float32)
    block = pl.BlockSpec((rows, depth), lambda g: (0, index))

    def full(x):
        return pl.BlockSpec(x.shape, lambda g: (0,) * x.ndim)

    return pl.pallas_call(
        last_kernel,
        grid=(1,),
        out_shape=(shape, shape),
        in_specs=[full(tiles), block, block, pl.BlockSpec((1, rows, cols), lambda g: (0, 0, 0)), full(other), full(amp), full(row_gap), full(col_gap)],
        out_specs=(full(shape), full(shape)),
        compiler_params=PARAMS,
    )(tiles, *left, total, other, amp, row_gap, col_gap)


def swap(x, axis):
    return lax.ppermute(x, axis, [(0, 1), (1, 0)])


def shift(x, by):
    return lax.ppermute(x, "z", [(i, (i + by) % Z) for i in range(Z)])


def exchange(x, mirrored):
    if not mirrored:
        return lax.all_to_all(x, ("xh", "y"), 0, 0, tiled=True)
    groups = [[(xh * Y + y) * XL + (xh ^ d) for xh in range(XH) for y in range(Y)] for d in range(XL)]
    return lax.all_to_all(x, ("xh", "y", "xl"), 0, 0, axis_index_groups=groups, tiled=True)


def body(amplitudes, integrals, send_tiles, task_slots, row_gap, column_gap):
    cols, rows = amplitudes.shape
    z, half = lax.axis_index("z"), lax.axis_index("xh")
    half = half[None].astype(jnp.int32)

    owned = amplitudes.T.reshape(ROW_TILES, TILE, cols)
    packed = jnp.concatenate([integrals[:, :, : TILE // 2], integrals[:, :, TILE // 2 :]], axis=3)
    packed = packed.reshape(ROW_TILES * TERM_SHARE, TILE // 2, 2 * TILE)
    across = swap(packed, "xl")
    beside = swap(packed, "co")
    diagonal = swap(across, "co")

    asked = lax.all_gather(send_tiles[0].reshape(Z, PLANE), "z", axis=0)
    asked = lax.dynamic_index_in_dim(asked, z, 1, keepdims=False)

    held = ROW_TILES // 2
    ring = {0: owned}
    for t in range(1, Z // 2):
        ring[-t] = shift(ring[1 - t], 1)
        ring[t] = shift(ring[t - 1], -1)
    far = (shift(ring[1 - Z // 2][:held], 1), shift(ring[Z // 2 - 1][held:], -1))

    order, received = [], []
    for offsets, mirrored in zip(STEPS, MIRRORED):
        places = (z + jnp.array(offsets, jnp.int32)) % Z
        choice = asked[places]
        sources = far if offsets == (Z // 2,) else [ring[o] for o in offsets]
        outgoing = select(choice, sources, len(sources) // len(offsets))
        received.append(exchange(outgoing, mirrored))
        order.append((places[None, :] * PLANE + jnp.arange(PLANE, dtype=jnp.int32)[:, None]).reshape(-1))
    order = jnp.concatenate(order)

    mine = lax.axis_index("xl") * CO + lax.axis_index("co")
    terms = jnp.arange(OWNERS, dtype=jnp.int32)
    term = jnp.sum(jnp.where(task_slots[:, None, :] == order[None, :, None], terms[None, None, :], 0), axis=2)
    relative = (term // TERM_SHARE) ^ mine
    spot = (relative * ROW_TILES + jnp.arange(ROW_TILES, dtype=jnp.int32)[:, None]) * TERM_SHARE + term % TERM_SHARE
    left = prepare(spot, (packed, beside, across, diagonal))

    total = None
    for n, index in ((3, 6), (0, 0), (1, 1), (2, 2)):
        total = step(MIRRORED[n], index, half, received[n], left, total)
    other = swap(total[1], "xl")
    return last(7, received[4], left, total, other, amplitudes, row_gap[None, :], column_gap[None, :])


def solution(mesh):
    fine = Mesh(mesh.devices.reshape(Z, XH, Y, XL, CO), ("z", "xh", "y", "xl", "co"))
    wide, narrow = ("z", "xh", "y"), ("xl", "co")
    return jax.shard_map(
        body,
        mesh=fine,
        in_specs=(P(narrow, wide), P(wide, narrow, None, None), P(wide, None), P(wide, None), P(wide), P(narrow)),
        out_specs=(P(narrow, wide), P(narrow, wide)),
        check_vma=False,
    )
```

time: 179 us -> 376 us (2.10)
  Pallas kernels: 17.9 us -> 227 us
  waiting for transfers between devices: 135 us -> 27.7 us
  starting transfers between devices: 15.4 us -> 52.8 us
  blocking collectives: 0 us -> 35 us
  local copies, waits for them, and re-layouts: 7.96 us -> 27.2 us
    pallas_call x1 -> x11, Pallas kernels: 17.9 us -> 227 us  [the longest x5 200 us: select(): pl.pallas_call(functools.partial(select_kernel, parts), out_shape=jax.Sha...]
    ppermute x3 -> x4, waiting for transfers between devices: 101 us -> 0.01 us  [swap(): return lax.ppermute(x, axis, [(0, 1), (1, 0)])]
    all_gather x0 -> x1, blocking collectives: none -> 35 us  [body(): asked = lax.all_gather(send_tiles[0].reshape(Z, PLANE), 'z', axis=0)]
    all_to_all x1 -> x5, waiting for transfers between devices: 33.9 us -> 8.93 us  [the longest x1 8.92 us: exchange(): return lax.all_to_all(x, ('xh', 'y'), 0, 0, tiled=True)]
    all_to_all x1 -> x5, starting transfers between devices: 14.7 us -> 36.2 us  [the longest x4 27.9 us: exchange(): lax.all_to_all(x, ('xh', 'y', 'xl'), 0, 0, axis_index_groups=groups, tile...]
    ppermute x0 -> x8, waiting for transfers between devices: none -> 18.8 us  [shift(): return lax.ppermute(x, 'z', [(i, (i + by) % Z) for i in range(Z)])]
    ppermute x0 -> x8, starting transfers between devices: none -> 15.9 us  [shift(): return lax.ppermute(x, 'z', [(i, (i + by) % Z) for i in range(Z)])]
    unnamed x9 -> x29, local copies, waits for them, and re-layouts: 1.42 us -> 13 us
  transfers between devices with their start and end apart: 4 -> 17, of which waited for: 3 -> 4; matrix products, arithmetic and copies ran while one was open for 2% -> 5% of each run, Pallas kernels for 0% -> 59%
where the time goes in v2:
time: 376 us; the launch traced here: 375 us
  Pallas kernels  227 us (60%)
  starting transfers between devices  52.8 us (14%)
  blocking collectives  35 us (9%)
  waiting for transfers between devices  27.7 us (7%)
  local copies, waits for them, and re-layouts  27.2 us (7%)
  other arithmetic  4.52 us (1%)
    pallas_call x5, Pallas kernels, select(): pl.pallas_call(functools.partial(select_kernel, parts), out_shape=jax.Sha...  200 us
    all_gather x1, blocking collectives, body(): asked = lax.all_gather(send_tiles[0].reshape(Z, PLANE), 'z', axis=0)  35 us
    all_to_all x4, starting transfers between devices, exchange(): lax.all_to_all(x, ('xh', 'y', 'xl'), 0, 0, axis_index_groups=groups, tile...  27.9 us
    ppermute x8, waiting for transfers between devices, shift(): return lax.ppermute(x, 'z', [(i, (i + by) % Z) for i in range(Z)])  18.8 us
    ppermute x8, starting transfers between devices, shift(): return lax.ppermute(x, 'z', [(i, (i + by) % Z) for i in range(Z)])  15.9 us
    unnamed x29, local copies, waits for them, and re-layouts  13 us
    pallas_call x1, Pallas kernels, prepare(): pl.pallas_call(prepare_kernel, grid=(OWNERS // GROUP,), out_shape=(shape,...  11.8 us
    pallas_call x4, Pallas kernels, step(): pl.pallas_call(functools.partial(step_kernel, mirrored, has_total), grid=...  11 us
  transfers between devices with their start and end apart: 17, of which 4 were waited for; matrix products, arithmetic and copies ran while one was open for 5% of the time, Pallas kernels for 59%

profile of v2, /device:TPU:8, one launch (start us, length us, event | category | flops | bytes accessed | tf_op | source)
XLA Modules:
  0.0 374.8 jit_solution(14474552051919919785)
XLA Ops:
  0.6 0.0 copy-start.11
  0.6 0.0 copy-start.12
  0.7 1.4 copy.17
  2.1 0.0 copy-start.8
  2.1 2.0 collective-permute-start
  4.1 4.0 %collective-permute-start.4 = (f32[8,64,384]{2,1,0:T(8,128)S(1)}, f32[8,64,384]{2,1,0:T(8,128)}, u32[]{:S(2)}, u32[]{:S(2)}) collective-permute-start(f32[8,64,384]{2,1,0:T(8,128)S(1)} %bitcast.25), channel_id=1, source_target_pairs={{0,224},{32,0},{64,32},{96,64},{128,96},{160,128},{192,160},{224,1... | collective-permute-start | bytes 2359304 | tf_op jit(solution)/shard_map/ppermute | solution.py:187
  8.1 0.5 broadcast.102
  8.6 1.3 reduce.3
  9.9 0.1 all_gather_reshape_squeeze.3
  10.0 35.0 %all_gather.3 = s32[8,8,8]{2,1,0:T(8,128)S(1)} all-gather(s32[1,8,8]{2,1,0:T(8,128)S(1)} %all_gather_reshape_squeeze.3), channel_id=1, replica_groups=mesh['z'=8,'xh'=2,'y'=4,'xl'=2,'co'=2] {'z'}, dimensions={0}, use_global_device_ids=true | all-gather | bytes 2304 | tf_op jit(solution)/shard_map/all_gather | solution.py:209
  45.0 0.5 fusion.12
  45.5 25.7 %shard_map.127 = f32[8,1,64,384]{3,2,1,0:T(8,128)} custom-call(s32[1,8]{1,0:T(1,128)} %get-tuple-element.36.choice, f32[8,64,384]{2,1,0:T(8,128)} %bitcast.26), custom_call_target="tpu_custom_call" | custom-call | tf_op jit(solution)/shard_map/pallas_call | solution.py:55
  71.2 7.1 %all-to-all-start.4 = ((f32[8,1,64,384]{3,2,1,0:T(8,128)}), f32[8,1,64,384]{3,2,1,0:T(8,128)S(1)}, u32[]{:S(2)}, u32[]{:S(2)}) async-start(f32[8,1,64,384]{3,2,1,0:T(8,128)} %shard_map.127), calls=%async_computation.4 | async-start | bytes 1572864 | tf_op jit(solution)/shard_map/all_to_all | solution.py:194
  78.4 1.1 gather_fusion.2
  79.5 4.8 %fusion.14 = (f32[8,16,32,64]{3,2,1,0:T(8,128)}, f32[8,16,32,64]{3,2,1,0:T(8,128)}) fusion(f32[8,16,64,64]{3,2,1,0:T(8,128)} %param.12), kind=kLoop, calls=%fused_computation.52 | loop fusion | bytes 4194304 | tf_op jit(solution)/shard_map/slice | solution.py:203
  84.3 49.6 %shard_map.126 = f32[8,2,64,384]{3,2,1,0:T(8,128)} custom-call(s32[2,8]{1,0:T(2,128)} %gather_fusion.2, f32[8,64,384]{2,1,0:T(8,128)} %collective-permute-done.4.refs_0_, f32[8,64,384]{2,1,0:T(8,128)} %collective-permute-done.refs_1_), custom_call_target="tpu_custom_call" | custom-call | tf_op jit(solution)/shard_map/pallas_call | solution.py:55
  133.9 0.0 all-to-all-done.4.tiles
  133.9 6.9 %all-to-all-start.3 = ((f32[8,2,64,384]{3,2,1,0:T(8,128)}), f32[8,2,64,384]{3,2,1,0:T(8,128)}, u32[]{:S(2)}, u32[]{:S(2)}) async-start(f32[8,2,64,384]{3,2,1,0:T(8,128)} %shard_map.126), calls=%async_computation.3 | async-start | bytes 3145728 | tf_op jit(solution)/shard_map/all_to_all | solution.py:194
  140.9 2.8 pad_maximum_fusion
  143.7 0.1 collective-permute-start.9
  143.8 2.3 collective-permute-start.1
  146.1 1.0 collective-permute-start.5
  147.1 1.1 gather_fusion.1
  148.2 9.4 %collective-permute-done.1.refs_1_ = f32[8,64,384]{2,1,0:T(8,128)} collective-permute-done((f32[8,64,384]{2,1,0:T(8,128)}, f32[8,64,384]{2,1,0:T(8,128)}, u32[]{:S(2)}, u32[]{:S(2)}) %collective-permute-start.1) | collective-permute-done | bytes 786464 | tf_op jit(solution)/shard_map/ppermute | solution.py:187
  157.6 0.8 collective-permute-done.5.refs_0_
  158.4 49.6 %shard_map.125 = f32[8,2,64,384]{3,2,1,0:T(8,128)} custom-call(s32[2,8]{1,0:T(2,128)} %gather_fusion.1, f32[8,64,384]{2,1,0:T(8,128)} %collective-permute-done.5.refs_0_, f32[8,64,384]{2,1,0:T(8,128)} %collective-permute-done.1.refs_1_), custom_call_target="tpu_custom_call" | custom-call | tf_op jit(solution)/shard_map/pallas_call | solution.py:55
  208.0 0.0 copy-start.13
  208.0 6.9 %all-to-all-start.2 = ((f32[8,2,64,384]{3,2,1,0:T(8,128)}), f32[8,2,64,384]{3,2,1,0:T(8,128)}, u32[]{:S(2)}, u32[]{:S(2)}) async-start(f32[8,2,64,384]{3,2,1,0:T(8,128)} %shard_map.125), calls=%async_computation.2 | async-start | bytes 3145728 | tf_op jit(solution)/shard_map/all_to_all | solution.py:194
  214.9 1.2 collective-permute-start.2
  216.1 2.0 collective-permute-start.6
  218.2 0.5 collective-permute-start.10
  218.7 1.1 gather_fusion
  219.8 8.6 %collective-permute-done.2.refs_1_ = f32[8,64,384]{2,1,0:T(8,128)} collective-permute-done((f32[8,64,384]{2,1,0:T(8,128)}, f32[8,64,384]{2,1,0:T(8,128)}, u32[]{:S(2)}, u32[]{:S(2)}) %collective-permute-start.2) | collective-permute-done | bytes 786464 | tf_op jit(solution)/shard_map/ppermute | solution.py:187
  228.4 49.6 %shard_map.124 = f32[8,2,64,384]{3,2,1,0:T(8,128)} custom-call(s32[2,8]{1,0:T(2,128)} %gather_fusion, f32[8,64,384]{2,1,0:T(8,128)} %collective-permute-done.6.refs_0_, f32[8,64,384]{2,1,0:T(8,128)} %collective-permute-done.2.refs_1_), custom_call_target="tpu_custom_call" | custom-call | tf_op jit(solution)/shard_map/pallas_call | solution.py:55
  278.0 0.0 copy-start.9
  278.1 6.9 %all-to-all-start.1 = ((f32[8,2,64,384]{3,2,1,0:T(8,128)}), f32[8,2,64,384]{3,2,1,0:T(8,128)}, u32[]{:S(2)}, u32[]{:S(2)}) async-start(f32[8,2,64,384]{3,2,1,0:T(8,128)} %shard_map.124), calls=%async_computation.1 | async-start | bytes 3145728 | tf_op jit(solution)/shard_map/all_to_all | solution.py:194
  285.0 0.1 add.176
  285.1 0.1 add.182
  285.2 0.1 add.188
  285.3 0.1 concatenate.6
  285.3 0.3 select_reduce_fusion
  285.6 1.0 slice.40
  286.7 2.1 collective-permute-start.3
  288.8 1.8 slice.41
  290.5 1.2 collective-permute-start.7
  291.8 11.8 %shard_map.123 = (bf16[512,4096]{1,0:T(8,128)(2,1)S(1)}, bf16[512,4096]{1,0:T(8,128)(2,1)}) custom-call(s32[8,64]{1,0:T(8,128)S(1)} %fusion.4.spot, f32[128,32,128]{2,1,0:T(8,128)S(1)} %bitcast.21, f32[128,32,128]{2,1,0:T(8,128)} %collective-permute-done.8.i1, f32[128,32,128]{2,1,0:T(8,128)} %collective-permute-done.9.i2, ...), custom_call_target="tpu_custom_call" | custom-call | tf_op jit(solution)/shard_map/pallas_call | solution.py:99
  303.6 3.7 copy-done.3
  307.3 1.1 shard_map.128.refs_0_
  308.4 3.3 shard_map.129.refs_0_
  311.7 3.3 shard_map.130.refs_0_
  315.1 2.2 copy-done.1
  317.3 2.2 copy-done.4
  319.4 3.3 shard_map.131.total
  322.8 0.0 copy-start.10
  322.8 0.0 copy-start.6
  322.8 0.0 copy-start.7
  322.8 0.9 slice_bitcast_fusion
  323.7 0.1 collective-permute-start.11
  323.9 25.7 %shard_map.122 = f32[8,1,64,384]{3,2,1,0:T(8,128)} custom-call(s32[1,8]{1,0:T(1,128)} %get-tuple-element.37.choice, f32[4,64,384]{2,1,0:T(8,128)} %collective-permute-done.3.refs_0_, f32[4,64,384]{2,1,0:T(8,128)} %collective-permute-done.7.refs_1_), custom_call_target="tpu_custom_call" | custom-call | tf_op jit(solution)/shard_map/pallas_call | solution.py:55
  349.5 8.3 %all-to-all-start = ((f32[8,1,64,384]{3,2,1,0:T(8,128)}), f32[8,1,64,384]{3,2,1,0:T(8,128)S(1)}, u32[]{:S(2)}, u32[]{:S(2)}) async-start(f32[8,1,64,384]{3,2,1,0:T(8,128)} %shard_map.122), calls=%async_computation | async-start | bytes 1572864 | tf_op jit(solution)/shard_map/all_to_all | solution.py:192
  357.8 8.9 %all-to-all-done.tiles = f32[8,1,64,384]{3,2,1,0:T(8,128)S(1)} async-done(((f32[8,1,64,384]{3,2,1,0:T(8,128)}), f32[8,1,64,384]{3,2,1,0:T(8,128)S(1)}, u32[]{:S(2)}, u32[]{:S(2)}) %all-to-all-start) | async-done | bytes 786464 | tf_op jit(solution)/shard_map/all_to_all | solution.py:192
  366.7 2.2 copy-done.2
  368.9 2.2 copy-done.5
  371.1 3.7 shard_map.132
  (43 shorter events, 0.2 us)
Async XLA Ops:
  0.6 77.7 %copy-start.11 = (s32[2]{0:T(128)S(1)}, s32[2]{0:T(128)}, u32[]{:S(2)}) copy-start(s32[2]{0:T(128)} %constant.117.clone) | copy-start | bytes 28
  0.6 77.7 %copy-start.12 = (s32[2]{0:T(128)S(1)}, s32[2]{0:T(128)}, u32[]{:S(2)}) copy-start(s32[2]{0:T(128)} %constant.118.clone) | copy-start | bytes 28
  2.1 43.5 %copy-start.8 = (f32[512,384]{1,0:T(8,128)}, f32[512,384]{1,0:T(8,128)S(1)}, u32[]{:S(2)}) copy-start(f32[512,384]{1,0:T(8,128)S(1)} %copy.17) | copy-start | bytes 2359300
  2.1 82.3 %collective-permute-start = (f32[8,64,384]{2,1,0:T(8,128)S(1)}, f32[8,64,384]{2,1,0:T(8,128)}, u32[]{:S(2)}, u32[]{:S(2)}) collective-permute-start(f32[8,64,384]{2,1,0:T(8,128)S(1)} %bitcast.24), channel_id=1, source_target_pairs={{0,32},{32,64},{64,96},{96,128},{128,160},{160,192},{192,224},{224... | collective-permute-start | bytes 2359304 | tf_op jit(solution)/shard_map/ppermute | solution.py:187
  4.1 80.3 %collective-permute-start.4 = (f32[8,64,384]{2,1,0:T(8,128)S(1)}, f32[8,64,384]{2,1,0:T(8,128)}, u32[]{:S(2)}, u32[]{:S(2)}) collective-permute-start(f32[8,64,384]{2,1,0:T(8,128)S(1)} %bitcast.25), channel_id=1, source_target_pairs={{0,224},{32,0},{64,32},{96,64},{128,96},{160,128},{192,160},{224,1... | collective-permute-start | bytes 2359304 | tf_op jit(solution)/shard_map/ppermute | solution.py:187
  71.2 62.7 %all-to-all-start.4 = ((f32[8,1,64,384]{3,2,1,0:T(8,128)}), f32[8,1,64,384]{3,2,1,0:T(8,128)S(1)}, u32[]{:S(2)}, u32[]{:S(2)}) async-start(f32[8,1,64,384]{3,2,1,0:T(8,128)} %shard_map.127), calls=%async_computation.4 | async-start | bytes 1572864 | tf_op jit(solution)/shard_map/all_to_all | solution.py:194
  133.9 74.1 %all-to-all-start.3 = ((f32[8,2,64,384]{3,2,1,0:T(8,128)}), f32[8,2,64,384]{3,2,1,0:T(8,128)}, u32[]{:S(2)}, u32[]{:S(2)}) async-start(f32[8,2,64,384]{3,2,1,0:T(8,128)} %shard_map.126), calls=%async_computation.3 | async-start | bytes 3145728 | tf_op jit(solution)/shard_map/all_to_all | solution.py:194
  143.7 74.5 %collective-permute-start.9 = (f32[128,32,128]{2,1,0:T(8,128)S(1)}, f32[128,32,128]{2,1,0:T(8,128)}, u32[]{:S(2)}, u32[]{:S(2)}) collective-permute-start(f32[128,32,128]{2,1,0:T(8,128)S(1)} %bitcast.19), channel_id=1, source_target_pairs={{0,2},{2,0},{1,3},{3,1},{4,6},{6,4},{5,7},{7,5},{8,10},{10,8},{9,1... | collective-permute-start | bytes 6291464 | tf_op jit(solution)/shard_map/ppermute | solution.py:183
  143.8 13.8 %collective-permute-start.1 = (f32[8,64,384]{2,1,0:T(8,128)}, f32[8,64,384]{2,1,0:T(8,128)}, u32[]{:S(2)}, u32[]{:S(2)}) collective-permute-start(f32[8,64,384]{2,1,0:T(8,128)} %collective-permute-done.refs_1_), channel_id=1, source_target_pairs={{0,32},{32,64},{64,96},{96,128},{128,160},{160,192},{192,224},{224... | collective-permute-start | bytes 2359304 | tf_op jit(solution)/shard_map/ppermute | solution.py:187
  146.1 12.3 %collective-permute-start.5 = (f32[8,64,384]{2,1,0:T(8,128)}, f32[8,64,384]{2,1,0:T(8,128)}, u32[]{:S(2)}, u32[]{:S(2)}) collective-permute-start(f32[8,64,384]{2,1,0:T(8,128)} %collective-permute-done.4.refs_0_), channel_id=1, source_target_pairs={{0,224},{32,0},{64,32},{96,64},{128,96},{160,128},{192,160},{224,1... | collective-permute-start | bytes 2359304 | tf_op jit(solution)/shard_map/ppermute | solution.py:187
  208.0 10.7 %copy-start.13 = (s32[2]{0:T(128)S(1)}, s32[2]{0:T(128)}, u32[]{:S(2)}) copy-start(s32[2]{0:T(128)} %constant.119.clone) | copy-start | bytes 28
  208.0 70.0 %all-to-all-start.2 = ((f32[8,2,64,384]{3,2,1,0:T(8,128)}), f32[8,2,64,384]{3,2,1,0:T(8,128)}, u32[]{:S(2)}, u32[]{:S(2)}) async-start(f32[8,2,64,384]{3,2,1,0:T(8,128)} %shard_map.125), calls=%async_computation.2 | async-start | bytes 3145728 | tf_op jit(solution)/shard_map/all_to_all | solution.py:194
  214.9 13.5 %collective-permute-start.2 = (f32[8,64,384]{2,1,0:T(8,128)}, f32[8,64,384]{2,1,0:T(8,128)}, u32[]{:S(2)}, u32[]{:S(2)}) collective-permute-start(f32[8,64,384]{2,1,0:T(8,128)} %collective-permute-done.1.refs_1_), channel_id=1, source_target_pairs={{0,32},{32,64},{64,96},{96,128},{128,160},{160,192},{192,224},{224... | collective-permute-start | bytes 2359304 | tf_op jit(solution)/shard_map/ppermute | solution.py:187
  216.1 12.3 %collective-permute-start.6 = (f32[8,64,384]{2,1,0:T(8,128)}, f32[8,64,384]{2,1,0:T(8,128)}, u32[]{:S(2)}, u32[]{:S(2)}) collective-permute-start(f32[8,64,384]{2,1,0:T(8,128)} %collective-permute-done.5.refs_0_), channel_id=1, source_target_pairs={{0,224},{32,0},{64,32},{96,64},{128,96},{160,128},{192,160},{224,1... | collective-permute-start | bytes 2359304 | tf_op jit(solution)/shard_map/ppermute | solution.py:187
  218.2 73.6 %collective-permute-start.8 = (f32[128,32,128]{2,1,0:T(8,128)S(1)}, f32[128,32,128]{2,1,0:T(8,128)}, u32[]{:S(2)}, u32[]{:S(2)}) collective-permute-start(f32[128,32,128]{2,1,0:T(8,128)S(1)} %bitcast.20), channel_id=1, source_target_pairs={{0,1},{1,0},{2,3},{3,2},{4,5},{5,4},{6,7},{7,6},{8,9},{9,8},{10,11... | collective-permute-start | bytes 6291464 | tf_op jit(solution)/shard_map/ppermute | solution.py:183
  218.2 73.6 %collective-permute-start.10 = (f32[128,32,128]{2,1,0:T(8,128)}, f32[128,32,128]{2,1,0:T(8,128)}, u32[]{:S(2)}, u32[]{:S(2)}) collective-permute-start(f32[128,32,128]{2,1,0:T(8,128)} %collective-permute-done.9.i2), channel_id=1, source_target_pairs={{0,1},{1,0},{2,3},{3,2},{4,5},{5,4},{6,7},{7,6},{8,9},{9,8},{10,11... | collective-permute-start | bytes 6291464 | tf_op jit(solution)/shard_map/ppermute | solution.py:183
  278.0 7.3 %copy-start.9 = (s32[8,64]{1,0:T(8,128)S(1)}, s32[8,64]{1,0:T(8,128)}, u32[]{:S(2)}) copy-start(s32[8,64]{1,0:T(8,128)} %param.14) | copy-start | bytes 6148
  278.1 37.0 %all-to-all-start.1 = ((f32[8,2,64,384]{3,2,1,0:T(8,128)}), f32[8,2,64,384]{3,2,1,0:T(8,128)}, u32[]{:S(2)}, u32[]{:S(2)}) async-start(f32[8,2,64,384]{3,2,1,0:T(8,128)} %shard_map.124), calls=%async_computation.1 | async-start | bytes 3145728 | tf_op jit(solution)/shard_map/all_to_all | solution.py:194
  286.7 37.2 %collective-permute-start.3 = (f32[4,64,384]{2,1,0:T(8,128)S(1)}, f32[4,64,384]{2,1,0:T(8,128)}, u32[]{:S(2)}, u32[]{:S(2)}) collective-permute-start(f32[4,64,384]{2,1,0:T(8,128)S(1)} %slice.40), channel_id=1, source_target_pairs={{0,32},{32,64},{64,96},{96,128},{128,160},{160,192},{192,224},{224... | collective-permute-start | bytes 1179656 | tf_op jit(solution)/shard_map/ppermute | solution.py:187
  290.5 33.3 %collective-permute-start.7 = (f32[4,64,384]{2,1,0:T(8,128)}, f32[4,64,384]{2,1,0:T(8,128)}, u32[]{:S(2)}, u32[]{:S(2)}) collective-permute-start(f32[4,64,384]{2,1,0:T(8,128)} %slice.41), channel_id=1, source_target_pairs={{0,224},{32,0},{64,32},{96,64},{128,96},{160,128},{192,160},{224,1... | collective-permute-start | bytes 1179656 | tf_op jit(solution)/shard_map/ppermute | solution.py:187
  303.6 8.1 %copy-start = (bf16[512,4096]{1,0:T(8,128)(2,1)}, bf16[512,4096]{1,0:T(8,128)(2,1)S(1)}, u32[]{:S(2)}) copy-start(bf16[512,4096]{1,0:T(8,128)(2,1)S(1)} %get-tuple-element.4.left_hi) | copy-start | bytes 12582916
  303.6 3.7 copy-start.3
  315.1 2.2 copy-start.1
  317.3 2.2 copy-start.4
  322.8 35.0 %copy-start.10 = (f32[384]{0:T(512)S(1)}, f32[384]{0:T(512)}, u32[]{:S(2)}) copy-start(f32[384]{0:T(512)} %param.16) | copy-start | bytes 4612
  322.8 44.0 %copy-start.6 = (f32[384,512]{1,0:T(8,128)S(1)}, f32[384,512]{1,0:T(8,128)}, u32[]{:S(2)}) copy-start(f32[384,512]{1,0:T(8,128)} %amp.1) | copy-start | bytes 2359300
  322.8 43.9 %copy-start.7 = (f32[512]{0:T(512)S(1)}, f32[512]{0:T(512)}, u32[]{:S(2)}) copy-start(f32[512]{0:T(512)} %param.15) | copy-start | bytes 6148
  323.7 43.0 %collective-permute-start.11 = (f32[512,384]{1,0:T(8,128)}, f32[512,384]{1,0:T(8,128)}, u32[]{:S(2)}, u32[]{:S(2)}) collective-permute-start(f32[512,384]{1,0:T(8,128)} %slice_bitcast_fusion), channel_id=1, source_target_pairs={{0,2},{2,0},{1,3},{3,1},{4,6},{6,4},{5,7},{7,5},{8,10},{10,8},{9,1... | collective-permute-start | bytes 2359304 | tf_op jit(solution)/shard_map/ppermute | solution.py:183
  349.5 17.2 %all-to-all-start = ((f32[8,1,64,384]{3,2,1,0:T(8,128)}), f32[8,1,64,384]{3,2,1,0:T(8,128)S(1)}, u32[]{:S(2)}, u32[]{:S(2)}) async-start(f32[8,1,64,384]{3,2,1,0:T(8,128)} %shard_map.122), calls=%async_computation | async-start | bytes 1572864 | tf_op jit(solution)/shard_map/all_to_all | solution.py:192
  366.7 2.2 copy-start.2
  368.9 2.2 copy-start.5

commit v3 on v2

v3 whole, which is shorter than its diff:
```python
import functools

import jax
import jax.numpy as jnp
from jax import lax
from jax.experimental import pallas as pl
from jax.experimental.pallas import tpu as pltpu
from jax.sharding import Mesh, PartitionSpec as P

Z, XH, Y, XL, CO = 8, 2, 4, 2, 2
PLANE = XH * Y
OWNERS = Z * PLANE
TILE = 64
ROW_TILES = 8
TERM_SHARE = 16
GROUP = 4
NOTE = 8
SELECT_COST = 40
STEPS = ((0,), (1, -1), (2, -2), (3, -3, 4))
MIRRORED = (True, True, True, False)
ANYWHERE = pl.BlockSpec(memory_space=pl.ANY)
IN_HBM = pl.BlockSpec(memory_space=pltpu.HBM)
INSIDE = pl.BlockSpec(memory_space=pltpu.VMEM)
SCALARS = pl.BlockSpec(memory_space=pltpu.SMEM)
PARAMS = pltpu.CompilerParams(vmem_limit_bytes=40 * 1024 * 1024)


def cost(micros):
    return pl.CostEstimate(flops=int(micros * 1e9), bytes_accessed=0, transcendentals=0)


def in_hbm(*xs):
    return [pltpu.with_memory_space_constraint(x, pltpu.HBM) for x in xs]


def split(x):
    hi = x.astype(jnp.bfloat16)
    lo = (x - hi.astype(jnp.float32)).astype(jnp.bfloat16)
    return hi, lo


def first_kernel(amp, send, out, held, sem):
    rows = amp.shape[1]
    held[pl.ds(0, rows)] = amp[...].T
    wide = jnp.pad(send[...].astype(jnp.float32), ((0, 0), (0, amp.shape[0] - OWNERS)))
    held[pl.ds(rows, NOTE)] = jnp.broadcast_to(wide, (NOTE, amp.shape[0]))
    copy = pltpu.make_async_copy(held, out, sem)
    copy.start()
    copy.wait()


def first(amp, send):
    cols, rows = amp.shape
    return pl.pallas_call(
        first_kernel,
        out_shape=jax.ShapeDtypeStruct((rows + NOTE, cols), jnp.float32),
        in_specs=[INSIDE, INSIDE],
        out_specs=IN_HBM,
        scratch_shapes=[pltpu.VMEM((rows + NOTE, cols), jnp.float32), pltpu.SemaphoreType.DMA],
    )(amp, send)


def select_kernel(base, *refs):
    owners = (len(refs) - 3)
    sources, out, notes, sems = refs[:owners], refs[owners], refs[owners + 1], refs[owners + 2]
    rows = ROW_TILES * TILE
    reads = [
        pltpu.make_async_copy(sources[n].at[pl.ds(rows, NOTE), pl.ds(0, 128)], notes.at[n], sems.at[PLANE * owners + n])
        for n in range(owners)
    ]
    for copy in reads:
        copy.start()
    copies = []
    for n in range(owners):
        reads[n].wait()
        for dest in range(PLANE):
            tile = jnp.clip(notes[n, 0, base[0] + dest].astype(jnp.int32), 0, ROW_TILES - 1)
            copy = pltpu.make_async_copy(
                sources[n].at[pl.ds(pl.multiple_of(tile * TILE, TILE), TILE)], out.at[dest, n], sems.at[n * PLANE + dest]
            )
            copy.start()
            copies.append(copy)
    for copy in copies:
        copy.wait()


def select(base, sources, micros):
    owners, cols = len(sources), sources[0].shape[1]
    return pl.pallas_call(
        select_kernel,
        out_shape=jax.ShapeDtypeStruct((PLANE, owners, TILE, cols), jnp.float32),
        in_specs=[SCALARS] + [IN_HBM] * owners,
        out_specs=INSIDE,
        scratch_shapes=[pltpu.SMEM((owners, NOTE, 128), jnp.float32), pltpu.SemaphoreType.DMA(((PLANE + 1) * owners,))],
        cost_estimate=cost(micros),
    )(base, *in_hbm(*sources))


def prepare_kernel(spot, i0, i1, i2, i3, out_hi, out_lo, held, sems):
    per = ROW_TILES * TERM_SHARE
    g = pl.program_id(0)

    @pl.when(g == 0)
    def _():
        copies = [
            pltpu.make_async_copy(piece, held.at[pl.ds(n * per, per)], sems.at[n])
            for n, piece in enumerate((i0, i1, i2, i3))
        ]
        for copy in copies:
            copy.start()
        for copy in copies:
            copy.wait()

    low = lax.broadcasted_iota(jnp.int32, (TILE // 2, 2 * TILE), 1) < TILE
    for x in range(ROW_TILES):
        for pair in range(GROUP // 2):
            s = g * GROUP + 2 * pair
            first = held[spot[x, s]]
            second = held[spot[x, s + 1]]
            top = jnp.where(low, first, pltpu.roll(second, TILE, 1))
            bottom = jnp.where(low, pltpu.roll(first, TILE, 1), second)
            for half, value in enumerate((top, bottom)):
                hi, lo = split(value)
                rows = pl.ds(x * TILE + half * (TILE // 2), TILE // 2)
                cols = pl.ds(pair * 2 * TILE, 2 * TILE)
                out_hi[rows, cols] = hi
                out_lo[rows, cols] = lo


def prepare(spot, pieces):
    rows, width = ROW_TILES * TILE, GROUP * TILE
    shape = jax.ShapeDtypeStruct((rows, OWNERS * TILE), jnp.bfloat16)
    block = pl.BlockSpec((rows, width), lambda g: (0, g))
    return pl.pallas_call(
        prepare_kernel,
        grid=(OWNERS // GROUP,),
        out_shape=(shape, shape),
        in_specs=[SCALARS] + [IN_HBM] * 4,
        out_specs=(block, block),
        scratch_shapes=[
            pltpu.VMEM((4 * ROW_TILES * TERM_SHARE, TILE // 2, 2 * TILE), jnp.float32),
            pltpu.SemaphoreType.DMA((4,)),
        ],
        compiler_params=PARAMS,
    )(spot, *in_hbm(*pieces))


def product(left_hi, left_lo, right):
    hi, lo = split(right)
    total = jnp.dot(left_hi, lo, preferred_element_type=jnp.float32)
    total += jnp.dot(left_lo, hi, preferred_element_type=jnp.float32)
    return total + jnp.dot(left_hi, hi, preferred_element_type=jnp.float32)


def steps_kernel(count, half, *refs):
    tiles, lefts, outs = refs[:count], refs[count : 3 * count], refs[3 * count :]
    for which in range(2):
        total = None
        for n in range(count):
            left_hi, left_lo = lefts[2 * n], lefts[2 * n + 1]
            depth = left_hi.shape[1] // XH
            part = pl.ds(which * depth, depth)
            value = tiles[n][half[0] ^ which].reshape(depth, tiles[n].shape[-1])
            term = product(left_hi[:, part], left_lo[:, part], value)
            total = term if total is None else total + term
        outs[which][...] = total


def column_block(rows, depth, index):
    return pl.BlockSpec((rows, depth), lambda g: (0, index))


def full(x):
    return pl.BlockSpec(x.shape, lambda g: (0,) * x.ndim)


def steps(half, tiles, indices, left, micros):
    rows, cols = left[0].shape[0], tiles[0].shape[-1]
    tiles = in_hbm(*[t.reshape(XH, Y, *t.shape[1:]) for t in tiles])
    shape = jax.ShapeDtypeStruct((rows, cols), jnp.float32)
    blocks = [column_block(rows, PLANE * t.shape[2] * TILE, index) for t, index in zip(tiles, indices)]
    return pl.pallas_call(
        functools.partial(steps_kernel, len(tiles)),
        grid=(1,),
        out_shape=(shape, shape),
        in_specs=[SCALARS] + [full(t) for t in tiles] + [block for block in blocks for _ in range(2)],
        out_specs=(full(shape), full(shape)),
        compiler_params=PARAMS,
        cost_estimate=cost(micros),
    )(half, *tiles, *(left * len(tiles)))


def last_kernel(tiles, left_hi, left_lo, total, other, amp, row_gap, col_gap, res, new):
    values = tiles[...].reshape(left_hi.shape[1], tiles.shape[-1])
    cycle = (total[...] + other[...] + product(left_hi[...], left_lo[...], values)).T
    column = jnp.broadcast_to(col_gap[...], (8, col_gap.shape[1])).T[:, :1]
    gap = column + row_gap[...]
    amplitudes = amp[...]
    residual = cycle - gap * amplitudes
    res[...] = residual
    new[...] = amplitudes + residual / gap


def last(offset, tiles, left, total, other, amp, row_gap, col_gap):
    rows, cols = left[0].shape[0], tiles.shape[-1]
    depth = PLANE * tiles.shape[1] * TILE
    (tiles,) = in_hbm(tiles)
    shape = jax.ShapeDtypeStruct((cols, rows), jnp.float32)
    block = pl.BlockSpec((pl.Element(rows), pl.Element(depth)), lambda g: (0, offset))
    return pl.pallas_call(
        last_kernel,
        grid=(1,),
        out_shape=(shape, shape),
        in_specs=[full(tiles), block, block, full(total), full(other), full(amp), full(row_gap), full(col_gap)],
        out_specs=(full(shape), full(shape)),
        compiler_params=PARAMS,
    )(tiles, *left, total, other, amp, row_gap, col_gap)


def tie_kernel(*refs):
    del refs


def tie(xs, after):
    return pl.pallas_call(
        tie_kernel,
        out_shape=[jax.ShapeDtypeStruct(x.shape, x.dtype) for x in xs],
        in_specs=[IN_HBM] * (len(xs) + len(after)),
        out_specs=[IN_HBM] * len(xs),
        input_output_aliases={n: n for n in range(len(xs))},
    )(*in_hbm(*xs, *after))


def pack_kernel(integrals, after, out):
    del after
    value = integrals[0]
    out[...] = jnp.concatenate([value[:, : TILE // 2], value[:, TILE // 2 :]], axis=2)


def pack(integrals, after):
    shape = (TERM_SHARE, TILE // 2, 2 * TILE)
    return pl.pallas_call(
        pack_kernel,
        grid=(ROW_TILES,),
        out_shape=jax.ShapeDtypeStruct((ROW_TILES * TERM_SHARE,) + shape[1:], jnp.float32),
        in_specs=[pl.BlockSpec((1,) + integrals.shape[1:], lambda x: (x, 0, 0, 0)), IN_HBM],
        out_specs=pl.BlockSpec(shape, lambda x: (x, 0, 0)),
    )(integrals, *in_hbm(after))


def swap(x, axis):
    return lax.ppermute(x, axis, [(0, 1), (1, 0)])


def shift(x, by):
    turns = [((z * CO + c), ((z + (by if c == 0 else -by)) % Z) * CO + c) for z in range(Z) for c in range(CO)]
    return lax.ppermute(x, ("z", "co"), turns)


def exchange(x, mirrored):
    if not mirrored:
        return lax.all_to_all(x, ("xh", "y"), 0, 0, tiled=True)
    groups = [[(xh * Y + y) * XL + (xh ^ d) for xh in range(XH) for y in range(Y)] for d in range(XL)]
    return lax.all_to_all(x, ("xh", "y", "xl"), 0, 0, axis_index_groups=groups, tiled=True)


def body(amplitudes, integrals, send_tiles, task_slots, row_gap, column_gap):
    z, half = lax.axis_index("z"), lax.axis_index("xh")
    core = lax.axis_index("co")
    sign = 1 - 2 * core
    base, half = (z * PLANE)[None].astype(jnp.int32), half[None].astype(jnp.int32)

    owned = first(amplitudes, send_tiles)
    packed = pack(integrals, owned)
    across = swap(packed, "xl")
    beside = swap(packed, "co")
    diagonal = swap(across, "co")

    ring = {0: owned}
    order, received = [], []
    for n, (offsets, mirrored) in enumerate(zip(STEPS, MIRRORED)):
        if n == len(STEPS) - 1:
            ring[n], ring[-n] = shift(ring[n - 1], 1), shift(ring[1 - n], -1)
            ring[n], ring[-n] = tie([ring[n], ring[-n]], [received[n - 2]])
            ring[n + 1] = shift(ring[n], 1)
        elif n > 0:
            ring[n], ring[-n] = shift(ring[n - 1], 1), shift(ring[1 - n], -1)
            if n > 1:
                ring[n], ring[-n] = tie([ring[n], ring[-n]], [received[n - 2]])
        outgoing = select(base, [ring[o] for o in offsets], SELECT_COST)
        received.append(exchange(outgoing, mirrored))
        places = (z - sign * jnp.array(offsets, jnp.int32)) % Z
        turn = half[0] if mirrored else 0
        peers = jnp.arange(PLANE, dtype=jnp.int32) ^ (turn * Y)
        order.append((places[None, :] * PLANE + peers[:, None]).reshape(-1))
    order = jnp.concatenate([order[n] for n in (1, 2, 0, 3)])

    mine = lax.axis_index("xl") * CO + core
    terms = jnp.arange(OWNERS, dtype=jnp.int32)
    term = jnp.sum(jnp.where(task_slots[:, None, :] == order[None, :, None], terms[None, None, :], 0), axis=2)
    relative = (term // TERM_SHARE) ^ mine
    spot = (relative * ROW_TILES + jnp.arange(ROW_TILES, dtype=jnp.int32)[:, None]) * TERM_SHARE + term % TERM_SHARE
    left = in_hbm(*prepare(spot, (packed, beside, across, diagonal)))

    total, other = steps(half, received[:3], (4, 0, 1), left, 60)
    other = swap(other, "xl")
    return last(5 * 512, received[3], left, total, other, amplitudes, row_gap[None, :], column_gap[None, :])


def solution(mesh):
    fine = Mesh(mesh.devices.reshape(Z, XH, Y, XL, CO), ("z", "xh", "y", "xl", "co"))
    wide, narrow = ("z", "xh", "y"), ("xl", "co")
    return jax.shard_map(
        body,
        mesh=fine,
        in_specs=(P(narrow, wide), P(wide, narrow, None, None), P(wide, None), P(wide, None), P(wide), P(narrow)),
        out_specs=(P(narrow, wide), P(narrow, wide)),
        check_vma=False,
    )
```

time: 376 us -> 167 us (0.44)
  Pallas kernels: 227 us -> 46.4 us
  waiting for transfers between devices: 27.7 us -> 67.6 us
  blocking collectives: 35 us -> 0 us
  local copies, waits for them, and re-layouts: 27.2 us -> 8.32 us
  starting transfers between devices: 52.8 us -> 41.9 us
  other arithmetic: 4.52 us -> 0.48 us
    pallas_call x9, Pallas kernels: 211 us -> 30.9 us  [the longest x4 14.1 us: select(): pl.pallas_call(select_kernel, out_shape=jax.ShapeDtypeStruct((PLANE, owne...]
    all_gather x1 -> x0, blocking collectives: 35 us -> none  [body(): asked = lax.all_gather(send_tiles[0].reshape(Z, PLANE), 'z', axis=0)]
    ppermute x4, waiting for transfers between devices: 0.01 us -> 32.1 us  [swap(): return lax.ppermute(x, axis, [(0, 1), (1, 0)])]
    all_to_all x4 -> x3, waiting for transfers between devices: 0.01 us -> 9.01 us  [exchange(): lax.all_to_all(x, ('xh', 'y', 'xl'), 0, 0, axis_index_groups=groups, tile...]
    all_to_all x1, waiting for transfers between devices: 8.92 us -> 0.01 us  [exchange(): return lax.all_to_all(x, ('xh', 'y'), 0, 0, tiled=True)]
    all_to_all x4 -> x3, starting transfers between devices: 27.9 us -> 19.3 us  [exchange(): lax.all_to_all(x, ('xh', 'y', 'xl'), 0, 0, axis_index_groups=groups, tile...]
    ppermute x8 -> x7, waiting for transfers between devices: 18.8 us -> 26.5 us  [shift(): return lax.ppermute(x, ('z', 'co'), turns)]
    slice x3 -> x0, local copies, waits for them, and re-layouts: 7.61 us -> none  [the longest x1 4.81 us: body(): integrals[:, :, :TILE // 2]]
  transfers between devices with their start and end apart: 17 -> 15, of which waited for: 4 -> 8; matrix products, arithmetic and copies ran while one was open for 5% -> 0% of each run, Pallas kernels for 59% -> 19%
where the time goes in v3:
time: 167 us; the launch traced here: 166 us
  waiting for transfers between devices  67.6 us (40%)
  Pallas kernels  46.4 us (28%)
  starting transfers between devices  41.9 us (25%)
  local copies, waits for them, and re-layouts  8.32 us (5%)
    ppermute x4, waiting for transfers between devices, swap(): return lax.ppermute(x, axis, [(0, 1), (1, 0)])  32.1 us
    ppermute x7, waiting for transfers between devices, shift(): return lax.ppermute(x, ('z', 'co'), turns)  26.5 us
    all_to_all x3, starting transfers between devices, exchange(): lax.all_to_all(x, ('xh', 'y', 'xl'), 0, 0, axis_index_groups=groups, tile...  19.3 us
    pallas_call x4, Pallas kernels, select(): pl.pallas_call(select_kernel, out_shape=jax.ShapeDtypeStruct((PLANE, owne...  14.1 us
    ppermute x7, starting transfers between devices, shift(): return lax.ppermute(x, ('z', 'co'), turns)  13.4 us
    all_to_all x3, waiting for transfers between devices, exchange(): lax.all_to_all(x, ('xh', 'y', 'xl'), 0, 0, axis_index_groups=groups, tile...  9.01 us
    pallas_call x1, Pallas kernels, prepare(): pl.pallas_call(prepare_kernel, grid=(OWNERS // GROUP,), out_shape=(shape,...  8.81 us
    unnamed x30, local copies, waits for them, and re-layouts  8.08 us
  transfers between devices with their start and end apart: 15, of which 8 were waited for; matrix products, arithmetic and copies ran while one was open for 0% of the time, Pallas kernels for 19%

profile of v3, /device:TPU:8, one launch (start us, length us, event | category | flops | bytes accessed | tf_op | source)
XLA Modules:
  0.0 165.5 jit_solution(2700459330164910391)
XLA Ops:
  0.6 2.3 %shard_map.113.refs_0_.after = f32[520,384]{1,0:T(8,128)} custom-call(f32[384,512]{1,0:T(8,128)} %amp.3, s32[1,64]{1,0:T(1,128)} %send.1), custom_call_target="tpu_custom_call" | custom-call | tf_op jit(solution)/shard_map/pallas_call | solution.py:54
  2.9 0.0 copy-start.5
  2.9 6.6 %shard_map.119.i0 = f32[128,32,128]{2,1,0:T(8,128)} custom-call(f32[8,16,64,64]{3,2,1,0:T(8,128)} %integrals.1, f32[520,384]{1,0:T(8,128)} %shard_map.113.refs_0_.after), custom_call_target="tpu_custom_call" | custom-call | tf_op jit(solution)/shard_map/pallas_call | solution.py:242
  9.5 1.5 collective-permute-start.8
  11.0 0.0 collective-permute-start.7
  11.0 0.0 copy-done.5
  11.0 1.9 %collective-permute-start = (f32[520,384]{1,0:T(8,128)S(1)}, f32[520,384]{1,0:T(8,128)}, u32[]{:S(2)}, u32[]{:S(2)}) collective-permute-start(f32[520,384]{1,0:T(8,128)S(1)} %copy-done.5), channel_id=1, source_target_pairs={{0,32},{1,225},{32,64},{33,1},{64,96},{65,33},{96,128},{97,65},{12... | collective-permute-start | bytes 2396168 | tf_op jit(solution)/shard_map/ppermute | solution.py:257
  12.9 4.0 %collective-permute-start.2 = (f32[520,384]{1,0:T(8,128)S(1)}, f32[520,384]{1,0:T(8,128)}, u32[]{:S(2)}, u32[]{:S(2)}) collective-permute-start(f32[520,384]{1,0:T(8,128)S(1)} %copy-done.5), channel_id=1, source_target_pairs={{0,224},{1,33},{32,0},{33,65},{64,32},{65,97},{96,64},{97,129},{12... | collective-permute-start | bytes 2396168 | tf_op jit(solution)/shard_map/ppermute | solution.py:257
  17.0 2.9 %shard_map.114 = f32[8,1,64,384]{3,2,1,0:T(8,128)} custom-call(s32[1]{0:T(128)} %bitcast.base, f32[520,384]{1,0:T(8,128)} %shard_map.113.refs_0_.after), custom_call_target="tpu_custom_call" | custom-call | flops 40000000000 | tf_op jit(solution)/shard_map/pallas_call | solution.py:89
  19.9 6.5 %all-to-all-start = ((f32[8,1,64,384]{3,2,1,0:T(8,128)}), f32[8,1,64,384]{3,2,1,0:T(8,128)S(1)}, u32[]{:S(2)}, u32[]{:S(2)}) async-start(f32[8,1,64,384]{3,2,1,0:T(8,128)} %shard_map.114), calls=%async_computation | async-start | bytes 1572864 | tf_op jit(solution)/shard_map/all_to_all | solution.py:264
  26.3 6.7 %collective-permute-done.refs_0_ = f32[520,384]{1,0:T(8,128)} collective-permute-done((f32[520,384]{1,0:T(8,128)S(1)}, f32[520,384]{1,0:T(8,128)}, u32[]{:S(2)}, u32[]{:S(2)}) %collective-permute-start) | collective-permute-done | bytes 798752 | tf_op jit(solution)/shard_map/ppermute | solution.py:257
  33.1 0.0 collective-permute-start.1
  33.1 1.6 collective-permute-done.2.refs_1_
  34.6 3.8 %collective-permute-start.3 = (f32[520,384]{1,0:T(8,128)}, f32[520,384]{1,0:T(8,128)}, u32[]{:S(2)}, u32[]{:S(2)}) collective-permute-start(f32[520,384]{1,0:T(8,128)} %collective-permute-done.2.refs_1_), channel_id=1, source_target_pairs={{0,224},{1,33},{32,0},{33,65},{64,32},{65,97},{96,64},{97,129},{12... | collective-permute-start | bytes 2396168 | tf_op jit(solution)/shard_map/ppermute | solution.py:257
  38.4 3.5 %shard_map.116 = f32[8,2,64,384]{3,2,1,0:T(8,128)} custom-call(s32[1]{0:T(128)} %bitcast.base, f32[520,384]{1,0:T(8,128)} %collective-permute-done.refs_0_, f32[520,384]{1,0:T(8,128)} %collective-permute-done.2.refs_1_), custom_call_target="tpu_custom_call" | custom-call | flops 40000000000 | tf_op jit(solution)/shard_map/pallas_call | solution.py:89
  42.0 0.0 copy-start.12
  42.0 0.0 copy-start.13
  42.0 0.0 copy-start.11
  42.0 0.0 copy-start.9
  42.0 0.0 all-to-all-done.refs_2_
  42.0 0.0 copy-start.6
  42.0 0.9 copy-done.6
  42.9 6.4 %all-to-all-start.1 = ((f32[8,2,64,384]{3,2,1,0:T(8,128)}), f32[8,2,64,384]{3,2,1,0:T(8,128)S(1)}, u32[]{:S(2)}, u32[]{:S(2)}) async-start(f32[8,2,64,384]{3,2,1,0:T(8,128)} %shard_map.116), calls=%async_computation.1 | async-start | bytes 3145728 | tf_op jit(solution)/shard_map/all_to_all | solution.py:264
  49.4 0.0 copy-done.12
  49.4 0.0 copy-done.13
  49.4 0.1 broadcast_add_fusion.1
  49.5 0.1 add.109
  49.5 0.1 add.113
  49.6 4.0 %collective-permute-done.1.refs_0_ = f32[520,384]{1,0:T(8,128)} collective-permute-done((f32[520,384]{1,0:T(8,128)}, f32[520,384]{1,0:T(8,128)}, u32[]{:S(2)}, u32[]{:S(2)}) %collective-permute-start.1) | collective-permute-done | bytes 798752 | tf_op jit(solution)/shard_map/ppermute | solution.py:257
  53.6 2.0 %collective-permute-done.3.refs_1_ = f32[520,384]{1,0:T(8,128)} collective-permute-done((f32[520,384]{1,0:T(8,128)}, f32[520,384]{1,0:T(8,128)}, u32[]{:S(2)}, u32[]{:S(2)}) %collective-permute-start.3) | collective-permute-done | bytes 798752 | tf_op jit(solution)/shard_map/ppermute | solution.py:257
  55.6 0.0 collective-permute-start.4
  55.6 3.7 %collective-permute-start.5 = (f32[520,384]{1,0:T(8,128)}, f32[520,384]{1,0:T(8,128)}, u32[]{:S(2)}, u32[]{:S(2)}) collective-permute-start(f32[520,384]{1,0:T(8,128)} %get-tuple-element.11.refs_1_), channel_id=1, source_target_pairs={{0,224},{1,33},{32,0},{33,65},{64,32},{65,97},{96,64},{97,129},{12... | collective-permute-start | bytes 2396168 | tf_op jit(solution)/shard_map/ppermute | solution.py:257
  59.3 0.0 copy-done.11
  59.3 0.1 add.122
  59.4 0.1 pad_add_fusion
  59.5 0.0 copy-done.9
  59.5 0.3 select_reduce_fusion
  59.8 9.0 %all-to-all-done.1.refs_2_ = f32[8,2,64,384]{3,2,1,0:T(8,128)S(1)} async-done(((f32[8,2,64,384]{3,2,1,0:T(8,128)}), f32[8,2,64,384]{3,2,1,0:T(8,128)S(1)}, u32[]{:S(2)}, u32[]{:S(2)}) %all-to-all-start.1) | async-done | bytes 1572896 | tf_op jit(solution)/shard_map/all_to_all | solution.py:264
  68.8 8.7 %collective-permute-done.4.refs_0_ = f32[520,384]{1,0:T(8,128)S(1)} collective-permute-done((f32[520,384]{1,0:T(8,128)}, f32[520,384]{1,0:T(8,128)S(1)}, u32[]{:S(2)}, u32[]{:S(2)}) %collective-permute-start.4) | collective-permute-done | bytes 798752 | tf_op jit(solution)/shard_map/ppermute | solution.py:257
  77.5 0.0 collective-permute-done.5.refs_1_
  77.5 0.9 copy-done.8
  78.4 0.0 collective-permute-start.6
  78.4 3.5 %shard_map.121 = f32[8,2,64,384]{3,2,1,0:T(8,128)} custom-call(s32[1]{0:T(128)} %bitcast.base, f32[520,384]{1,0:T(8,128)} %get-tuple-element.10.refs_0_, f32[520,384]{1,0:T(8,128)} %get-tuple-element.11.refs_1_), custom_call_target="tpu_custom_call" | custom-call | flops 40000000000 | tf_op jit(solution)/shard_map/pallas_call | solution.py:89
  81.9 6.4 %all-to-all-start.3 = ((f32[8,2,64,384]{3,2,1,0:T(8,128)}), f32[8,2,64,384]{3,2,1,0:T(8,128)}, u32[]{:S(2)}, u32[]{:S(2)}) async-start(f32[8,2,64,384]{3,2,1,0:T(8,128)} %shard_map.121), calls=%async_computation.3 | async-start | bytes 3145728 | tf_op jit(solution)/shard_map/all_to_all | solution.py:264
  88.4 0.0 collective-permute-done.8.i2
  88.4 0.0 collective-permute-start.9
  88.4 3.5 %collective-permute-done.6.refs_2_ = f32[520,384]{1,0:T(8,128)S(1)} collective-permute-done((f32[520,384]{1,0:T(8,128)}, f32[520,384]{1,0:T(8,128)S(1)}, u32[]{:S(2)}, u32[]{:S(2)}) %collective-permute-start.6) | collective-permute-done | bytes 798752 | tf_op jit(solution)/shard_map/ppermute | solution.py:257
  91.9 0.9 copy-done.14
  92.8 4.1 %shard_map.118 = f32[8,3,64,384]{3,2,1,0:T(8,128)} custom-call(s32[1]{0:T(128)} %bitcast.base, f32[520,384]{1,0:T(8,128)} %get-tuple-element.12.refs_0_, f32[520,384]{1,0:T(8,128)} %get-tuple-element.13.refs_1_, f32[520,384]{1,0:T(8,128)} %copy-done.14), custom_call_target="tpu_custom_call" | custom-call | flops 40000000000 | tf_op jit(solution)/shard_map/pallas_call | solution.py:89
  97.0 0.0 collective-permute-done.7.i1
  97.0 0.0 collective-permute-done.9.i3
  97.0 1.4 copy-done.7
  98.4 8.8 %shard_map.120 = (bf16[512,4096]{1,0:T(8,128)(2,1)S(1)}, bf16[512,4096]{1,0:T(8,128)(2,1)S(1)}) custom-call(s32[8,64]{1,0:T(8,128)S(1)} %fusion.4.spot, f32[128,32,128]{2,1,0:T(8,128)} %shard_map.119.i0, f32[128,32,128]{2,1,0:T(8,128)} %collective-permute-done.7.i1, f32[128,32,128]{2,1,0:T(8,128)} %collective-permute-done.8.i2, f32[128,32,128]{2,1,0:T(8,128)} %copy-done.7), custom_call_target="tpu_custom_call" | custom-call | tf_op jit(solution)/shard_map/pallas_call | solution.py:134
  107.2 2.0 %copy-done = bf16[512,4096]{1,0:T(8,128)(2,1)} copy-done((bf16[512,4096]{1,0:T(8,128)(2,1)}, bf16[512,4096]{1,0:T(8,128)(2,1)S(1)}, u32[]{:S(2)}) %copy-start) | copy-done | bytes 4194328
  109.2 2.0 %copy-done.1 = bf16[512,4096]{1,0:T(8,128)(2,1)} copy-done((bf16[512,4096]{1,0:T(8,128)(2,1)}, bf16[512,4096]{1,0:T(8,128)(2,1)S(1)}, u32[]{:S(2)}) %copy-start.1) | copy-done | bytes 4194328
  111.2 0.0 all-to-all-done.3
  111.2 7.1 %all-to-all-start.2 = ((f32[8,3,64,384]{3,2,1,0:T(8,128)}), f32[8,3,64,384]{3,2,1,0:T(8,128)}, u32[]{:S(2)}, u32[]{:S(2)}) async-start(f32[8,3,64,384]{3,2,1,0:T(8,128)} %shard_map.118), calls=%async_computation.2 | async-start | bytes 4718592 | tf_op jit(solution)/shard_map/all_to_all | solution.py:262
  118.3 7.9 %shard_map.122 = (f32[512,384]{1,0:T(8,128)S(1)}, f32[512,384]{1,0:T(8,128)S(1)}) custom-call(s32[1]{0:T(128)} %bitcast.3.half, f32[2,4,1,64,384]{4,3,2,1,0:T(8,128)} %bitcast.10, f32[2,4,2,64,384]{4,3,2,1,0:T(8,128)} %bitcast.9, f32[2,4,2,64,384]{4,3,2,1,0:T(8,128)} %bitcast.6.refs_2_, bf16[512,4096]{1,0:T(8,128)(2,1)} %copy-done, ...), custom_call_target="tpu_custom_call" | custom-call | flops 60000002048 | tf_op jit(solution)/shard_map/pallas_call | solution.py:182
  126.2 0.5 collective-permute-start.10
  126.7 0.0 copy-done.10
  126.7 32.1 %collective-permute-done.10.other = f32[512,384]{1,0:T(8,128)S(1)} collective-permute-done((f32[512,384]{1,0:T(8,128)S(1)}, f32[512,384]{1,0:T(8,128)S(1)}, u32[]{:S(2)}, u32[]{:S(2)}) %collective-permute-start.10) | collective-permute-done | bytes 786464 | tf_op jit(solution)/shard_map/ppermute | solution.py:252
  158.8 0.0 all-to-all-done.2.tiles
  158.8 0.0 copy-done.3
  158.8 6.7 %shard_map.123 = (f32[384,512]{1,0:T(8,128)}, f32[384,512]{1,0:T(8,128)}) custom-call(f32[8,3,64,384]{3,2,1,0:T(8,128)} %all-to-all-done.2.tiles, bf16[512,4096]{1,0:T(8,128)(2,1)} %copy-done, bf16[512,4096]{1,0:T(8,128)(2,1)} %copy-done.1, f32[512,384]{1,0:T(8,128)S(1)} %get-tuple-element.16.total, f32[512,384]{1,0:T(8,128)S(1)} %collective-permute-done.10.other, ...), custom_call_target="tpu_custom_call" | custom-call | tf_op jit(solution)/shard_map/pallas_call | solution.py:210
  (19 shorter events, 0.1 us)
Async XLA Ops:
  2.9 8.1 %copy-start.5 = (f32[520,384]{1,0:T(8,128)S(1)}, f32[520,384]{1,0:T(8,128)}, u32[]{:S(2)}) copy-start(f32[520,384]{1,0:T(8,128)} %shard_map.113.refs_0_.after) | copy-start | bytes 2396164
  9.5 78.9 %collective-permute-start.8 = (f32[128,32,128]{2,1,0:T(8,128)}, f32[128,32,128]{2,1,0:T(8,128)}, u32[]{:S(2)}, u32[]{:S(2)}) collective-permute-start(f32[128,32,128]{2,1,0:T(8,128)} %shard_map.119.i0), channel_id=1, source_target_pairs={{0,2},{2,0},{1,3},{3,1},{4,6},{6,4},{5,7},{7,5},{8,10},{10,8},{9,1... | collective-permute-start | bytes 6291464 | tf_op jit(solution)/shard_map/ppermute | solution.py:252
  11.0 86.0 %collective-permute-start.7 = (f32[128,32,128]{2,1,0:T(8,128)}, f32[128,32,128]{2,1,0:T(8,128)}, u32[]{:S(2)}, u32[]{:S(2)}) collective-permute-start(f32[128,32,128]{2,1,0:T(8,128)} %shard_map.119.i0), channel_id=1, source_target_pairs={{0,1},{1,0},{2,3},{3,2},{4,5},{5,4},{6,7},{7,6},{8,9},{9,8},{10,11... | collective-permute-start | bytes 6291464 | tf_op jit(solution)/shard_map/ppermute | solution.py:252
  11.0 22.0 %collective-permute-start = (f32[520,384]{1,0:T(8,128)S(1)}, f32[520,384]{1,0:T(8,128)}, u32[]{:S(2)}, u32[]{:S(2)}) collective-permute-start(f32[520,384]{1,0:T(8,128)S(1)} %copy-done.5), channel_id=1, source_target_pairs={{0,32},{1,225},{32,64},{33,1},{64,96},{65,33},{96,128},{97,65},{12... | collective-permute-start | bytes 2396168 | tf_op jit(solution)/shard_map/ppermute | solution.py:257
  12.9 21.7 %collective-permute-start.2 = (f32[520,384]{1,0:T(8,128)S(1)}, f32[520,384]{1,0:T(8,128)}, u32[]{:S(2)}, u32[]{:S(2)}) collective-permute-start(f32[520,384]{1,0:T(8,128)S(1)} %copy-done.5), channel_id=1, source_target_pairs={{0,224},{1,33},{32,0},{33,65},{64,32},{65,97},{96,64},{97,129},{12... | collective-permute-start | bytes 2396168 | tf_op jit(solution)/shard_map/ppermute | solution.py:257
  19.9 22.1 %all-to-all-start = ((f32[8,1,64,384]{3,2,1,0:T(8,128)}), f32[8,1,64,384]{3,2,1,0:T(8,128)S(1)}, u32[]{:S(2)}, u32[]{:S(2)}) async-start(f32[8,1,64,384]{3,2,1,0:T(8,128)} %shard_map.114), calls=%async_computation | async-start | bytes 1572864 | tf_op jit(solution)/shard_map/all_to_all | solution.py:264
  33.1 20.6 %collective-permute-start.1 = (f32[520,384]{1,0:T(8,128)}, f32[520,384]{1,0:T(8,128)}, u32[]{:S(2)}, u32[]{:S(2)}) collective-permute-start(f32[520,384]{1,0:T(8,128)} %collective-permute-done.refs_0_), channel_id=1, source_target_pairs={{0,32},{1,225},{32,64},{33,1},{64,96},{65,33},{96,128},{97,65},{12... | collective-permute-start | bytes 2396168 | tf_op jit(solution)/shard_map/ppermute | solution.py:257
  34.6 21.0 %collective-permute-start.3 = (f32[520,384]{1,0:T(8,128)}, f32[520,384]{1,0:T(8,128)}, u32[]{:S(2)}, u32[]{:S(2)}) collective-permute-start(f32[520,384]{1,0:T(8,128)} %collective-permute-done.2.refs_1_), channel_id=1, source_target_pairs={{0,224},{1,33},{32,0},{33,65},{64,32},{65,97},{96,64},{97,129},{12... | collective-permute-start | bytes 2396168 | tf_op jit(solution)/shard_map/ppermute | solution.py:257
  42.0 7.4 %copy-start.12 = (s32[2]{0:T(128)S(1)}, s32[2]{0:T(128)}, u32[]{:S(2)}) copy-start(s32[2]{0:T(128)} %constant.106.clone) | copy-start | bytes 28
  42.0 7.4 %copy-start.13 = (s32[2]{0:T(128)S(1)}, s32[2]{0:T(128)}, u32[]{:S(2)}) copy-start(s32[2]{0:T(128)} %constant.107.clone) | copy-start | bytes 28
  42.0 17.3 %copy-start.11 = (s32[3]{0:T(128)S(1)}, s32[3]{0:T(128)}, u32[]{:S(2)}) copy-start(s32[3]{0:T(128)} %constant.108.clone) | copy-start | bytes 40
  42.0 17.5 %copy-start.9 = (s32[8,64]{1,0:T(8,128)S(1)}, s32[8,64]{1,0:T(8,128)}, u32[]{:S(2)}) copy-start(s32[8,64]{1,0:T(8,128)} %param.13) | copy-start | bytes 6148
  42.0 0.9 copy-start.6
  42.9 25.9 %all-to-all-start.1 = ((f32[8,2,64,384]{3,2,1,0:T(8,128)}), f32[8,2,64,384]{3,2,1,0:T(8,128)S(1)}, u32[]{:S(2)}, u32[]{:S(2)}) async-start(f32[8,2,64,384]{3,2,1,0:T(8,128)} %shard_map.116), calls=%async_computation.1 | async-start | bytes 3145728 | tf_op jit(solution)/shard_map/all_to_all | solution.py:264
  55.6 21.9 %collective-permute-start.4 = (f32[520,384]{1,0:T(8,128)}, f32[520,384]{1,0:T(8,128)S(1)}, u32[]{:S(2)}, u32[]{:S(2)}) collective-permute-start(f32[520,384]{1,0:T(8,128)} %get-tuple-element.10.refs_0_), channel_id=1, source_target_pairs={{0,32},{1,225},{32,64},{33,1},{64,96},{65,33},{96,128},{97,65},{12... | collective-permute-start | bytes 2396168 | tf_op jit(solution)/shard_map/ppermute | solution.py:257
  55.6 21.9 %collective-permute-start.5 = (f32[520,384]{1,0:T(8,128)}, f32[520,384]{1,0:T(8,128)}, u32[]{:S(2)}, u32[]{:S(2)}) collective-permute-start(f32[520,384]{1,0:T(8,128)} %get-tuple-element.11.refs_1_), channel_id=1, source_target_pairs={{0,224},{1,33},{32,0},{33,65},{64,32},{65,97},{96,64},{97,129},{12... | collective-permute-start | bytes 2396168 | tf_op jit(solution)/shard_map/ppermute | solution.py:257
  68.8 8.7 %copy-start.4 = (f32[8,2,64,384]{3,2,1,0:T(8,128)}, f32[8,2,64,384]{3,2,1,0:T(8,128)S(1)}, u32[]{:S(2)}) copy-start(f32[8,2,64,384]{3,2,1,0:T(8,128)S(1)} %all-to-all-done.1.refs_2_) | copy-start | bytes 4718596
  77.5 0.9 copy-start.8
  78.4 13.5 %collective-permute-start.6 = (f32[520,384]{1,0:T(8,128)}, f32[520,384]{1,0:T(8,128)S(1)}, u32[]{:S(2)}, u32[]{:S(2)}) collective-permute-start(f32[520,384]{1,0:T(8,128)} %get-tuple-element.12.refs_0_), channel_id=1, source_target_pairs={{0,32},{1,225},{32,64},{33,1},{64,96},{65,33},{96,128},{97,65},{12... | collective-permute-start | bytes 2396168 | tf_op jit(solution)/shard_map/ppermute | solution.py:257
  81.9 29.3 %all-to-all-start.3 = ((f32[8,2,64,384]{3,2,1,0:T(8,128)}), f32[8,2,64,384]{3,2,1,0:T(8,128)}, u32[]{:S(2)}, u32[]{:S(2)}) async-start(f32[8,2,64,384]{3,2,1,0:T(8,128)} %shard_map.121), calls=%async_computation.3 | async-start | bytes 3145728 | tf_op jit(solution)/shard_map/all_to_all | solution.py:264
  88.4 8.6 %collective-permute-start.9 = (f32[128,32,128]{2,1,0:T(8,128)}, f32[128,32,128]{2,1,0:T(8,128)S(1)}, u32[]{:S(2)}, u32[]{:S(2)}) collective-permute-start(f32[128,32,128]{2,1,0:T(8,128)} %collective-permute-done.8.i2), channel_id=1, source_target_pairs={{0,1},{1,0},{2,3},{3,2},{4,5},{5,4},{6,7},{7,6},{8,9},{9,8},{10,11... | collective-permute-start | bytes 6291464 | tf_op jit(solution)/shard_map/ppermute | solution.py:252
  91.9 0.9 copy-start.14
  97.0 1.4 copy-start.7
  107.2 2.0 %copy-start = (bf16[512,4096]{1,0:T(8,128)(2,1)}, bf16[512,4096]{1,0:T(8,128)(2,1)S(1)}, u32[]{:S(2)}) copy-start(bf16[512,4096]{1,0:T(8,128)(2,1)S(1)} %get-tuple-element.14.refs_3_.refs_5_.refs_7_.left_hi) | copy-start | bytes 12582916
  109.2 2.0 %copy-start.1 = (bf16[512,4096]{1,0:T(8,128)(2,1)}, bf16[512,4096]{1,0:T(8,128)(2,1)S(1)}, u32[]{:S(2)}) copy-start(bf16[512,4096]{1,0:T(8,128)(2,1)S(1)} %get-tuple-element.15.refs_4_.refs_6_.refs_8_.left_lo) | copy-start | bytes 12582916
  111.2 47.6 %all-to-all-start.2 = ((f32[8,3,64,384]{3,2,1,0:T(8,128)}), f32[8,3,64,384]{3,2,1,0:T(8,128)}, u32[]{:S(2)}, u32[]{:S(2)}) async-start(f32[8,3,64,384]{3,2,1,0:T(8,128)} %shard_map.118), calls=%async_computation.2 | async-start | bytes 4718592 | tf_op jit(solution)/shard_map/all_to_all | solution.py:262
  118.3 8.4 %copy-start.10 = (f32[384]{0:T(512)S(1)}, f32[384]{0:T(512)}, u32[]{:S(2)}) copy-start(f32[384]{0:T(512)} %param.15) | copy-start | bytes 4612
  118.3 40.5 %copy-start.2 = (f32[384,512]{1,0:T(8,128)S(1)}, f32[384,512]{1,0:T(8,128)}, u32[]{:S(2)}) copy-start(f32[384,512]{1,0:T(8,128)} %amp.3) | copy-start | bytes 2359300
  118.3 40.5 %copy-start.3 = (f32[512]{0:T(512)S(1)}, f32[512]{0:T(512)}, u32[]{:S(2)}) copy-start(f32[512]{0:T(512)} %param.14) | copy-start | bytes 6148
  126.2 32.6 %collective-permute-start.10 = (f32[512,384]{1,0:T(8,128)S(1)}, f32[512,384]{1,0:T(8,128)S(1)}, u32[]{:S(2)}, u32[]{:S(2)}) collective-permute-start(f32[512,384]{1,0:T(8,128)S(1)} %get-tuple-element.17), channel_id=1, source_target_pairs={{0,2},{2,0},{1,3},{3,1},{4,6},{6,4},{5,7},{7,5},{8,10},{10,8},{9,1... | collective-permute-start | bytes 2359304 | tf_op jit(solution)/shard_map/ppermute | solution.py:252

commit v4 on v3

--- a/solution.py
+++ b/solution.py
@@ -15,9 +15,9 @@
 TERM_SHARE = 16
 GROUP = 4
 NOTE = 8
-SELECT_COST = 40
-STEPS = ((0,), (1, -1), (2, -2), (3, -3, 4))
-MIRRORED = (True, True, True, False)
+SELECT_COST = (40, 40, 40, 8, 30)
+STEPS = ((0,), (1, -1), (2, -2), (3, -3), (4,))
+MIRRORED = (True, True, True, False, False)
 ANYWHERE = pl.BlockSpec(memory_space=pl.ANY)
 IN_HBM = pl.BlockSpec(memory_space=pltpu.HBM)
 INSIDE = pl.BlockSpec(memory_space=pltpu.VMEM)
@@ -176,7 +176,7 @@
 
 def steps(half, tiles, indices, left, micros):
     rows, cols = left[0].shape[0], tiles[0].shape[-1]
-    tiles = in_hbm(*[t.reshape(XH, Y, *t.shape[1:]) for t in tiles])
+    tiles = [t.reshape(XH, Y, *t.shape[1:]) for t in tiles]
     shape = jax.ShapeDtypeStruct((rows, cols), jnp.float32)
     blocks = [column_block(rows, PLANE * t.shape[2] * TILE, index) for t, index in zip(tiles, indices)]
     return pl.pallas_call(
@@ -201,12 +201,10 @@
     new[...] = amplitudes + residual / gap
 
 
-def last(offset, tiles, left, total, other, amp, row_gap, col_gap):
+def last(index, tiles, left, total, other, amp, row_gap, col_gap):
     rows, cols = left[0].shape[0], tiles.shape[-1]
-    depth = PLANE * tiles.shape[1] * TILE
-    (tiles,) = in_hbm(tiles)
+    block = column_block(rows, PLANE * tiles.shape[1] * TILE, index)
     shape = jax.ShapeDtypeStruct((cols, rows), jnp.float32)
-    block = pl.BlockSpec((pl.Element(rows), pl.Element(depth)), lambda g: (0, offset))
     return pl.pallas_call(
         last_kernel,
         grid=(1,),
@@ -217,6 +215,25 @@
     )(tiles, *left, total, other, amp, row_gap, col_gap)
 
 
+def more_kernel(tiles, left_hi, left_lo, total, out):
+    values = tiles[...].reshape(left_hi.shape[1], tiles.shape[-1])
+    out[...] = total[...] + product(left_hi[...], left_lo[...], values)
+
+
+def more(index, tiles, left, total, micros):
+    rows = left[0].shape[0]
+    block = column_block(rows, PLANE * tiles.shape[1] * TILE, index)
+    return pl.pallas_call(
+        more_kernel,
+        grid=(1,),
+        out_shape=jax.ShapeDtypeStruct(total.shape, jnp.float32),
+        in_specs=[full(tiles), block, block, full(total)],
+        out_specs=full(total),
+        compiler_params=PARAMS,
+        cost_estimate=cost(micros),
+    )(tiles, *left, total)
+
+
 def tie_kernel(*refs):
     del refs
 
@@ -225,10 +242,10 @@
     return pl.pallas_call(
         tie_kernel,
         out_shape=[jax.ShapeDtypeStruct(x.shape, x.dtype) for x in xs],
-        in_specs=[IN_HBM] * (len(xs) + len(after)),
+        in_specs=[IN_HBM] * len(xs) + [ANYWHERE] * len(after),
         out_specs=[IN_HBM] * len(xs),
         input_output_aliases={n: n for n in range(len(xs))},
-    )(*in_hbm(*xs, *after))
+    )(*in_hbm(*xs), *after)
 
 
 def pack_kernel(integrals, after, out):
@@ -271,29 +288,28 @@
     base, half = (z * PLANE)[None].astype(jnp.int32), half[None].astype(jnp.int32)
 
     owned = first(amplitudes, send_tiles)
-    packed = pack(integrals, owned)
-    across = swap(packed, "xl")
-    beside = swap(packed, "co")
-    diagonal = swap(across, "co")
-
     ring = {0: owned}
     order, received = [], []
     for n, (offsets, mirrored) in enumerate(zip(STEPS, MIRRORED)):
-        if n == len(STEPS) - 1:
-            ring[n], ring[-n] = shift(ring[n - 1], 1), shift(ring[1 - n], -1)
-            ring[n], ring[-n] = tie([ring[n], ring[-n]], [received[n - 2]])
-            ring[n + 1] = shift(ring[n], 1)
+        if n == Z // 2:
+            ring[n] = shift(ring[n - 1], 1)
         elif n > 0:
             ring[n], ring[-n] = shift(ring[n - 1], 1), shift(ring[1 - n], -1)
             if n > 1:
                 ring[n], ring[-n] = tie([ring[n], ring[-n]], [received[n - 2]])
-        outgoing = select(base, [ring[o] for o in offsets], SELECT_COST)
+        outgoing = select(base, [ring[o] for o in offsets], SELECT_COST[n])
+        if n == 0:
+            packed = pack(integrals, outgoing)
         received.append(exchange(outgoing, mirrored))
         places = (z - sign * jnp.array(offsets, jnp.int32)) % Z
         turn = half[0] if mirrored else 0
         peers = jnp.arange(PLANE, dtype=jnp.int32) ^ (turn * Y)
         order.append((places[None, :] * PLANE + peers[:, None]).reshape(-1))
-    order = jnp.concatenate([order[n] for n in (1, 2, 0, 3)])
+    across = swap(packed, "xl")
+    beside = swap(packed, "co")
+    diagonal = swap(tie([across], [ring[3]])[0], "co")
+
+    order = jnp.concatenate([order[n] for n in (1, 2, 3, 0, 4)])
 
     mine = lax.axis_index("xl") * CO + core
     terms = jnp.arange(OWNERS, dtype=jnp.int32)
@@ -302,9 +318,10 @@
     spot = (relative * ROW_TILES + jnp.arange(ROW_TILES, dtype=jnp.int32)[:, None]) * TERM_SHARE + term % TERM_SHARE
     left = in_hbm(*prepare(spot, (packed, beside, across, diagonal)))
 
-    total, other = steps(half, received[:3], (4, 0, 1), left, 60)
+    total, other = steps(half, received[:3], (6, 0, 1), left, 8)
     other = swap(other, "xl")
-    return last(5 * 512, received[3], left, total, other, amplitudes, row_gap[None, :], column_gap[None, :])
+    total = more(2, received[3], left, total, 60)
+    return last(7, received[4], left, total, other, amplitudes, row_gap[None, :], column_gap[None, :])
 
 
 def solution(mesh):

time: 167 us -> 149 us (0.89)
  waiting for transfers between devices: 67.6 us -> 39.1 us
  starting transfers between devices: 41.9 us -> 46.9 us
  local copies, waits for them, and re-layouts: 8.32 us -> 12.1 us
  Pallas kernels: 46.4 us -> 48.8 us
    ppermute x4, waiting for transfers between devices: 32.1 us -> 3.37 us  [swap(): return lax.ppermute(x, axis, [(0, 1), (1, 0)])]
    ppermute x7, waiting for transfers between devices: 26.5 us -> 10.3 us  [shift(): return lax.ppermute(x, ('z', 'co'), turns)]
    all_to_all x1 -> x2, waiting for transfers between devices: 0.01 us -> 14.2 us  [exchange(): return lax.all_to_all(x, ('xh', 'y'), 0, 0, tiled=True)]
    all_to_all x1 -> x2, starting transfers between devices: 7.09 us -> 12.7 us  [exchange(): return lax.all_to_all(x, ('xh', 'y'), 0, 0, tiled=True)]
    unnamed x30 -> x35, local copies, waits for them, and re-layouts: 8.08 us -> 11.8 us
    pallas_call x0 -> x1, Pallas kernels: none -> 3.42 us  [more(): pl.pallas_call(more_kernel, grid=(1,), out_shape=jax.ShapeDtypeStruct(tot...]
    pallas_call x1, Pallas kernels: 6.69 us -> 3.66 us  [last(): pl.pallas_call(last_kernel, grid=(1,), out_shape=(shape, shape), in_specs...]
    pallas_call x4 -> x5, Pallas kernels: 14.1 us -> 16.4 us  [select(): pl.pallas_call(select_kernel, out_shape=jax.ShapeDtypeStruct((PLANE, owne...]
  transfers between devices with their start and end apart: 15 -> 16, of which waited for: 8 -> 7; matrix products, arithmetic and copies ran while one was open for 0% -> 3% of each run, Pallas kernels for 19% -> 29%
where the time goes in v4:
time: 149 us; the launch traced here: 148 us
  Pallas kernels  48.8 us (33%)
  starting transfers between devices  46.9 us (31%)
  waiting for transfers between devices  39.1 us (26%)
  local copies, waits for them, and re-layouts  12.1 us (8%)
    all_to_all x3, starting transfers between devices, exchange(): lax.all_to_all(x, ('xh', 'y', 'xl'), 0, 0, axis_index_groups=groups, tile...  19.6 us
    pallas_call x5, Pallas kernels, select(): pl.pallas_call(select_kernel, out_shape=jax.ShapeDtypeStruct((PLANE, owne...  16.4 us
    all_to_all x2, waiting for transfers between devices, exchange(): return lax.all_to_all(x, ('xh', 'y'), 0, 0, tiled=True)  14.2 us
    ppermute x7, starting transfers between devices, shift(): return lax.ppermute(x, ('z', 'co'), turns)  13 us
    all_to_all x2, starting transfers between devices, exchange(): return lax.all_to_all(x, ('xh', 'y'), 0, 0, tiled=True)  12.7 us
    unnamed x35, local copies, waits for them, and re-layouts  11.8 us
    all_to_all x3, waiting for transfers between devices, exchange(): lax.all_to_all(x, ('xh', 'y', 'xl'), 0, 0, axis_index_groups=groups, tile...  11.2 us
    ppermute x7, waiting for transfers between devices, shift(): return lax.ppermute(x, ('z', 'co'), turns)  10.3 us
  transfers between devices with their start and end apart: 16, of which 7 were waited for; matrix products, arithmetic and copies ran while one was open for 3% of the time, Pallas kernels for 29%

profile of v4, /device:TPU:8, one launch (start us, length us, event | category | flops | bytes accessed | tf_op | source)
XLA Modules:
  0.0 148.1 jit_solution(2796084558378834476)
XLA Ops:
  0.6 2.3 %shard_map.122.refs_0_ = f32[520,384]{1,0:T(8,128)} custom-call(f32[384,512]{1,0:T(8,128)} %amp.3, s32[1,64]{1,0:T(1,128)} %send.1), custom_call_target="tpu_custom_call" | custom-call | tf_op jit(solution)/shard_map/pallas_call | solution.py:54
  2.9 2.0 %collective-permute-start = (f32[520,384]{1,0:T(8,128)}, f32[520,384]{1,0:T(8,128)}, u32[]{:S(2)}, u32[]{:S(2)}) collective-permute-start(f32[520,384]{1,0:T(8,128)} %shard_map.122.refs_0_), channel_id=1, source_target_pairs={{0,32},{1,225},{32,64},{33,1},{64,96},{65,33},{96,128},{97,65},{12... | collective-permute-start | bytes 2396168 | tf_op jit(solution)/shard_map/ppermute | solution.py:274
  4.9 4.0 %collective-permute-start.2 = (f32[520,384]{1,0:T(8,128)}, f32[520,384]{1,0:T(8,128)}, u32[]{:S(2)}, u32[]{:S(2)}) collective-permute-start(f32[520,384]{1,0:T(8,128)} %shard_map.122.refs_0_), channel_id=1, source_target_pairs={{0,224},{1,33},{32,0},{33,65},{64,32},{65,97},{96,64},{97,129},{12... | collective-permute-start | bytes 2396168 | tf_op jit(solution)/shard_map/ppermute | solution.py:274
  8.9 2.9 %shard_map.123.after = f32[8,1,64,384]{3,2,1,0:T(8,128)} custom-call(s32[1]{0:T(128)} %bitcast.base, f32[520,384]{1,0:T(8,128)} %shard_map.122.refs_0_), custom_call_target="tpu_custom_call" | custom-call | flops 40000000000 | tf_op jit(solution)/shard_map/pallas_call | solution.py:89
  11.9 7.1 %all-to-all-start = ((f32[8,1,64,384]{3,2,1,0:T(8,128)}), f32[8,1,64,384]{3,2,1,0:T(8,128)S(1)}, u32[]{:S(2)}, u32[]{:S(2)}) async-start(f32[8,1,64,384]{3,2,1,0:T(8,128)} %shard_map.123.after), calls=%async_computation | async-start | bytes 1572864 | tf_op jit(solution)/shard_map/all_to_all | solution.py:281
  19.0 6.5 %shard_map.128.i0 = f32[128,32,128]{2,1,0:T(8,128)} custom-call(f32[8,16,64,64]{3,2,1,0:T(8,128)} %integrals.1, f32[8,1,64,384]{3,2,1,0:T(8,128)} %shard_map.123.after), custom_call_target="tpu_custom_call" | custom-call | tf_op jit(solution)/shard_map/pallas_call | solution.py:259
  25.6 0.2 collective-permute-start.8
  25.8 0.0 collective-permute-start.7
  25.8 0.0 copy-done.15
  25.8 0.1 broadcast_add_fusion
  25.9 0.1 add.124
  26.0 0.1 add.128
  26.1 0.0 collective-permute-done.refs_0_
  26.1 0.1 collective-permute-start.1
  26.2 0.1 collective-permute-done.2.refs_1_
  26.2 3.7 %collective-permute-start.3 = (f32[520,384]{1,0:T(8,128)}, f32[520,384]{1,0:T(8,128)}, u32[]{:S(2)}, u32[]{:S(2)}) collective-permute-start(f32[520,384]{1,0:T(8,128)} %collective-permute-done.2.refs_1_), channel_id=1, source_target_pairs={{0,224},{1,33},{32,0},{33,65},{64,32},{65,97},{96,64},{97,129},{12... | collective-permute-start | bytes 2396168 | tf_op jit(solution)/shard_map/ppermute | solution.py:274
  29.9 3.5 %shard_map.125 = f32[8,2,64,384]{3,2,1,0:T(8,128)} custom-call(s32[1]{0:T(128)} %bitcast.base, f32[520,384]{1,0:T(8,128)} %collective-permute-done.refs_0_, f32[520,384]{1,0:T(8,128)} %collective-permute-done.2.refs_1_), custom_call_target="tpu_custom_call" | custom-call | flops 40000000000 | tf_op jit(solution)/shard_map/pallas_call | solution.py:89
  33.5 0.0 all-to-all-done.refs_2_
  33.5 0.0 copy-start.5
  33.5 7.1 %all-to-all-start.1 = ((f32[8,2,64,384]{3,2,1,0:T(8,128)}), f32[8,2,64,384]{3,2,1,0:T(8,128)S(1)}, u32[]{:S(2)}, u32[]{:S(2)}) async-start(f32[8,2,64,384]{3,2,1,0:T(8,128)} %shard_map.125), calls=%async_computation.1 | async-start | bytes 3145728 | tf_op jit(solution)/shard_map/all_to_all | solution.py:281
  40.6 6.4 %collective-permute-done.1.refs_0_ = f32[520,384]{1,0:T(8,128)} collective-permute-done((f32[520,384]{1,0:T(8,128)}, f32[520,384]{1,0:T(8,128)}, u32[]{:S(2)}, u32[]{:S(2)}) %collective-permute-start.1) | collective-permute-done | bytes 798752 | tf_op jit(solution)/shard_map/ppermute | solution.py:274
  47.0 0.0 collective-permute-done.3.refs_1_
  47.0 0.0 collective-permute-start.4
  47.1 3.2 %collective-permute-start.5 = (f32[520,384]{1,0:T(8,128)}, f32[520,384]{1,0:T(8,128)}, u32[]{:S(2)}, u32[]{:S(2)}) collective-permute-start(f32[520,384]{1,0:T(8,128)} %get-tuple-element.11.refs_1_), channel_id=1, source_target_pairs={{0,224},{1,33},{32,0},{33,65},{64,32},{65,97},{96,64},{97,129},{12... | collective-permute-start | bytes 2396168 | tf_op jit(solution)/shard_map/ppermute | solution.py:274
  50.3 3.5 %shard_map.132 = f32[8,2,64,384]{3,2,1,0:T(8,128)} custom-call(s32[1]{0:T(128)} %bitcast.base, f32[520,384]{1,0:T(8,128)} %get-tuple-element.10.refs_0_, f32[520,384]{1,0:T(8,128)} %get-tuple-element.11.refs_1_), custom_call_target="tpu_custom_call" | custom-call | flops 40000000000 | tf_op jit(solution)/shard_map/pallas_call | solution.py:89
  53.8 0.0 copy-start.12
  53.8 5.5 %all-to-all-done.1.refs_2_ = f32[8,2,64,384]{3,2,1,0:T(8,128)S(1)} async-done(((f32[8,2,64,384]{3,2,1,0:T(8,128)}), f32[8,2,64,384]{3,2,1,0:T(8,128)S(1)}, u32[]{:S(2)}, u32[]{:S(2)}) %all-to-all-start.1) | async-done | bytes 1572896 | tf_op jit(solution)/shard_map/all_to_all | solution.py:281
  59.3 5.4 %all-to-all-start.4 = ((f32[8,2,64,384]{3,2,1,0:T(8,128)}), f32[8,2,64,384]{3,2,1,0:T(8,128)S(1)}, u32[]{:S(2)}, u32[]{:S(2)}) async-start(f32[8,2,64,384]{3,2,1,0:T(8,128)} %shard_map.132), calls=%async_computation.4 | async-start | bytes 3145728 | tf_op jit(solution)/shard_map/all_to_all | solution.py:281
  64.7 0.1 add.133
  64.7 0.1 concatenate.3
  64.8 0.0 copy-done.12
  64.8 0.3 select_reduce_fusion
  65.1 3.8 %collective-permute-done.4.refs_0_ = f32[520,384]{1,0:T(8,128)} collective-permute-done((f32[520,384]{1,0:T(8,128)}, f32[520,384]{1,0:T(8,128)}, u32[]{:S(2)}, u32[]{:S(2)}) %collective-permute-start.4) | collective-permute-done | bytes 798752 | tf_op jit(solution)/shard_map/ppermute | solution.py:274
  68.9 0.0 collective-permute-done.5.refs_1_
  68.9 0.0 copy-done
  68.9 0.0 collective-permute-start.6
  69.0 3.4 %collective-permute-done.8.i2 = f32[128,32,128]{2,1,0:T(8,128)} collective-permute-done((f32[128,32,128]{2,1,0:T(8,128)}, f32[128,32,128]{2,1,0:T(8,128)}, u32[]{:S(2)}, u32[]{:S(2)}) %collective-permute-start.8) | collective-permute-done | bytes 2097184 | tf_op jit(solution)/shard_map/ppermute | solution.py:269
  72.3 3.1 %copy.22.refs_0_ = f32[128,32,128]{2,1,0:T(8,128)} copy(f32[128,32,128]{2,1,0:T(8,128)} %collective-permute-done.8.i2) | data formatting | bytes 4194304
  75.5 0.0 collective-permute-start.9
  75.5 3.5 %shard_map.131 = f32[8,2,64,384]{3,2,1,0:T(8,128)} custom-call(s32[1]{0:T(128)} %bitcast.base, f32[520,384]{1,0:T(8,128)} %get-tuple-element.12.refs_1_.refs_0_, f32[520,384]{1,0:T(8,128)} %get-tuple-element.15.refs_1_), custom_call_target="tpu_custom_call" | custom-call | flops 8000000000 | tf_op jit(solution)/shard_map/pallas_call | solution.py:89
  79.0 5.8 %all-to-all-done.4 = f32[8,2,64,384]{3,2,1,0:T(8,128)S(1)} async-done(((f32[8,2,64,384]{3,2,1,0:T(8,128)}), f32[8,2,64,384]{3,2,1,0:T(8,128)S(1)}, u32[]{:S(2)}, u32[]{:S(2)}) %all-to-all-start.4) | async-done | bytes 1572896 | tf_op jit(solution)/shard_map/all_to_all | solution.py:281
  84.7 4.8 %all-to-all-start.3 = ((f32[8,2,64,384]{3,2,1,0:T(8,128)}), f32[8,2,64,384]{3,2,1,0:T(8,128)S(1)}, u32[]{:S(2)}, u32[]{:S(2)}) async-start(f32[8,2,64,384]{3,2,1,0:T(8,128)} %shard_map.131), calls=%async_computation.3 | async-start | bytes 3145728 | tf_op jit(solution)/shard_map/all_to_all | solution.py:279
  89.6 0.0 collective-permute-done.6.refs_0_
  89.6 2.9 %shard_map.127 = f32[8,1,64,384]{3,2,1,0:T(8,128)} custom-call(s32[1]{0:T(128)} %bitcast.base, f32[520,384]{1,0:T(8,128)} %collective-permute-done.6.refs_0_), custom_call_target="tpu_custom_call" | custom-call | flops 30000001024 | tf_op jit(solution)/shard_map/pallas_call | solution.py:89
  92.5 0.0 copy-start.6
  92.5 0.0 collective-permute-done.7.i1
  92.5 0.0 collective-permute-done.9.i3
  92.5 8.9 %shard_map.130 = (bf16[512,4096]{1,0:T(8,128)(2,1)S(1)}, bf16[512,4096]{1,0:T(8,128)(2,1)S(1)}) custom-call(s32[8,64]{1,0:T(8,128)S(1)} %fusion.4.spot, f32[128,32,128]{2,1,0:T(8,128)} %shard_map.128.i0, f32[128,32,128]{2,1,0:T(8,128)} %collective-permute-done.7.i1, f32[128,32,128]{2,1,0:T(8,128)} %collective-permute-done.8.i2, ...), custom_call_target="tpu_custom_call" | custom-call | tf_op jit(solution)/shard_map/pallas_call | solution.py:134
  101.4 2.0 %copy-done.2 = bf16[512,4096]{1,0:T(8,128)(2,1)} copy-done((bf16[512,4096]{1,0:T(8,128)(2,1)}, bf16[512,4096]{1,0:T(8,128)(2,1)S(1)}, u32[]{:S(2)}) %copy-start.2) | copy-done | bytes 4194328
  103.4 2.0 %copy-done.3 = bf16[512,4096]{1,0:T(8,128)(2,1)} copy-done((bf16[512,4096]{1,0:T(8,128)(2,1)}, bf16[512,4096]{1,0:T(8,128)(2,1)S(1)}, u32[]{:S(2)}) %copy-start.3) | copy-done | bytes 4194328
  105.5 0.0 copy-done.1
  105.5 7.6 %shard_map.133 = (f32[512,384]{1,0:T(8,128)S(1)}, f32[512,384]{1,0:T(8,128)}) custom-call(s32[1]{0:T(128)} %bitcast.5.half, f32[2,4,1,64,384]{4,3,2,1,0:T(8,128)S(1)} %bitcast.11, f32[2,4,2,64,384]{4,3,2,1,0:T(8,128)S(1)} %bitcast.10, f32[2,4,2,64,384]{4,3,2,1,0:T(8,128)S(1)} %bitcast.12, bf16[512,4096]{1,0:T(8,128)(2,1)} %copy-done.2, ...), custom_call_target="tpu_custom_call" | custom-call | flops 8000000000 | tf_op jit(solution)/shard_map/pallas_call | solution.py:182
  113.1 0.9 copy-done.10
  114.0 1.4 collective-permute-start.10
  115.3 0.0 all-to-all-done.3.tiles
  115.3 1.1 copy-done.7
  116.5 7.8 %all-to-all-start.2 = ((f32[8,1,64,384]{3,2,1,0:T(8,128)}), f32[8,1,64,384]{3,2,1,0:T(8,128)S(1)}, u32[]{:S(2)}, u32[]{:S(2)}) async-start(f32[8,1,64,384]{3,2,1,0:T(8,128)} %shard_map.127), calls=%async_computation.2 | async-start | bytes 1572864 | tf_op jit(solution)/shard_map/all_to_all | solution.py:279
  124.3 1.4 copy-done.8
  125.7 1.1 copy-done.11
  126.8 3.4 %shard_map.134.total = f32[512,384]{1,0:T(8,128)S(1)} custom-call(f32[8,2,64,384]{3,2,1,0:T(8,128)S(1)} %copy-done.8, bf16[512,4096]{1,0:T(8,128)(2,1)} %copy-done.2, bf16[512,4096]{1,0:T(8,128)(2,1)} %copy-done.3, f32[512,384]{1,0:T(8,128)S(1)} %copy-done.11), custom_call_target="tpu_custom_call" | custom-call | flops 60000002048 | tf_op jit(solution)/shard_map/pallas_call | solution.py:226
  130.3 14.2 %all-to-all-done.2.tiles = f32[8,1,64,384]{3,2,1,0:T(8,128)S(1)} async-done(((f32[8,1,64,384]{3,2,1,0:T(8,128)}), f32[8,1,64,384]{3,2,1,0:T(8,128)S(1)}, u32[]{:S(2)}, u32[]{:S(2)}) %all-to-all-start.2) | async-done | bytes 786464 | tf_op jit(solution)/shard_map/all_to_all | solution.py:279
  144.4 0.0 collective-permute-done.10.other
  144.4 0.0 copy-done.4
  144.4 3.7 %shard_map.135 = (f32[384,512]{1,0:T(8,128)}, f32[384,512]{1,0:T(8,128)}) custom-call(f32[8,1,64,384]{3,2,1,0:T(8,128)S(1)} %all-to-all-done.2.tiles, bf16[512,4096]{1,0:T(8,128)(2,1)} %copy-done.2, bf16[512,4096]{1,0:T(8,128)(2,1)} %copy-done.3, f32[512,384]{1,0:T(8,128)S(1)} %shard_map.134.total, f32[512,384]{1,0:T(8,128)S(1)} %collective-permute-done.10.other, ...), custom_call_target="tpu_custom_call" | custom-call | tf_op jit(solution)/shard_map/pallas_call | solution.py:208
  (30 shorter events, 0.1 us)
Async XLA Ops:
  2.9 23.2 %collective-permute-start = (f32[520,384]{1,0:T(8,128)}, f32[520,384]{1,0:T(8,128)}, u32[]{:S(2)}, u32[]{:S(2)}) collective-permute-start(f32[520,384]{1,0:T(8,128)} %shard_map.122.refs_0_), channel_id=1, source_target_pairs={{0,32},{1,225},{32,64},{33,1},{64,96},{65,33},{96,128},{97,65},{12... | collective-permute-start | bytes 2396168 | tf_op jit(solution)/shard_map/ppermute | solution.py:274
  4.9 21.3 %collective-permute-start.2 = (f32[520,384]{1,0:T(8,128)}, f32[520,384]{1,0:T(8,128)}, u32[]{:S(2)}, u32[]{:S(2)}) collective-permute-start(f32[520,384]{1,0:T(8,128)} %shard_map.122.refs_0_), channel_id=1, source_target_pairs={{0,224},{1,33},{32,0},{33,65},{64,32},{65,97},{96,64},{97,129},{12... | collective-permute-start | bytes 2396168 | tf_op jit(solution)/shard_map/ppermute | solution.py:274
  11.9 21.6 %all-to-all-start = ((f32[8,1,64,384]{3,2,1,0:T(8,128)}), f32[8,1,64,384]{3,2,1,0:T(8,128)S(1)}, u32[]{:S(2)}, u32[]{:S(2)}) async-start(f32[8,1,64,384]{3,2,1,0:T(8,128)} %shard_map.123.after), calls=%async_computation | async-start | bytes 1572864 | tf_op jit(solution)/shard_map/all_to_all | solution.py:281
  19.0 6.8 %copy-start.15 = (s32[2]{0:T(128)S(1)}, s32[2]{0:T(128)}, u32[]{:S(2)}) copy-start(s32[2]{0:T(128)} %constant.112.clone) | copy-start | bytes 28
  19.0 6.8 %copy-start.16 = (s32[2]{0:T(128)S(1)}, s32[2]{0:T(128)}, u32[]{:S(2)}) copy-start(s32[2]{0:T(128)} %constant.113.clone) | copy-start | bytes 28
  19.0 7.0 %copy-start.14 = (s32[2]{0:T(128)S(1)}, s32[2]{0:T(128)}, u32[]{:S(2)}) copy-start(s32[2]{0:T(128)} %constant.114.clone) | copy-start | bytes 28
  25.6 46.8 %collective-permute-start.8 = (f32[128,32,128]{2,1,0:T(8,128)}, f32[128,32,128]{2,1,0:T(8,128)}, u32[]{:S(2)}, u32[]{:S(2)}) collective-permute-start(f32[128,32,128]{2,1,0:T(8,128)} %shard_map.128.i0), channel_id=1, source_target_pairs={{0,2},{2,0},{1,3},{3,1},{4,6},{6,4},{5,7},{7,5},{8,10},{10,8},{9,1... | collective-permute-start | bytes 6291464 | tf_op jit(solution)/shard_map/ppermute | solution.py:269
  25.8 66.7 %collective-permute-start.7 = (f32[128,32,128]{2,1,0:T(8,128)}, f32[128,32,128]{2,1,0:T(8,128)}, u32[]{:S(2)}, u32[]{:S(2)}) collective-permute-start(f32[128,32,128]{2,1,0:T(8,128)} %shard_map.128.i0), channel_id=1, source_target_pairs={{0,1},{1,0},{2,3},{3,2},{4,5},{5,4},{6,7},{7,6},{8,9},{9,8},{10,11... | collective-permute-start | bytes 6291464 | tf_op jit(solution)/shard_map/ppermute | solution.py:269
  26.1 21.0 %collective-permute-start.1 = (f32[520,384]{1,0:T(8,128)}, f32[520,384]{1,0:T(8,128)}, u32[]{:S(2)}, u32[]{:S(2)}) collective-permute-start(f32[520,384]{1,0:T(8,128)} %collective-permute-done.refs_0_), channel_id=1, source_target_pairs={{0,32},{1,225},{32,64},{33,1},{64,96},{65,33},{96,128},{97,65},{12... | collective-permute-start | bytes 2396168 | tf_op jit(solution)/shard_map/ppermute | solution.py:274
  26.2 20.8 %collective-permute-start.3 = (f32[520,384]{1,0:T(8,128)}, f32[520,384]{1,0:T(8,128)}, u32[]{:S(2)}, u32[]{:S(2)}) collective-permute-start(f32[520,384]{1,0:T(8,128)} %collective-permute-done.2.refs_1_), channel_id=1, source_target_pairs={{0,224},{1,33},{32,0},{33,65},{64,32},{65,97},{96,64},{97,129},{12... | collective-permute-start | bytes 2396168 | tf_op jit(solution)/shard_map/ppermute | solution.py:274
  33.5 13.6 %copy-start.5 = (f32[8,1,64,384]{3,2,1,0:T(8,128)}, f32[8,1,64,384]{3,2,1,0:T(8,128)S(1)}, u32[]{:S(2)}) copy-start(f32[8,1,64,384]{3,2,1,0:T(8,128)S(1)} %all-to-all-done.refs_2_) | copy-start | bytes 2359300
  33.5 25.8 %all-to-all-start.1 = ((f32[8,2,64,384]{3,2,1,0:T(8,128)}), f32[8,2,64,384]{3,2,1,0:T(8,128)S(1)}, u32[]{:S(2)}, u32[]{:S(2)}) async-start(f32[8,2,64,384]{3,2,1,0:T(8,128)} %shard_map.125), calls=%async_computation.1 | async-start | bytes 3145728 | tf_op jit(solution)/shard_map/all_to_all | solution.py:281
  47.0 21.9 %collective-permute-start.4 = (f32[520,384]{1,0:T(8,128)}, f32[520,384]{1,0:T(8,128)}, u32[]{:S(2)}, u32[]{:S(2)}) collective-permute-start(f32[520,384]{1,0:T(8,128)} %get-tuple-element.10.refs_0_), channel_id=1, source_target_pairs={{0,32},{1,225},{32,64},{33,1},{64,96},{65,33},{96,128},{97,65},{12... | collective-permute-start | bytes 2396168 | tf_op jit(solution)/shard_map/ppermute | solution.py:274
  47.1 21.9 %collective-permute-start.5 = (f32[520,384]{1,0:T(8,128)}, f32[520,384]{1,0:T(8,128)}, u32[]{:S(2)}, u32[]{:S(2)}) collective-permute-start(f32[520,384]{1,0:T(8,128)} %get-tuple-element.11.refs_1_), channel_id=1, source_target_pairs={{0,224},{1,33},{32,0},{33,65},{64,32},{65,97},{96,64},{97,129},{12... | collective-permute-start | bytes 2396168 | tf_op jit(solution)/shard_map/ppermute | solution.py:274
  53.8 11.0 %copy-start.12 = (s32[8,64]{1,0:T(8,128)S(1)}, s32[8,64]{1,0:T(8,128)}, u32[]{:S(2)}) copy-start(s32[8,64]{1,0:T(8,128)} %param.14) | copy-start | bytes 6148
  59.3 9.6 %copy-start = (f32[8,2,64,384]{3,2,1,0:T(8,128)}, f32[8,2,64,384]{3,2,1,0:T(8,128)S(1)}, u32[]{:S(2)}) copy-start(f32[8,2,64,384]{3,2,1,0:T(8,128)S(1)} %all-to-all-done.1.refs_2_) | copy-start | bytes 4718596
  59.3 25.4 %all-to-all-start.4 = ((f32[8,2,64,384]{3,2,1,0:T(8,128)}), f32[8,2,64,384]{3,2,1,0:T(8,128)S(1)}, u32[]{:S(2)}, u32[]{:S(2)}) async-start(f32[8,2,64,384]{3,2,1,0:T(8,128)} %shard_map.132), calls=%async_computation.4 | async-start | bytes 3145728 | tf_op jit(solution)/shard_map/all_to_all | solution.py:281
  64.7 4.3 %copy-start.13 = (f32[384]{0:T(512)S(1)}, f32[384]{0:T(512)}, u32[]{:S(2)}) copy-start(f32[384]{0:T(512)} %param.16) | copy-start | bytes 4612
  68.9 20.7 %collective-permute-start.6 = (f32[520,384]{1,0:T(8,128)}, f32[520,384]{1,0:T(8,128)}, u32[]{:S(2)}, u32[]{:S(2)}) collective-permute-start(f32[520,384]{1,0:T(8,128)} %get-tuple-element.12.refs_1_.refs_0_), channel_id=1, source_target_pairs={{0,32},{1,225},{32,64},{33,1},{64,96},{65,33},{96,128},{97,65},{12... | collective-permute-start | bytes 2396168 | tf_op jit(solution)/shard_map/ppermute | solution.py:274
  75.5 17.1 %collective-permute-start.9 = (f32[128,32,128]{2,1,0:T(8,128)}, f32[128,32,128]{2,1,0:T(8,128)}, u32[]{:S(2)}, u32[]{:S(2)}) collective-permute-start(f32[128,32,128]{2,1,0:T(8,128)} %shard_map.129), channel_id=1, source_target_pairs={{0,1},{1,0},{2,3},{3,2},{4,5},{5,4},{6,7},{7,6},{8,9},{9,8},{10,11... | collective-permute-start | bytes 6291464 | tf_op jit(solution)/shard_map/ppermute | solution.py:269
  84.7 30.6 %all-to-all-start.3 = ((f32[8,2,64,384]{3,2,1,0:T(8,128)}), f32[8,2,64,384]{3,2,1,0:T(8,128)S(1)}, u32[]{:S(2)}, u32[]{:S(2)}) async-start(f32[8,2,64,384]{3,2,1,0:T(8,128)} %shard_map.131), calls=%async_computation.3 | async-start | bytes 3145728 | tf_op jit(solution)/shard_map/all_to_all | solution.py:279
  92.5 13.0 %copy-start.1 = (f32[8,2,64,384]{3,2,1,0:T(8,128)S(1)}, f32[8,2,64,384]{3,2,1,0:T(8,128)}, u32[]{:S(2)}) copy-start(f32[8,2,64,384]{3,2,1,0:T(8,128)} %copy-done) | copy-start | bytes 4718596
  92.5 12.9 %copy-start.6 = (f32[8,1,64,384]{3,2,1,0:T(8,128)S(1)}, f32[8,1,64,384]{3,2,1,0:T(8,128)}, u32[]{:S(2)}) copy-start(f32[8,1,64,384]{3,2,1,0:T(8,128)} %copy-done.5) | copy-start | bytes 2359300
  101.4 2.0 %copy-start.2 = (bf16[512,4096]{1,0:T(8,128)(2,1)}, bf16[512,4096]{1,0:T(8,128)(2,1)S(1)}, u32[]{:S(2)}) copy-start(bf16[512,4096]{1,0:T(8,128)(2,1)S(1)} %get-tuple-element.13.refs_3_.refs_5_.refs_7_.left_hi) | copy-start | bytes 12582916
  103.4 2.0 %copy-start.3 = (bf16[512,4096]{1,0:T(8,128)(2,1)}, bf16[512,4096]{1,0:T(8,128)(2,1)S(1)}, u32[]{:S(2)}) copy-start(bf16[512,4096]{1,0:T(8,128)(2,1)S(1)} %get-tuple-element.14.refs_4_.refs_6_.refs_8_.left_lo) | copy-start | bytes 12582916
  113.1 0.9 copy-start.10
  114.0 30.5 %collective-permute-start.10 = (f32[512,384]{1,0:T(8,128)}, f32[512,384]{1,0:T(8,128)S(1)}, u32[]{:S(2)}, u32[]{:S(2)}) collective-permute-start(f32[512,384]{1,0:T(8,128)} %get-tuple-element.17), channel_id=1, source_target_pairs={{0,2},{2,0},{1,3},{3,1},{4,6},{6,4},{5,7},{7,5},{8,10},{10,8},{9,1... | collective-permute-start | bytes 2359304 | tf_op jit(solution)/shard_map/ppermute | solution.py:269
  115.3 1.1 copy-start.7
  116.5 27.9 %all-to-all-start.2 = ((f32[8,1,64,384]{3,2,1,0:T(8,128)}), f32[8,1,64,384]{3,2,1,0:T(8,128)S(1)}, u32[]{:S(2)}, u32[]{:S(2)}) async-start(f32[8,1,64,384]{3,2,1,0:T(8,128)} %shard_map.127), calls=%async_computation.2 | async-start | bytes 1572864 | tf_op jit(solution)/shard_map/all_to_all | solution.py:279
  124.3 1.4 copy-start.8
  125.7 1.1 copy-start.11
  126.8 17.6 %copy-start.4 = (f32[384,512]{1,0:T(8,128)S(1)}, f32[384,512]{1,0:T(8,128)}, u32[]{:S(2)}) copy-start(f32[384,512]{1,0:T(8,128)} %amp.3) | copy-start | bytes 2359300
  126.8 17.6 %copy-start.9 = (f32[512]{0:T(512)S(1)}, f32[512]{0:T(512)}, u32[]{:S(2)}) copy-start(f32[512]{0:T(512)} %param.15) | copy-start | bytes 6148

commit v5 on v4

--- a/solution.py
+++ b/solution.py
@@ -15,14 +15,19 @@
 TERM_SHARE = 16
 GROUP = 4
 NOTE = 8
-SELECT_COST = (40, 40, 40, 8, 30)
+SELECT_COST = (3, 40, 40, 15, 30)
+MORE_COST = 60
+PACK_COST = 40
+PREPARE_COST = 10
+OTHER_COST = 3
+OWN_COST = 60
 STEPS = ((0,), (1, -1), (2, -2), (3, -3), (4,))
-MIRRORED = (True, True, True, False, False)
+MIRRORED = (True, True, False, False, False)
 ANYWHERE = pl.BlockSpec(memory_space=pl.ANY)
 IN_HBM = pl.BlockSpec(memory_space=pltpu.HBM)
 INSIDE = pl.BlockSpec(memory_space=pltpu.VMEM)
 SCALARS = pl.BlockSpec(memory_space=pltpu.SMEM)
-PARAMS = pltpu.CompilerParams(vmem_limit_bytes=40 * 1024 * 1024)
+PARAMS = pltpu.CompilerParams(vmem_limit_bytes=65500 * 1024)
 
 
 def cost(micros):
@@ -53,6 +58,7 @@
     cols, rows = amp.shape
     return pl.pallas_call(
         first_kernel,
+        compiler_params=PARAMS,
         out_shape=jax.ShapeDtypeStruct((rows + NOTE, cols), jnp.float32),
         in_specs=[INSIDE, INSIDE],
         out_specs=IN_HBM,
@@ -60,9 +66,8 @@
     )(amp, send)
 
 
-def select_kernel(base, *refs):
-    owners = (len(refs) - 3)
-    sources, out, notes, sems = refs[:owners], refs[owners], refs[owners + 1], refs[owners + 2]
+def select_kernel(owners, base, *refs):
+    sources, (out, notes, sems) = refs[:owners], refs[-3:]
     rows = ROW_TILES * TILE
     reads = [
         pltpu.make_async_copy(sources[n].at[pl.ds(rows, NOTE), pl.ds(0, 128)], notes.at[n], sems.at[PLANE * owners + n])
@@ -84,21 +89,23 @@
         copy.wait()
 
 
-def select(base, sources, micros):
+def select(base, sources, after, micros):
     owners, cols = len(sources), sources[0].shape[1]
     return pl.pallas_call(
-        select_kernel,
+        functools.partial(select_kernel, owners),
+        compiler_params=PARAMS,
         out_shape=jax.ShapeDtypeStruct((PLANE, owners, TILE, cols), jnp.float32),
-        in_specs=[SCALARS] + [IN_HBM] * owners,
+        in_specs=[SCALARS] + [IN_HBM] * owners + [ANYWHERE] * len(after),
         out_specs=INSIDE,
         scratch_shapes=[pltpu.SMEM((owners, NOTE, 128), jnp.float32), pltpu.SemaphoreType.DMA(((PLANE + 1) * owners,))],
         cost_estimate=cost(micros),
-    )(base, *in_hbm(*sources))
-
-
-def prepare_kernel(spot, i0, i1, i2, i3, out_hi, out_lo, held, sems):
+    )(base, *in_hbm(*sources), *after)
+
+
+def prepare_kernel(spot, i0, i1, i2, i3, out_hi, out_lo, held, stage_hi, stage_lo, sems, out_sems):
     per = ROW_TILES * TERM_SHARE
-    g = pl.program_id(0)
+    g, groups = pl.program_id(0), OWNERS // GROUP
+    slot, width = g % 2, GROUP * TILE
 
     @pl.when(g == 0)
     def _():
@@ -109,6 +116,18 @@
         for copy in copies:
             copy.start()
         for copy in copies:
+            copy.wait()
+
+    def leave(step):
+        cols = pl.ds(pl.multiple_of(step * width, width), width)
+        return [
+            pltpu.make_async_copy(stage.at[step % 2], out.at[:, cols], out_sems.at[n, step % 2])
+            for n, (stage, out) in enumerate(((stage_hi, out_hi), (stage_lo, out_lo)))
+        ]
+
+    @pl.when(g >= 2)
+    def _():
+        for copy in leave(g - 2):
             copy.wait()
 
     low = lax.broadcasted_iota(jnp.int32, (TILE // 2, 2 * TILE), 1) < TILE
@@ -123,26 +142,36 @@
                 hi, lo = split(value)
                 rows = pl.ds(x * TILE + half * (TILE // 2), TILE // 2)
                 cols = pl.ds(pair * 2 * TILE, 2 * TILE)
-                out_hi[rows, cols] = hi
-                out_lo[rows, cols] = lo
+                stage_hi[slot, rows, cols] = hi
+                stage_lo[slot, rows, cols] = lo
+    for copy in leave(g):
+        copy.start()
+
+    @pl.when(g == groups - 1)
+    def _():
+        for copy in leave(g - 1) + leave(g):
+            copy.wait()
 
 
 def prepare(spot, pieces):
     rows, width = ROW_TILES * TILE, GROUP * TILE
     shape = jax.ShapeDtypeStruct((rows, OWNERS * TILE), jnp.bfloat16)
-    block = pl.BlockSpec((rows, width), lambda g: (0, g))
     return pl.pallas_call(
         prepare_kernel,
         grid=(OWNERS // GROUP,),
         out_shape=(shape, shape),
-        in_specs=[SCALARS] + [IN_HBM] * 4,
-        out_specs=(block, block),
+        in_specs=[SCALARS] + [ANYWHERE] * 4,
+        out_specs=(IN_HBM, IN_HBM),
         scratch_shapes=[
             pltpu.VMEM((4 * ROW_TILES * TERM_SHARE, TILE // 2, 2 * TILE), jnp.float32),
+            pltpu.VMEM((2, rows, width), jnp.bfloat16),
+            pltpu.VMEM((2, rows, width), jnp.bfloat16),
             pltpu.SemaphoreType.DMA((4,)),
+            pltpu.SemaphoreType.DMA((2, 2)),
         ],
         compiler_params=PARAMS,
-    )(spot, *in_hbm(*pieces))
+        cost_estimate=cost(PREPARE_COST),
+    )(spot, *pieces)
 
 
 def product(left_hi, left_lo, right):
@@ -152,42 +181,49 @@
     return total + jnp.dot(left_hi, hi, preferred_element_type=jnp.float32)
 
 
-def steps_kernel(count, half, *refs):
-    tiles, lefts, outs = refs[:count], refs[count : 3 * count], refs[3 * count :]
-    for which in range(2):
-        total = None
-        for n in range(count):
-            left_hi, left_lo = lefts[2 * n], lefts[2 * n + 1]
-            depth = left_hi.shape[1] // XH
-            part = pl.ds(which * depth, depth)
-            value = tiles[n][half[0] ^ which].reshape(depth, tiles[n].shape[-1])
-            term = product(left_hi[:, part], left_lo[:, part], value)
-            total = term if total is None else total + term
-        outs[which][...] = total
-
-
-def column_block(rows, depth, index):
-    return pl.BlockSpec((rows, depth), lambda g: (0, index))
+def steps_kernel(parts, half, *refs):
+    count = len(parts)
+    tiles, lefts, out = refs[:count], refs[count : 3 * count], refs[3 * count]
+    total = None
+    for n, part in enumerate(parts):
+        value = tiles[n][...].reshape(-1, tiles[n].shape[-1])
+        term = product(lefts[2 * n][...], lefts[2 * n + 1][...], value)
+        total = term if total is None else total + term
+    out[...] = total
 
 
 def full(x):
     return pl.BlockSpec(x.shape, lambda g: (0,) * x.ndim)
 
 
-def steps(half, tiles, indices, left, micros):
+def steps(half, tiles, offsets, parts, left, micros):
     rows, cols = left[0].shape[0], tiles[0].shape[-1]
-    tiles = [t.reshape(XH, Y, *t.shape[1:]) for t in tiles]
     shape = jax.ShapeDtypeStruct((rows, cols), jnp.float32)
-    blocks = [column_block(rows, PLANE * t.shape[2] * TILE, index) for t, index in zip(tiles, indices)]
-    return pl.pallas_call(
-        functools.partial(steps_kernel, len(tiles)),
-        grid=(1,),
-        out_shape=(shape, shape),
-        in_specs=[SCALARS] + [full(t) for t in tiles] + [block for block in blocks for _ in range(2)],
-        out_specs=(full(shape), full(shape)),
+    tile_specs, left_specs, lefts = [], [], []
+    for t, offset, part in zip(tiles, offsets, parts):
+        sources = PLANE if part is None else Y
+        depth = sources * t.shape[1] * TILE
+        block = (sources,) + t.shape[1:]
+        if part is None:
+            tile_specs.append(pl.BlockSpec(block, lambda g, half: (0, 0, 0, 0)))
+            index = offset // depth
+        else:
+            tile_specs.append(pl.BlockSpec(block, functools.partial(lambda p, g, half: (half[0] ^ p, 0, 0, 0), part)))
+            index = offset // depth + part
+        left_specs += [pl.BlockSpec((rows, depth), functools.partial(lambda i, g, half: (0, i), index))] * 2
+        lefts += left
+    return pl.pallas_call(
+        functools.partial(steps_kernel, parts),
+        out_shape=shape,
+        grid_spec=pltpu.PrefetchScalarGridSpec(
+            num_scalar_prefetch=1,
+            grid=(1,),
+            in_specs=tile_specs + left_specs,
+            out_specs=pl.BlockSpec((rows, cols), lambda g, half: (0, 0)),
+        ),
         compiler_params=PARAMS,
         cost_estimate=cost(micros),
-    )(half, *tiles, *(left * len(tiles)))
+    )(half, *tiles, *lefts)
 
 
 def last_kernel(tiles, left_hi, left_lo, total, other, amp, row_gap, col_gap, res, new):
@@ -201,9 +237,10 @@
     new[...] = amplitudes + residual / gap
 
 
-def last(index, tiles, left, total, other, amp, row_gap, col_gap):
+def last(offset, tiles, left, total, other, amp, row_gap, col_gap):
     rows, cols = left[0].shape[0], tiles.shape[-1]
-    block = column_block(rows, PLANE * tiles.shape[1] * TILE, index)
+    depth = PLANE * tiles.shape[1] * TILE
+    block = pl.BlockSpec((pl.Element(rows), pl.Element(depth)), lambda g: (0, offset))
     shape = jax.ShapeDtypeStruct((cols, rows), jnp.float32)
     return pl.pallas_call(
         last_kernel,
@@ -222,7 +259,7 @@
 
 def more(index, tiles, left, total, micros):
     rows = left[0].shape[0]
-    block = column_block(rows, PLANE * tiles.shape[1] * TILE, index)
+    block = pl.BlockSpec((rows, PLANE * tiles.shape[1] * TILE), lambda g: (0, index))
     return pl.pallas_call(
         more_kernel,
         grid=(1,),
@@ -241,6 +278,7 @@
 def tie(xs, after):
     return pl.pallas_call(
         tie_kernel,
+        compiler_params=PARAMS,
         out_shape=[jax.ShapeDtypeStruct(x.shape, x.dtype) for x in xs],
         in_specs=[IN_HBM] * len(xs) + [ANYWHERE] * len(after),
         out_specs=[IN_HBM] * len(xs),
@@ -259,9 +297,11 @@
     return pl.pallas_call(
         pack_kernel,
         grid=(ROW_TILES,),
+        compiler_params=PARAMS,
         out_shape=jax.ShapeDtypeStruct((ROW_TILES * TERM_SHARE,) + shape[1:], jnp.float32),
         in_specs=[pl.BlockSpec((1,) + integrals.shape[1:], lambda x: (x, 0, 0, 0)), IN_HBM],
         out_specs=pl.BlockSpec(shape, lambda x: (x, 0, 0)),
+        cost_estimate=cost(PACK_COST),
     )(integrals, *in_hbm(after))
 
 
@@ -288,8 +328,25 @@
     base, half = (z * PLANE)[None].astype(jnp.int32), half[None].astype(jnp.int32)
 
     owned = first(amplitudes, send_tiles)
+    packed = pack(integrals, owned)
+    across = swap(packed, "xl")
+    beside = swap(packed, "co")
+
+    order = []
+    for offsets, mirrored in zip(STEPS, MIRRORED):
+        places = (z - sign * jnp.array(offsets, jnp.int32)) % Z
+        turn = half[0] if mirrored else 0
+        peers = jnp.arange(PLANE, dtype=jnp.int32) ^ (turn * Y)
+        order.append((places[None, :] * PLANE + peers[:, None]).reshape(-1))
+    order = jnp.concatenate([order[n] for n in (1, 2, 3, 0, 4)])
+    mine = lax.axis_index("xl") * CO + core
+    terms = jnp.arange(OWNERS, dtype=jnp.int32)
+    term = jnp.sum(jnp.where(task_slots[:, None, :] == order[None, :, None], terms[None, None, :], 0), axis=2)
+    relative = (term // TERM_SHARE) ^ mine
+    spot = (relative * ROW_TILES + jnp.arange(ROW_TILES, dtype=jnp.int32)[:, None]) * TERM_SHARE + term % TERM_SHARE
+
     ring = {0: owned}
-    order, received = [], []
+    received, left, other = [], [], None
     for n, (offsets, mirrored) in enumerate(zip(STEPS, MIRRORED)):
         if n == Z // 2:
             ring[n] = shift(ring[n - 1], 1)
@@ -297,31 +354,17 @@
             ring[n], ring[-n] = shift(ring[n - 1], 1), shift(ring[1 - n], -1)
             if n > 1:
                 ring[n], ring[-n] = tie([ring[n], ring[-n]], [received[n - 2]])
-        outgoing = select(base, [ring[o] for o in offsets], SELECT_COST[n])
-        if n == 0:
-            packed = pack(integrals, outgoing)
+        if n == 3:
+            left = in_hbm(*prepare(spot, (packed, beside, across, swap(across, "co"))))
+        after = {0: [packed], 3: left[:1], 4: [other]}.get(n, [])
+        outgoing = select(base, [ring[o] for o in offsets], after, SELECT_COST[n])
         received.append(exchange(outgoing, mirrored))
-        places = (z - sign * jnp.array(offsets, jnp.int32)) % Z
-        turn = half[0] if mirrored else 0
-        peers = jnp.arange(PLANE, dtype=jnp.int32) ^ (turn * Y)
-        order.append((places[None, :] * PLANE + peers[:, None]).reshape(-1))
-    across = swap(packed, "xl")
-    beside = swap(packed, "co")
-    diagonal = swap(tie([across], [ring[3]])[0], "co")
-
-    order = jnp.concatenate([order[n] for n in (1, 2, 3, 0, 4)])
-
-    mine = lax.axis_index("xl") * CO + core
-    terms = jnp.arange(OWNERS, dtype=jnp.int32)
-    term = jnp.sum(jnp.where(task_slots[:, None, :] == order[None, :, None], terms[None, None, :], 0), axis=2)
-    relative = (term // TERM_SHARE) ^ mine
-    spot = (relative * ROW_TILES + jnp.arange(ROW_TILES, dtype=jnp.int32)[:, None]) * TERM_SHARE + term % TERM_SHARE
-    left = in_hbm(*prepare(spot, (packed, beside, across, diagonal)))
-
-    total, other = steps(half, received[:3], (6, 0, 1), left, 8)
+        if n == 3:
+            other = steps(half, received[:2], (3072, 0), (1, 1), left, OTHER_COST)
     other = swap(other, "xl")
-    total = more(2, received[3], left, total, 60)
-    return last(7, received[4], left, total, other, amplitudes, row_gap[None, :], column_gap[None, :])
+    total = steps(half, received[:3], (3072, 0, 1024), (0, 0, None), left, OWN_COST)
+    total = more(2, received[3], left, total, MORE_COST)
+    return last(3584, received[4], left, total, other, amplitudes, row_gap[None, :], column_gap[None, :])
 
 
 def solution(mesh):

time: 149 us -> 158 us (1.060)
  local copies, waits for them, and re-layouts: 12.1 us -> 1.55 us
  Pallas kernels: 48.8 us -> 58.5 us
  waiting for transfers between devices: 39.1 us -> 46.3 us
  other arithmetic: 0.4 us -> 3.02 us
    unnamed x35 -> x0, local copies, waits for them, and re-layouts: 11.8 us -> none
    all_to_all x2 -> x3, waiting for transfers between devices: 14.2 us -> 25.2 us  [exchange(): return lax.all_to_all(x, ('xh', 'y'), 0, 0, tiled=True)]
    all_to_all x3 -> x2, starting transfers between devices: 19.6 us -> 12.9 us  [exchange(): lax.all_to_all(x, ('xh', 'y', 'xl'), 0, 0, axis_index_groups=groups, tile...]
    all_to_all x3 -> x2, waiting for transfers between devices: 11.2 us -> 5.12 us  [exchange(): lax.all_to_all(x, ('xh', 'y', 'xl'), 0, 0, axis_index_groups=groups, tile...]
    ppermute x7, waiting for transfers between devices: 10.3 us -> 16 us  [shift(): return lax.ppermute(x, ('z', 'co'), turns)]
    all_to_all x2 -> x3, starting transfers between devices: 12.7 us -> 17.6 us  [exchange(): return lax.all_to_all(x, ('xh', 'y'), 0, 0, tiled=True)]
    pallas_call x1, Pallas kernels: 8.87 us -> 12.9 us  [prepare(): pl.pallas_call(prepare_kernel, grid=(OWNERS // GROUP,), out_shape=(shape,...]
    ppermute x4, waiting for transfers between devices: 3.37 us -> 0.01 us  [swap(): return lax.ppermute(x, axis, [(0, 1), (1, 0)])]
  transfers between devices with their start and end apart: 16 -> 16, of which waited for: 7 -> 8; matrix products, arithmetic and copies ran while one was open for 3% -> 3% of each run, Pallas kernels for 29% -> 29%
where the time goes in v5:
time: 158 us; the launch traced here: 156 us
  Pallas kernels  58.5 us (37%)
  waiting for transfers between devices  46.3 us (29%)
  starting transfers between devices  45.8 us (29%)
  other arithmetic  3.02 us (2%)
    all_to_all x3, waiting for transfers between devices, exchange(): return lax.all_to_all(x, ('xh', 'y'), 0, 0, tiled=True)  25.2 us
    all_to_all x3, starting transfers between devices, exchange(): return lax.all_to_all(x, ('xh', 'y'), 0, 0, tiled=True)  17.6 us
    pallas_call x5, Pallas kernels, select(): pl.pallas_call(functools.partial(select_kernel, owners), compiler_params=...  16.4 us
    ppermute x7, waiting for transfers between devices, shift(): return lax.ppermute(x, ('z', 'co'), turns)  16 us
    ppermute x7, starting transfers between devices, shift(): return lax.ppermute(x, ('z', 'co'), turns)  13.3 us
    pallas_call x1, Pallas kernels, prepare(): pl.pallas_call(prepare_kernel, grid=(OWNERS // GROUP,), out_shape=(shape,...  12.9 us
    all_to_all x2, starting transfers between devices, exchange(): lax.all_to_all(x, ('xh', 'y', 'xl'), 0, 0, axis_index_groups=groups, tile...  12.9 us
    pallas_call x2, Pallas kernels, steps(): pl.pallas_call(functools.partial(steps_kernel, parts), out_shape=shape, g...  10.8 us
  transfers between devices with their start and end apart: 16, of which 8 were waited for; matrix products, arithmetic and copies ran while one was open for 3% of the time, Pallas kernels for 29%

profile of v5, /device:TPU:8, one launch (start us, length us, event | category | flops | bytes accessed | tf_op | source)
XLA Modules:
  0.0 155.9 jit_solution(1776679161116109834)
XLA Ops:
  0.6 2.3 %shard_map.122.after.refs_0_ = f32[520,384]{1,0:T(8,128)} custom-call(f32[384,512]{1,0:T(8,128)} %amp.3, s32[1,64]{1,0:T(1,128)} %send.1), custom_call_target="tpu_custom_call" | custom-call | tf_op jit(solution)/shard_map/pallas_call | solution.py:59
  2.9 6.5 %shard_map.123.refs_1_.i0 = f32[128,32,128]{2,1,0:T(8,128)} custom-call(f32[8,16,64,64]{3,2,1,0:T(8,128)} %integrals.1, f32[520,384]{1,0:T(8,128)} %shard_map.122.after.refs_0_), custom_call_target="tpu_custom_call" | custom-call | flops 40000000000 | tf_op jit(solution)/shard_map/pallas_call | solution.py:297
  9.5 1.5 collective-permute-start.8
  11.0 0.0 collective-permute-start.7
  11.0 1.9 %collective-permute-start = (f32[520,384]{1,0:T(8,128)}, f32[520,384]{1,0:T(8,128)}, u32[]{:S(2)}, u32[]{:S(2)}) collective-permute-start(f32[520,384]{1,0:T(8,128)} %shard_map.122.after.refs_0_), channel_id=1, source_target_pairs={{0,32},{1,225},{32,64},{33,1},{64,96},{65,33},{96,128},{97,65},{12... | collective-permute-start | bytes 2396168 | tf_op jit(solution)/shard_map/ppermute | solution.py:314
  12.9 3.9 %collective-permute-start.2 = (f32[520,384]{1,0:T(8,128)}, f32[520,384]{1,0:T(8,128)}, u32[]{:S(2)}, u32[]{:S(2)}) collective-permute-start(f32[520,384]{1,0:T(8,128)} %shard_map.122.after.refs_0_), channel_id=1, source_target_pairs={{0,224},{1,33},{32,0},{33,65},{64,32},{65,97},{96,64},{97,129},{12... | collective-permute-start | bytes 2396168 | tf_op jit(solution)/shard_map/ppermute | solution.py:314
  16.8 2.9 %shard_map.124 = f32[8,1,64,384]{3,2,1,0:T(8,128)} custom-call(s32[1]{0:T(128)} %bitcast.base, f32[520,384]{1,0:T(8,128)} %shard_map.122.after.refs_0_, f32[128,32,128]{2,1,0:T(8,128)} %shard_map.123.refs_1_.i0), custom_call_target="tpu_custom_call" | custom-call | flops 3000000000 | tf_op jit(solution)/shard_map/pallas_call | solution.py:94
  19.8 6.5 %all-to-all-start = ((f32[8,1,64,384]{3,2,1,0:T(8,128)}), f32[8,1,64,384]{3,2,1,0:T(8,128)}, u32[]{:S(2)}, u32[]{:S(2)}) async-start(f32[8,1,64,384]{3,2,1,0:T(8,128)} %shard_map.124), calls=%async_computation | async-start | bytes 1572864 | tf_op jit(solution)/shard_map/all_to_all | solution.py:321
  26.2 0.7 fusion.9
  26.9 0.1 broadcast_add_fusion
  27.0 0.1 add.126
  27.1 0.1 add.131
  27.1 0.7 fusion.11
  27.8 0.1 add.136
  27.9 1.2 broadcast_in_dim.25.col_gap
  29.1 0.1 concatenate.3
  29.2 1.0 select_reduce_fusion
  30.2 0.6 fusion.4.spot
  30.8 2.4 %collective-permute-done.refs_0_ = f32[520,384]{1,0:T(8,128)} collective-permute-done((f32[520,384]{1,0:T(8,128)}, f32[520,384]{1,0:T(8,128)}, u32[]{:S(2)}, u32[]{:S(2)}) %collective-permute-start) | collective-permute-done | bytes 798752 | tf_op jit(solution)/shard_map/ppermute | solution.py:314
  33.2 0.0 collective-permute-start.1
  33.2 1.6 %collective-permute-done.2.refs_1_ = f32[520,384]{1,0:T(8,128)} collective-permute-done((f32[520,384]{1,0:T(8,128)}, f32[520,384]{1,0:T(8,128)}, u32[]{:S(2)}, u32[]{:S(2)}) %collective-permute-start.2) | collective-permute-done | bytes 798752 | tf_op jit(solution)/shard_map/ppermute | solution.py:314
  34.9 3.7 %collective-permute-start.3 = (f32[520,384]{1,0:T(8,128)}, f32[520,384]{1,0:T(8,128)}, u32[]{:S(2)}, u32[]{:S(2)}) collective-permute-start(f32[520,384]{1,0:T(8,128)} %collective-permute-done.2.refs_1_), channel_id=1, source_target_pairs={{0,224},{1,33},{32,0},{33,65},{64,32},{65,97},{96,64},{97,129},{12... | collective-permute-start | bytes 2396168 | tf_op jit(solution)/shard_map/ppermute | solution.py:314
  38.6 3.5 %shard_map.126 = f32[8,2,64,384]{3,2,1,0:T(8,128)} custom-call(s32[1]{0:T(128)} %bitcast.base, f32[520,384]{1,0:T(8,128)} %collective-permute-done.refs_0_, f32[520,384]{1,0:T(8,128)} %collective-permute-done.2.refs_1_), custom_call_target="tpu_custom_call" | custom-call | flops 40000000000 | tf_op jit(solution)/shard_map/pallas_call | solution.py:94
  42.1 0.0 all-to-all-done.refs_2_.refs_0_
  42.1 6.5 %all-to-all-start.1 = ((f32[8,2,64,384]{3,2,1,0:T(8,128)}), f32[8,2,64,384]{3,2,1,0:T(8,128)}, u32[]{:S(2)}, u32[]{:S(2)}) async-start(f32[8,2,64,384]{3,2,1,0:T(8,128)} %shard_map.126), calls=%async_computation.1 | async-start | bytes 3145728 | tf_op jit(solution)/shard_map/all_to_all | solution.py:321
  48.5 5.2 %collective-permute-done.1.refs_0_ = f32[520,384]{1,0:T(8,128)} collective-permute-done((f32[520,384]{1,0:T(8,128)}, f32[520,384]{1,0:T(8,128)}, u32[]{:S(2)}, u32[]{:S(2)}) %collective-permute-start.1) | collective-permute-done | bytes 798752 | tf_op jit(solution)/shard_map/ppermute | solution.py:314
  53.7 2.1 %collective-permute-done.3.refs_1_ = f32[520,384]{1,0:T(8,128)} collective-permute-done((f32[520,384]{1,0:T(8,128)}, f32[520,384]{1,0:T(8,128)}, u32[]{:S(2)}, u32[]{:S(2)}) %collective-permute-start.3) | collective-permute-done | bytes 798752 | tf_op jit(solution)/shard_map/ppermute | solution.py:314
  55.8 0.0 collective-permute-start.4
  55.8 3.7 %collective-permute-start.5 = (f32[520,384]{1,0:T(8,128)}, f32[520,384]{1,0:T(8,128)}, u32[]{:S(2)}, u32[]{:S(2)}) collective-permute-start(f32[520,384]{1,0:T(8,128)} %get-tuple-element.9.refs_1_), channel_id=1, source_target_pairs={{0,224},{1,33},{32,0},{33,65},{64,32},{65,97},{96,64},{97,129},{12... | collective-permute-start | bytes 2396168 | tf_op jit(solution)/shard_map/ppermute | solution.py:314
  59.5 0.0 collective-permute-done.8.i2
  59.5 0.0 collective-permute-start.9
  59.5 3.5 %shard_map.132 = f32[8,2,64,384]{3,2,1,0:T(8,128)} custom-call(s32[1]{0:T(128)} %bitcast.base, f32[520,384]{1,0:T(8,128)} %get-tuple-element.8.refs_0_, f32[520,384]{1,0:T(8,128)} %get-tuple-element.9.refs_1_), custom_call_target="tpu_custom_call" | custom-call | flops 40000000000 | tf_op jit(solution)/shard_map/pallas_call | solution.py:94
  63.1 5.1 %all-to-all-done.1.refs_2_.refs_1_ = f32[8,2,64,384]{3,2,1,0:T(8,128)} async-done(((f32[8,2,64,384]{3,2,1,0:T(8,128)}), f32[8,2,64,384]{3,2,1,0:T(8,128)}, u32[]{:S(2)}, u32[]{:S(2)}) %all-to-all-start.1) | async-done | bytes 1572896 | tf_op jit(solution)/shard_map/all_to_all | solution.py:321
  68.2 4.8 %all-to-all-start.4 = ((f32[8,2,64,384]{3,2,1,0:T(8,128)}), f32[8,2,64,384]{3,2,1,0:T(8,128)}, u32[]{:S(2)}, u32[]{:S(2)}) async-start(f32[8,2,64,384]{3,2,1,0:T(8,128)} %shard_map.132), calls=%async_computation.4 | async-start | bytes 3145728 | tf_op jit(solution)/shard_map/all_to_all | solution.py:319
  73.0 4.7 %collective-permute-done.4.refs_0_ = f32[520,384]{1,0:T(8,128)} collective-permute-done((f32[520,384]{1,0:T(8,128)}, f32[520,384]{1,0:T(8,128)}, u32[]{:S(2)}, u32[]{:S(2)}) %collective-permute-start.4) | collective-permute-done | bytes 798752 | tf_op jit(solution)/shard_map/ppermute | solution.py:314
  77.7 0.0 collective-permute-done.5.refs_1_
  77.7 0.0 collective-permute-start.6
  77.7 0.0 collective-permute-done.7.i1
  77.7 0.0 collective-permute-done.9.i3
  77.7 12.9 %shard_map.128 = (bf16[512,4096]{1,0:T(8,128)(2,1)}, bf16[512,4096]{1,0:T(8,128)(2,1)}) custom-call(s32[8,64]{1,0:T(8,128)} %fusion.4.spot, f32[128,32,128]{2,1,0:T(8,128)} %shard_map.123.refs_1_.i0, f32[128,32,128]{2,1,0:T(8,128)} %collective-permute-done.7.i1, f32[128,32,128]{2,1,0:T(8,128)} %collective-permute-done.8.i2, ...), custom_call_target="tpu_custom_call" | custom-call | flops 10000000000 | tf_op jit(solution)/shard_map/pallas_call | solution.py:159
  90.7 4.0 %shard_map.129.refs_1_ = f32[512,384]{1,0:T(8,128)} custom-call(s32[1]{0:T(128)} %bitcast.1.half, f32[8,1,64,384]{3,2,1,0:T(8,128)} %all-to-all-done.refs_2_.refs_0_, f32[8,2,64,384]{3,2,1,0:T(8,128)} %all-to-all-done.1.refs_2_.refs_1_, bf16[512,4096]{1,0:T(8,128)(2,1)} %get-tuple-element.11.refs_2_.refs_4_.refs_3_.refs_5_.refs_7_.left_hi, ...), custom_call_target="tpu_custom_call" | custom-call | flops 3000000000 | tf_op jit(solution)/shard_map/pallas_call | solution.py:215
  94.7 0.5 collective-permute-start.10
  95.2 3.5 %shard_map.131 = f32[8,2,64,384]{3,2,1,0:T(8,128)} custom-call(s32[1]{0:T(128)} %bitcast.base, f32[520,384]{1,0:T(8,128)} %get-tuple-element.10.refs_0_, f32[520,384]{1,0:T(8,128)} %get-tuple-element.13.refs_1_, bf16[512,4096]{1,0:T(8,128)(2,1)} %get-tuple-element.11.refs_2_.refs_4_.refs_3_.refs_5_.refs_7_.left_hi), custom_call_target="tpu_custom_call" | custom-call | flops 15000000512 | tf_op jit(solution)/shard_map/pallas_call | solution.py:94
  98.7 0.0 all-to-all-done.4.refs_2_
  98.7 7.4 %all-to-all-start.3 = ((f32[8,2,64,384]{3,2,1,0:T(8,128)}), f32[8,2,64,384]{3,2,1,0:T(8,128)}, u32[]{:S(2)}, u32[]{:S(2)}) async-start(f32[8,2,64,384]{3,2,1,0:T(8,128)} %shard_map.131), calls=%async_computation.3 | async-start | bytes 3145728 | tf_op jit(solution)/shard_map/all_to_all | solution.py:319
  106.1 6.8 %shard_map.133.total = f32[512,384]{1,0:T(8,128)} custom-call(s32[1]{0:T(128)} %bitcast.1.half, f32[8,1,64,384]{3,2,1,0:T(8,128)} %all-to-all-done.refs_2_.refs_0_, f32[8,2,64,384]{3,2,1,0:T(8,128)} %all-to-all-done.1.refs_2_.refs_1_, f32[8,2,64,384]{3,2,1,0:T(8,128)} %all-to-all-done.4.refs_2_, ...), custom_call_target="tpu_custom_call" | custom-call | flops 60000002048 | tf_op jit(solution)/shard_map/pallas_call | solution.py:215
  112.9 0.0 collective-permute-done.6.refs_0_
  112.9 2.9 %shard_map.130 = f32[8,1,64,384]{3,2,1,0:T(8,128)} custom-call(s32[1]{0:T(128)} %bitcast.base, f32[520,384]{1,0:T(8,128)} %collective-permute-done.6.refs_0_, f32[512,384]{1,0:T(8,128)} %shard_map.129.refs_1_), custom_call_target="tpu_custom_call" | custom-call | flops 30000001024 | tf_op jit(solution)/shard_map/pallas_call | solution.py:94
  115.8 18.2 %all-to-all-done.3.tiles = f32[8,2,64,384]{3,2,1,0:T(8,128)} async-done(((f32[8,2,64,384]{3,2,1,0:T(8,128)}), f32[8,2,64,384]{3,2,1,0:T(8,128)}, u32[]{:S(2)}, u32[]{:S(2)}) %all-to-all-start.3) | async-done | bytes 1572896 | tf_op jit(solution)/shard_map/all_to_all | solution.py:319
  134.0 5.4 %all-to-all-start.2 = ((f32[8,1,64,384]{3,2,1,0:T(8,128)}), f32[8,1,64,384]{3,2,1,0:T(8,128)}, u32[]{:S(2)}, u32[]{:S(2)}) async-start(f32[8,1,64,384]{3,2,1,0:T(8,128)} %shard_map.130), calls=%async_computation.2 | async-start | bytes 1572864 | tf_op jit(solution)/shard_map/all_to_all | solution.py:319
  139.3 4.9 %shard_map.134.total = f32[512,384]{1,0:T(8,128)} custom-call(f32[8,2,64,384]{3,2,1,0:T(8,128)} %all-to-all-done.3.tiles, bf16[512,4096]{1,0:T(8,128)(2,1)} %get-tuple-element.11.refs_2_.refs_4_.refs_3_.refs_5_.refs_7_.left_hi, bf16[512,4096]{1,0:T(8,128)(2,1)} %get-tuple-element.12.refs_3_.refs_5_.refs_4_.refs_6_.refs_8_.left_lo, f32[512,384]{1,0:T(8,128)} %shard_map.133.total), custom_call_target="tpu_custom_call" | custom-call | flops 60000002048 | tf_op jit(solution)/shard_map/pallas_call | solution.py:263
  144.3 7.0 %all-to-all-done.2.tiles = f32[8,1,64,384]{3,2,1,0:T(8,128)} async-done(((f32[8,1,64,384]{3,2,1,0:T(8,128)}), f32[8,1,64,384]{3,2,1,0:T(8,128)}, u32[]{:S(2)}, u32[]{:S(2)}) %all-to-all-start.2) | async-done | bytes 786464 | tf_op jit(solution)/shard_map/all_to_all | solution.py:319
  151.3 0.0 collective-permute-done.10.other
  151.3 4.6 %shard_map.135 = (f32[384,512]{1,0:T(8,128)}, f32[384,512]{1,0:T(8,128)}) custom-call(f32[8,1,64,384]{3,2,1,0:T(8,128)} %all-to-all-done.2.tiles, bf16[512,4096]{1,0:T(8,128)(2,1)} %get-tuple-element.11.refs_2_.refs_4_.refs_3_.refs_5_.refs_7_.left_hi, bf16[512,4096]{1,0:T(8,128)(2,1)} %get-tuple-element.12.refs_3_.refs_5_.refs_4_.refs_6_.refs_8_.left_lo, ...), custom_call_target="tpu_custom_call" | custom-call | tf_op jit(solution)/shard_map/pallas_call | solution.py:245
  (6 shorter events, 0.0 us)
Async XLA Ops:
  9.5 50.1 %collective-permute-start.8 = (f32[128,32,128]{2,1,0:T(8,128)}, f32[128,32,128]{2,1,0:T(8,128)}, u32[]{:S(2)}, u32[]{:S(2)}) collective-permute-start(f32[128,32,128]{2,1,0:T(8,128)} %shard_map.123.refs_1_.i0), channel_id=1, source_target_pairs={{0,2},{2,0},{1,3},{3,1},{4,6},{6,4},{5,7},{7,5},{8,10},{10,8},{9,1... | collective-permute-start | bytes 6291464 | tf_op jit(solution)/shard_map/ppermute | solution.py:309
  11.0 66.7 %collective-permute-start.7 = (f32[128,32,128]{2,1,0:T(8,128)}, f32[128,32,128]{2,1,0:T(8,128)}, u32[]{:S(2)}, u32[]{:S(2)}) collective-permute-start(f32[128,32,128]{2,1,0:T(8,128)} %shard_map.123.refs_1_.i0), channel_id=1, source_target_pairs={{0,1},{1,0},{2,3},{3,2},{4,5},{5,4},{6,7},{7,6},{8,9},{9,8},{10,11... | collective-permute-start | bytes 6291464 | tf_op jit(solution)/shard_map/ppermute | solution.py:309
  11.0 22.3 %collective-permute-start = (f32[520,384]{1,0:T(8,128)}, f32[520,384]{1,0:T(8,128)}, u32[]{:S(2)}, u32[]{:S(2)}) collective-permute-start(f32[520,384]{1,0:T(8,128)} %shard_map.122.after.refs_0_), channel_id=1, source_target_pairs={{0,32},{1,225},{32,64},{33,1},{64,96},{65,33},{96,128},{97,65},{12... | collective-permute-start | bytes 2396168 | tf_op jit(solution)/shard_map/ppermute | solution.py:314
  12.9 22.0 %collective-permute-start.2 = (f32[520,384]{1,0:T(8,128)}, f32[520,384]{1,0:T(8,128)}, u32[]{:S(2)}, u32[]{:S(2)}) collective-permute-start(f32[520,384]{1,0:T(8,128)} %shard_map.122.after.refs_0_), channel_id=1, source_target_pairs={{0,224},{1,33},{32,0},{33,65},{64,32},{65,97},{96,64},{97,129},{12... | collective-permute-start | bytes 2396168 | tf_op jit(solution)/shard_map/ppermute | solution.py:314
  19.8 22.3 %all-to-all-start = ((f32[8,1,64,384]{3,2,1,0:T(8,128)}), f32[8,1,64,384]{3,2,1,0:T(8,128)}, u32[]{:S(2)}, u32[]{:S(2)}) async-start(f32[8,1,64,384]{3,2,1,0:T(8,128)} %shard_map.124), calls=%async_computation | async-start | bytes 1572864 | tf_op jit(solution)/shard_map/all_to_all | solution.py:321
  33.2 20.5 %collective-permute-start.1 = (f32[520,384]{1,0:T(8,128)}, f32[520,384]{1,0:T(8,128)}, u32[]{:S(2)}, u32[]{:S(2)}) collective-permute-start(f32[520,384]{1,0:T(8,128)} %collective-permute-done.refs_0_), channel_id=1, source_target_pairs={{0,32},{1,225},{32,64},{33,1},{64,96},{65,33},{96,128},{97,65},{12... | collective-permute-start | bytes 2396168 | tf_op jit(solution)/shard_map/ppermute | solution.py:314
  34.9 21.0 %collective-permute-start.3 = (f32[520,384]{1,0:T(8,128)}, f32[520,384]{1,0:T(8,128)}, u32[]{:S(2)}, u32[]{:S(2)}) collective-permute-start(f32[520,384]{1,0:T(8,128)} %collective-permute-done.2.refs_1_), channel_id=1, source_target_pairs={{0,224},{1,33},{32,0},{33,65},{64,32},{65,97},{96,64},{97,129},{12... | collective-permute-start | bytes 2396168 | tf_op jit(solution)/shard_map/ppermute | solution.py:314
  42.1 26.1 %all-to-all-start.1 = ((f32[8,2,64,384]{3,2,1,0:T(8,128)}), f32[8,2,64,384]{3,2,1,0:T(8,128)}, u32[]{:S(2)}, u32[]{:S(2)}) async-start(f32[8,2,64,384]{3,2,1,0:T(8,128)} %shard_map.126), calls=%async_computation.1 | async-start | bytes 3145728 | tf_op jit(solution)/shard_map/all_to_all | solution.py:321
  55.8 21.9 %collective-permute-start.4 = (f32[520,384]{1,0:T(8,128)}, f32[520,384]{1,0:T(8,128)}, u32[]{:S(2)}, u32[]{:S(2)}) collective-permute-start(f32[520,384]{1,0:T(8,128)} %get-tuple-element.8.refs_0_), channel_id=1, source_target_pairs={{0,32},{1,225},{32,64},{33,1},{64,96},{65,33},{96,128},{97,65},{12... | collective-permute-start | bytes 2396168 | tf_op jit(solution)/shard_map/ppermute | solution.py:314
  55.8 21.9 %collective-permute-start.5 = (f32[520,384]{1,0:T(8,128)}, f32[520,384]{1,0:T(8,128)}, u32[]{:S(2)}, u32[]{:S(2)}) collective-permute-start(f32[520,384]{1,0:T(8,128)} %get-tuple-element.9.refs_1_), channel_id=1, source_target_pairs={{0,224},{1,33},{32,0},{33,65},{64,32},{65,97},{96,64},{97,129},{12... | collective-permute-start | bytes 2396168 | tf_op jit(solution)/shard_map/ppermute | solution.py:314
  59.5 18.2 %collective-permute-start.9 = (f32[128,32,128]{2,1,0:T(8,128)}, f32[128,32,128]{2,1,0:T(8,128)}, u32[]{:S(2)}, u32[]{:S(2)}) collective-permute-start(f32[128,32,128]{2,1,0:T(8,128)} %collective-permute-done.8.i2), channel_id=1, source_target_pairs={{0,1},{1,0},{2,3},{3,2},{4,5},{5,4},{6,7},{7,6},{8,9},{9,8},{10,11... | collective-permute-start | bytes 6291464 | tf_op jit(solution)/shard_map/ppermute | solution.py:309
  68.2 30.6 %all-to-all-start.4 = ((f32[8,2,64,384]{3,2,1,0:T(8,128)}), f32[8,2,64,384]{3,2,1,0:T(8,128)}, u32[]{:S(2)}, u32[]{:S(2)}) async-start(f32[8,2,64,384]{3,2,1,0:T(8,128)} %shard_map.132), calls=%async_computation.4 | async-start | bytes 3145728 | tf_op jit(solution)/shard_map/all_to_all | solution.py:319
  77.7 35.2 %collective-permute-start.6 = (f32[520,384]{1,0:T(8,128)}, f32[520,384]{1,0:T(8,128)}, u32[]{:S(2)}, u32[]{:S(2)}) collective-permute-start(f32[520,384]{1,0:T(8,128)} %get-tuple-element.10.refs_0_), channel_id=1, source_target_pairs={{0,32},{1,225},{32,64},{33,1},{64,96},{65,33},{96,128},{97,65},{12... | collective-permute-start | bytes 2396168 | tf_op jit(solution)/shard_map/ppermute | solution.py:314
  94.7 56.6 %collective-permute-start.10 = (f32[512,384]{1,0:T(8,128)}, f32[512,384]{1,0:T(8,128)}, u32[]{:S(2)}, u32[]{:S(2)}) collective-permute-start(f32[512,384]{1,0:T(8,128)} %shard_map.129.refs_1_), channel_id=1, source_target_pairs={{0,2},{2,0},{1,3},{3,1},{4,6},{6,4},{5,7},{7,5},{8,10},{10,8},{9,1... | collective-permute-start | bytes 2359304 | tf_op jit(solution)/shard_map/ppermute | solution.py:309
  98.7 35.2 %all-to-all-start.3 = ((f32[8,2,64,384]{3,2,1,0:T(8,128)}), f32[8,2,64,384]{3,2,1,0:T(8,128)}, u32[]{:S(2)}, u32[]{:S(2)}) async-start(f32[8,2,64,384]{3,2,1,0:T(8,128)} %shard_map.131), calls=%async_computation.3 | async-start | bytes 3145728 | tf_op jit(solution)/shard_map/all_to_all | solution.py:319
  134.0 17.3 %all-to-all-start.2 = ((f32[8,1,64,384]{3,2,1,0:T(8,128)}), f32[8,1,64,384]{3,2,1,0:T(8,128)}, u32[]{:S(2)}, u32[]{:S(2)}) async-start(f32[8,1,64,384]{3,2,1,0:T(8,128)} %shard_map.130), calls=%async_computation.2 | async-start | bytes 1572864 | tf_op jit(solution)/shard_map/all_to_all | solution.py:319

commit v6 on v4

--- a/solution.py
+++ b/solution.py
@@ -15,14 +15,19 @@
 TERM_SHARE = 16
 GROUP = 4
 NOTE = 8
-SELECT_COST = (40, 40, 40, 8, 30)
+SELECT_COST = (40, 40, 40, 15, 30)
+MORE_COST = 60
+PACK_COST = 40
+PREPARE_COST = 3
+OTHER_COST = 3
+OWN_COST = 10
 STEPS = ((0,), (1, -1), (2, -2), (3, -3), (4,))
 MIRRORED = (True, True, True, False, False)
 ANYWHERE = pl.BlockSpec(memory_space=pl.ANY)
 IN_HBM = pl.BlockSpec(memory_space=pltpu.HBM)
 INSIDE = pl.BlockSpec(memory_space=pltpu.VMEM)
 SCALARS = pl.BlockSpec(memory_space=pltpu.SMEM)
-PARAMS = pltpu.CompilerParams(vmem_limit_bytes=40 * 1024 * 1024)
+PARAMS = pltpu.CompilerParams(vmem_limit_bytes=65500 * 1024)
 
 
 def cost(micros):
@@ -53,6 +58,7 @@
     cols, rows = amp.shape
     return pl.pallas_call(
         first_kernel,
+        compiler_params=PARAMS,
         out_shape=jax.ShapeDtypeStruct((rows + NOTE, cols), jnp.float32),
         in_specs=[INSIDE, INSIDE],
         out_specs=IN_HBM,
@@ -88,6 +94,7 @@
     owners, cols = len(sources), sources[0].shape[1]
     return pl.pallas_call(
         select_kernel,
+        compiler_params=PARAMS,
         out_shape=jax.ShapeDtypeStruct((PLANE, owners, TILE, cols), jnp.float32),
         in_specs=[SCALARS] + [IN_HBM] * owners,
         out_specs=INSIDE,
@@ -142,6 +149,7 @@
             pltpu.SemaphoreType.DMA((4,)),
         ],
         compiler_params=PARAMS,
+        cost_estimate=cost(PREPARE_COST),
     )(spot, *in_hbm(*pieces))
 
 
@@ -152,42 +160,49 @@
     return total + jnp.dot(left_hi, hi, preferred_element_type=jnp.float32)
 
 
-def steps_kernel(count, half, *refs):
-    tiles, lefts, outs = refs[:count], refs[count : 3 * count], refs[3 * count :]
-    for which in range(2):
-        total = None
-        for n in range(count):
-            left_hi, left_lo = lefts[2 * n], lefts[2 * n + 1]
-            depth = left_hi.shape[1] // XH
-            part = pl.ds(which * depth, depth)
-            value = tiles[n][half[0] ^ which].reshape(depth, tiles[n].shape[-1])
-            term = product(left_hi[:, part], left_lo[:, part], value)
-            total = term if total is None else total + term
-        outs[which][...] = total
-
-
-def column_block(rows, depth, index):
-    return pl.BlockSpec((rows, depth), lambda g: (0, index))
+def steps_kernel(parts, half, *refs):
+    count = len(parts)
+    tiles, lefts, out = refs[:count], refs[count : 3 * count], refs[3 * count]
+    total = None
+    for n, part in enumerate(parts):
+        value = tiles[n][...].reshape(-1, tiles[n].shape[-1])
+        term = product(lefts[2 * n][...], lefts[2 * n + 1][...], value)
+        total = term if total is None else total + term
+    out[...] = total
 
 
 def full(x):
     return pl.BlockSpec(x.shape, lambda g: (0,) * x.ndim)
 
 
-def steps(half, tiles, indices, left, micros):
+def steps(half, tiles, offsets, parts, left, micros):
     rows, cols = left[0].shape[0], tiles[0].shape[-1]
-    tiles = [t.reshape(XH, Y, *t.shape[1:]) for t in tiles]
     shape = jax.ShapeDtypeStruct((rows, cols), jnp.float32)
-    blocks = [column_block(rows, PLANE * t.shape[2] * TILE, index) for t, index in zip(tiles, indices)]
-    return pl.pallas_call(
-        functools.partial(steps_kernel, len(tiles)),
-        grid=(1,),
-        out_shape=(shape, shape),
-        in_specs=[SCALARS] + [full(t) for t in tiles] + [block for block in blocks for _ in range(2)],
-        out_specs=(full(shape), full(shape)),
+    tile_specs, left_specs, lefts = [], [], []
+    for t, offset, part in zip(tiles, offsets, parts):
+        sources = PLANE if part is None else Y
+        depth = sources * t.shape[1] * TILE
+        block = (sources,) + t.shape[1:]
+        if part is None:
+            tile_specs.append(pl.BlockSpec(block, lambda g, half: (0, 0, 0, 0)))
+            index = offset // depth
+        else:
+            tile_specs.append(pl.BlockSpec(block, functools.partial(lambda p, g, half: (half[0] ^ p, 0, 0, 0), part)))
+            index = offset // depth + part
+        left_specs += [pl.BlockSpec((rows, depth), functools.partial(lambda i, g, half: (0, i), index))] * 2
+        lefts += left
+    return pl.pallas_call(
+        functools.partial(steps_kernel, parts),
+        out_shape=shape,
+        grid_spec=pltpu.PrefetchScalarGridSpec(
+            num_scalar_prefetch=1,
+            grid=(1,),
+            in_specs=tile_specs + left_specs,
+            out_specs=pl.BlockSpec((rows, cols), lambda g, half: (0, 0)),
+        ),
         compiler_params=PARAMS,
         cost_estimate=cost(micros),
-    )(half, *tiles, *(left * len(tiles)))
+    )(half, *tiles, *lefts)
 
 
 def last_kernel(tiles, left_hi, left_lo, total, other, amp, row_gap, col_gap, res, new):
@@ -201,9 +216,10 @@
     new[...] = amplitudes + residual / gap
 
 
-def last(index, tiles, left, total, other, amp, row_gap, col_gap):
+def last(offset, tiles, left, total, other, amp, row_gap, col_gap):
     rows, cols = left[0].shape[0], tiles.shape[-1]
-    block = column_block(rows, PLANE * tiles.shape[1] * TILE, index)
+    depth = PLANE * tiles.shape[1] * TILE
+    block = pl.BlockSpec((pl.Element(rows), pl.Element(depth)), lambda g: (0, offset))
     shape = jax.ShapeDtypeStruct((cols, rows), jnp.float32)
     return pl.pallas_call(
         last_kernel,
@@ -222,7 +238,7 @@
 
 def more(index, tiles, left, total, micros):
     rows = left[0].shape[0]
-    block = column_block(rows, PLANE * tiles.shape[1] * TILE, index)
+    block = pl.BlockSpec((rows, PLANE * tiles.shape[1] * TILE), lambda g: (0, index))
     return pl.pallas_call(
         more_kernel,
         grid=(1,),
@@ -241,6 +257,7 @@
 def tie(xs, after):
     return pl.pallas_call(
         tie_kernel,
+        compiler_params=PARAMS,
         out_shape=[jax.ShapeDtypeStruct(x.shape, x.dtype) for x in xs],
         in_specs=[IN_HBM] * len(xs) + [ANYWHERE] * len(after),
         out_specs=[IN_HBM] * len(xs),
@@ -259,9 +276,11 @@
     return pl.pallas_call(
         pack_kernel,
         grid=(ROW_TILES,),
+        compiler_params=PARAMS,
         out_shape=jax.ShapeDtypeStruct((ROW_TILES * TERM_SHARE,) + shape[1:], jnp.float32),
         in_specs=[pl.BlockSpec((1,) + integrals.shape[1:], lambda x: (x, 0, 0, 0)), IN_HBM],
         out_specs=pl.BlockSpec(shape, lambda x: (x, 0, 0)),
+        cost_estimate=cost(PACK_COST),
     )(integrals, *in_hbm(after))
 
 
@@ -307,7 +326,8 @@
         order.append((places[None, :] * PLANE + peers[:, None]).reshape(-1))
     across = swap(packed, "xl")
     beside = swap(packed, "co")
-    diagonal = swap(tie([across], [ring[3]])[0], "co")
+    (across,) = tie([across], [ring[3]])
+    diagonal = swap(across, "co")
 
     order = jnp.concatenate([order[n] for n in (1, 2, 3, 0, 4)])
 
@@ -318,10 +338,11 @@
     spot = (relative * ROW_TILES + jnp.arange(ROW_TILES, dtype=jnp.int32)[:, None]) * TERM_SHARE + term % TERM_SHARE
     left = in_hbm(*prepare(spot, (packed, beside, across, diagonal)))
 
-    total, other = steps(half, received[:3], (6, 0, 1), left, 8)
+    other = steps(half, received[:3], (3072, 0, 1024), (1, 1, 1), left, OTHER_COST)
     other = swap(other, "xl")
-    total = more(2, received[3], left, total, 60)
-    return last(7, received[4], left, total, other, amplitudes, row_gap[None, :], column_gap[None, :])
+    total = steps(half, received[:3], (3072, 0, 1024), (0, 0, 0), left, OWN_COST)
+    total = more(2, received[3], left, total, MORE_COST)
+    return last(3584, received[4], left, total, other, amplitudes, row_gap[None, :], column_gap[None, :])
 
 
 def solution(mesh):

time: 149 us -> 151 us (1.013); the launches traced: 148 us -> 148 us
  local copies, waits for them, and re-layouts: 12.1 us -> 1.6 us
  Pallas kernels: 48.8 us -> 58.6 us
  waiting for transfers between devices: 39.1 us -> 36.4 us
  other arithmetic: 0.4 us -> 3.02 us
    unnamed x35 -> x0, local copies, waits for them, and re-layouts: 11.8 us -> none
    ppermute x7, waiting for transfers between devices: 10.3 us -> 21.4 us  [shift(): return lax.ppermute(x, ('z', 'co'), turns)]
    all_to_all x3, waiting for transfers between devices: 11.2 us -> 4.86 us  [exchange(): lax.all_to_all(x, ('xh', 'y', 'xl'), 0, 0, axis_index_groups=groups, tile...]
    pallas_call x1, Pallas kernels: 8.87 us -> 13.2 us  [prepare(): pl.pallas_call(prepare_kernel, grid=(OWNERS // GROUP,), out_shape=(shape,...]
    all_to_all x2, waiting for transfers between devices: 14.2 us -> 10.1 us  [exchange(): return lax.all_to_all(x, ('xh', 'y'), 0, 0, tiled=True)]
    ppermute x4, waiting for transfers between devices: 3.37 us -> 0.01 us  [swap(): return lax.ppermute(x, axis, [(0, 1), (1, 0)])]
    pallas_call x11 -> x12, Pallas kernels: 32.8 us -> 35.9 us  [the longest x5 16.4 us: select(): pl.pallas_call(select_kernel, compiler_params=PARAMS, out_shape=jax.Shape...]
    all_to_all x2, starting transfers between devices: 12.7 us -> 15.4 us  [exchange(): return lax.all_to_all(x, ('xh', 'y'), 0, 0, tiled=True)]
  transfers between devices with their start and end apart: 16 -> 16, of which waited for: 7 -> 5; matrix products, arithmetic and copies ran while one was open for 3% -> 3% of each run, Pallas kernels for 29% -> 35%
where the time goes in v6:
time: 151 us; the launch traced here: 148 us
  Pallas kernels  58.6 us (39%)
  starting transfers between devices  48 us (32%)
  waiting for transfers between devices  36.4 us (24%)
  other arithmetic  3.02 us (2%)
  local copies, waits for them, and re-layouts  1.6 us (1%)
    ppermute x7, waiting for transfers between devices, shift(): return lax.ppermute(x, ('z', 'co'), turns)  21.4 us
    all_to_all x3, starting transfers between devices, exchange(): lax.all_to_all(x, ('xh', 'y', 'xl'), 0, 0, axis_index_groups=groups, tile...  19.2 us
    pallas_call x5, Pallas kernels, select(): pl.pallas_call(select_kernel, compiler_params=PARAMS, out_shape=jax.Shape...  16.4 us
    all_to_all x2, starting transfers between devices, exchange(): return lax.all_to_all(x, ('xh', 'y'), 0, 0, tiled=True)  15.4 us
    pallas_call x1, Pallas kernels, prepare(): pl.pallas_call(prepare_kernel, grid=(OWNERS // GROUP,), out_shape=(shape,...  13.2 us
    ppermute x7, starting transfers between devices, shift(): return lax.ppermute(x, ('z', 'co'), turns)  12.5 us
    pallas_call x2, Pallas kernels, steps(): pl.pallas_call(functools.partial(steps_kernel, parts), out_shape=shape, g...  10.7 us
    all_to_all x2, waiting for transfers between devices, exchange(): return lax.all_to_all(x, ('xh', 'y'), 0, 0, tiled=True)  10.1 us
  transfers between devices with their start and end apart: 16, of which 5 were waited for; matrix products, arithmetic and copies ran while one was open for 3% of the time, Pallas kernels for 35%

profile of v6, /device:TPU:8, one launch (start us, length us, event | category | flops | bytes accessed | tf_op | source)
XLA Modules:
  0.0 148.4 jit_solution(253170697981501820)
XLA Ops:
  0.6 2.3 %shard_map.122.refs_0_ = f32[520,384]{1,0:T(8,128)} custom-call(f32[384,512]{1,0:T(8,128)} %amp.3, s32[1,64]{1,0:T(1,128)} %send.1), custom_call_target="tpu_custom_call" | custom-call | tf_op jit(solution)/shard_map/pallas_call | solution.py:59
  2.9 2.0 %collective-permute-start = (f32[520,384]{1,0:T(8,128)}, f32[520,384]{1,0:T(8,128)}, u32[]{:S(2)}, u32[]{:S(2)}) collective-permute-start(f32[520,384]{1,0:T(8,128)} %shard_map.122.refs_0_), channel_id=1, source_target_pairs={{0,32},{1,225},{32,64},{33,1},{64,96},{65,33},{96,128},{97,65},{12... | collective-permute-start | bytes 2396168 | tf_op jit(solution)/shard_map/ppermute | solution.py:293
  4.9 4.0 %collective-permute-start.2 = (f32[520,384]{1,0:T(8,128)}, f32[520,384]{1,0:T(8,128)}, u32[]{:S(2)}, u32[]{:S(2)}) collective-permute-start(f32[520,384]{1,0:T(8,128)} %shard_map.122.refs_0_), channel_id=1, source_target_pairs={{0,224},{1,33},{32,0},{33,65},{64,32},{65,97},{96,64},{97,129},{12... | collective-permute-start | bytes 2396168 | tf_op jit(solution)/shard_map/ppermute | solution.py:293
  9.0 2.9 %shard_map.123.after = f32[8,1,64,384]{3,2,1,0:T(8,128)} custom-call(s32[1]{0:T(128)} %bitcast.base, f32[520,384]{1,0:T(8,128)} %shard_map.122.refs_0_), custom_call_target="tpu_custom_call" | custom-call | flops 40000000000 | tf_op jit(solution)/shard_map/pallas_call | solution.py:95
  11.9 7.1 %all-to-all-start = ((f32[8,1,64,384]{3,2,1,0:T(8,128)}), f32[8,1,64,384]{3,2,1,0:T(8,128)}, u32[]{:S(2)}, u32[]{:S(2)}) async-start(f32[8,1,64,384]{3,2,1,0:T(8,128)} %shard_map.123.after), calls=%async_computation | async-start | bytes 1572864 | tf_op jit(solution)/shard_map/all_to_all | solution.py:300
  19.0 6.5 %shard_map.128.i0 = f32[128,32,128]{2,1,0:T(8,128)} custom-call(f32[8,16,64,64]{3,2,1,0:T(8,128)} %integrals.1, f32[8,1,64,384]{3,2,1,0:T(8,128)} %shard_map.123.after), custom_call_target="tpu_custom_call" | custom-call | flops 40000000000 | tf_op jit(solution)/shard_map/pallas_call | solution.py:276
  25.5 0.2 collective-permute-start.8
  25.8 0.0 collective-permute-start.7
  25.8 0.7 fusion.9
  26.5 0.1 broadcast_add_fusion
  26.5 0.1 add.124
  26.6 0.1 add.128
  26.7 0.7 fusion.11
  27.4 0.1 add.133
  27.5 1.3 broadcast_in_dim.25.col_gap
  28.7 0.1 concatenate.3
  28.8 1.0 select_reduce_fusion
  29.8 0.6 fusion.4.spot
  30.4 0.0 collective-permute-done.refs_0_
  30.4 0.0 collective-permute-start.1
  30.4 0.0 collective-permute-done.2.refs_1_
  30.4 3.2 %collective-permute-start.3 = (f32[520,384]{1,0:T(8,128)}, f32[520,384]{1,0:T(8,128)}, u32[]{:S(2)}, u32[]{:S(2)}) collective-permute-start(f32[520,384]{1,0:T(8,128)} %collective-permute-done.2.refs_1_), channel_id=1, source_target_pairs={{0,224},{1,33},{32,0},{33,65},{64,32},{65,97},{96,64},{97,129},{12... | collective-permute-start | bytes 2396168 | tf_op jit(solution)/shard_map/ppermute | solution.py:293
  33.6 3.5 %shard_map.125 = f32[8,2,64,384]{3,2,1,0:T(8,128)} custom-call(s32[1]{0:T(128)} %bitcast.base, f32[520,384]{1,0:T(8,128)} %collective-permute-done.refs_0_, f32[520,384]{1,0:T(8,128)} %collective-permute-done.2.refs_1_), custom_call_target="tpu_custom_call" | custom-call | flops 40000000000 | tf_op jit(solution)/shard_map/pallas_call | solution.py:95
  37.2 0.0 all-to-all-done.refs_2_.refs_0_
  37.2 6.7 %all-to-all-start.1 = ((f32[8,2,64,384]{3,2,1,0:T(8,128)}), f32[8,2,64,384]{3,2,1,0:T(8,128)}, u32[]{:S(2)}, u32[]{:S(2)}) async-start(f32[8,2,64,384]{3,2,1,0:T(8,128)} %shard_map.125), calls=%async_computation.1 | async-start | bytes 3145728 | tf_op jit(solution)/shard_map/all_to_all | solution.py:300
  43.9 7.5 %collective-permute-done.1.refs_0_ = f32[520,384]{1,0:T(8,128)} collective-permute-done((f32[520,384]{1,0:T(8,128)}, f32[520,384]{1,0:T(8,128)}, u32[]{:S(2)}, u32[]{:S(2)}) %collective-permute-start.1) | collective-permute-done | bytes 798752 | tf_op jit(solution)/shard_map/ppermute | solution.py:293
  51.4 0.0 collective-permute-done.3.refs_1_
  51.4 0.0 collective-permute-start.4
  51.4 3.2 %collective-permute-start.5 = (f32[520,384]{1,0:T(8,128)}, f32[520,384]{1,0:T(8,128)}, u32[]{:S(2)}, u32[]{:S(2)}) collective-permute-start(f32[520,384]{1,0:T(8,128)} %get-tuple-element.9.refs_1_), channel_id=1, source_target_pairs={{0,224},{1,33},{32,0},{33,65},{64,32},{65,97},{96,64},{97,129},{12... | collective-permute-start | bytes 2396168 | tf_op jit(solution)/shard_map/ppermute | solution.py:293
  54.6 3.5 %shard_map.132 = f32[8,2,64,384]{3,2,1,0:T(8,128)} custom-call(s32[1]{0:T(128)} %bitcast.base, f32[520,384]{1,0:T(8,128)} %get-tuple-element.8.refs_0_, f32[520,384]{1,0:T(8,128)} %get-tuple-element.9.refs_1_), custom_call_target="tpu_custom_call" | custom-call | flops 40000000000 | tf_op jit(solution)/shard_map/pallas_call | solution.py:95
  58.1 4.9 %all-to-all-done.1.refs_2_.refs_1_ = f32[8,2,64,384]{3,2,1,0:T(8,128)} async-done(((f32[8,2,64,384]{3,2,1,0:T(8,128)}), f32[8,2,64,384]{3,2,1,0:T(8,128)}, u32[]{:S(2)}, u32[]{:S(2)}) %all-to-all-start.1) | async-done | bytes 1572896 | tf_op jit(solution)/shard_map/all_to_all | solution.py:300
  63.0 5.4 %all-to-all-start.4 = ((f32[8,2,64,384]{3,2,1,0:T(8,128)}), f32[8,2,64,384]{3,2,1,0:T(8,128)}, u32[]{:S(2)}, u32[]{:S(2)}) async-start(f32[8,2,64,384]{3,2,1,0:T(8,128)} %shard_map.132), calls=%async_computation.4 | async-start | bytes 3145728 | tf_op jit(solution)/shard_map/all_to_all | solution.py:300
  68.4 4.4 %collective-permute-done.4.refs_0_ = f32[520,384]{1,0:T(8,128)} collective-permute-done((f32[520,384]{1,0:T(8,128)}, f32[520,384]{1,0:T(8,128)}, u32[]{:S(2)}, u32[]{:S(2)}) %collective-permute-start.4) | collective-permute-done | bytes 798752 | tf_op jit(solution)/shard_map/ppermute | solution.py:293
  72.8 0.0 collective-permute-done.5.refs_1_
  72.8 0.0 collective-permute-start.6
  72.8 0.0 collective-permute-done.8.refs_0_
  72.8 0.7 collective-permute-start.9
  73.5 3.5 %shard_map.131 = f32[8,2,64,384]{3,2,1,0:T(8,128)} custom-call(s32[1]{0:T(128)} %bitcast.base, f32[520,384]{1,0:T(8,128)} %get-tuple-element.10.refs_1_.refs_0_, f32[520,384]{1,0:T(8,128)} %get-tuple-element.13.refs_1_), custom_call_target="tpu_custom_call" | custom-call | flops 15000000512 | tf_op jit(solution)/shard_map/pallas_call | solution.py:95
  77.0 9.4 %collective-permute-done.6.refs_0_ = f32[520,384]{1,0:T(8,128)} collective-permute-done((f32[520,384]{1,0:T(8,128)}, f32[520,384]{1,0:T(8,128)}, u32[]{:S(2)}, u32[]{:S(2)}) %collective-permute-start.6) | collective-permute-done | bytes 798752 | tf_op jit(solution)/shard_map/ppermute | solution.py:293
  86.5 2.9 %shard_map.127 = f32[8,1,64,384]{3,2,1,0:T(8,128)} custom-call(s32[1]{0:T(128)} %bitcast.base, f32[520,384]{1,0:T(8,128)} %collective-permute-done.6.refs_0_), custom_call_target="tpu_custom_call" | custom-call | flops 30000001024 | tf_op jit(solution)/shard_map/pallas_call | solution.py:95
  89.4 0.0 all-to-all-done.4.refs_2_
  89.4 8.2 %all-to-all-start.3 = ((f32[8,2,64,384]{3,2,1,0:T(8,128)}), f32[8,2,64,384]{3,2,1,0:T(8,128)}, u32[]{:S(2)}, u32[]{:S(2)}) async-start(f32[8,2,64,384]{3,2,1,0:T(8,128)} %shard_map.131), calls=%async_computation.3 | async-start | bytes 3145728 | tf_op jit(solution)/shard_map/all_to_all | solution.py:298
  97.5 0.0 collective-permute-done.7.i1
  97.5 0.0 collective-permute-done.9.i3
  97.5 13.2 %shard_map.130 = (bf16[512,4096]{1,0:T(8,128)(2,1)}, bf16[512,4096]{1,0:T(8,128)(2,1)}) custom-call(s32[8,64]{1,0:T(8,128)} %fusion.4.spot, f32[128,32,128]{2,1,0:T(8,128)} %shard_map.128.i0, f32[128,32,128]{2,1,0:T(8,128)} %collective-permute-done.7.i1, f32[128,32,128]{2,1,0:T(8,128)} %shard_map.129.i2, f32[128,32,128]{2,1,0:T(8,128)} %collective-permute-done.9.i3), custom_call_target="tpu_custom_call" | custom-call | flops 3000000000 | tf_op jit(solution)/shard_map/pallas_call | solution.py:141
  110.7 5.4 %shard_map.135 = f32[512,384]{1,0:T(8,128)} custom-call(s32[1]{0:T(128)} %bitcast.5.half, f32[8,1,64,384]{3,2,1,0:T(8,128)} %all-to-all-done.refs_2_.refs_0_, f32[8,2,64,384]{3,2,1,0:T(8,128)} %all-to-all-done.1.refs_2_.refs_1_, f32[8,2,64,384]{3,2,1,0:T(8,128)} %all-to-all-done.4.refs_2_, ...), custom_call_target="tpu_custom_call" | custom-call | flops 3000000000 | tf_op jit(solution)/shard_map/pallas_call | solution.py:194
  116.1 0.0 collective-permute-start.10
  116.1 5.4 %shard_map.133.total = f32[512,384]{1,0:T(8,128)} custom-call(s32[1]{0:T(128)} %bitcast.5.half, f32[8,1,64,384]{3,2,1,0:T(8,128)} %all-to-all-done.refs_2_.refs_0_, f32[8,2,64,384]{3,2,1,0:T(8,128)} %all-to-all-done.1.refs_2_.refs_1_, f32[8,2,64,384]{3,2,1,0:T(8,128)} %all-to-all-done.4.refs_2_, ...), custom_call_target="tpu_custom_call" | custom-call | flops 10000000000 | tf_op jit(solution)/shard_map/pallas_call | solution.py:194
  121.4 0.0 all-to-all-done.3.tiles
  121.4 7.3 %all-to-all-start.2 = ((f32[8,1,64,384]{3,2,1,0:T(8,128)}), f32[8,1,64,384]{3,2,1,0:T(8,128)}, u32[]{:S(2)}, u32[]{:S(2)}) async-start(f32[8,1,64,384]{3,2,1,0:T(8,128)} %shard_map.127), calls=%async_computation.2 | async-start | bytes 1572864 | tf_op jit(solution)/shard_map/all_to_all | solution.py:298
  128.7 4.9 %shard_map.134.total = f32[512,384]{1,0:T(8,128)} custom-call(f32[8,2,64,384]{3,2,1,0:T(8,128)} %all-to-all-done.3.tiles, bf16[512,4096]{1,0:T(8,128)(2,1)} %get-tuple-element.11.refs_3_.refs_5_.refs_7_.left_hi, bf16[512,4096]{1,0:T(8,128)(2,1)} %get-tuple-element.12.refs_4_.refs_6_.refs_8_.left_lo, f32[512,384]{1,0:T(8,128)} %shard_map.133.total), custom_call_target="tpu_custom_call" | custom-call | flops 60000002048 | tf_op jit(solution)/shard_map/pallas_call | solution.py:242
  133.6 10.1 %all-to-all-done.2.tiles = f32[8,1,64,384]{3,2,1,0:T(8,128)} async-done(((f32[8,1,64,384]{3,2,1,0:T(8,128)}), f32[8,1,64,384]{3,2,1,0:T(8,128)}, u32[]{:S(2)}, u32[]{:S(2)}) %all-to-all-start.2) | async-done | bytes 786464 | tf_op jit(solution)/shard_map/all_to_all | solution.py:298
  143.8 0.0 collective-permute-done.10.other
  143.8 4.6 %shard_map.136 = (f32[384,512]{1,0:T(8,128)}, f32[384,512]{1,0:T(8,128)}) custom-call(f32[8,1,64,384]{3,2,1,0:T(8,128)} %all-to-all-done.2.tiles, bf16[512,4096]{1,0:T(8,128)(2,1)} %get-tuple-element.11.refs_3_.refs_5_.refs_7_.left_hi, bf16[512,4096]{1,0:T(8,128)(2,1)} %get-tuple-element.12.refs_4_.refs_6_.refs_8_.left_lo, f32[512,384]{1,0:T(8,128)} %shard_map.134.total, ...), custom_call_target="tpu_custom_call" | custom-call | tf_op jit(solution)/shard_map/pallas_call | solution.py:224
  (6 shorter events, 0.0 us)
Async XLA Ops:
  2.9 27.4 %collective-permute-start = (f32[520,384]{1,0:T(8,128)}, f32[520,384]{1,0:T(8,128)}, u32[]{:S(2)}, u32[]{:S(2)}) collective-permute-start(f32[520,384]{1,0:T(8,128)} %shard_map.122.refs_0_), channel_id=1, source_target_pairs={{0,32},{1,225},{32,64},{33,1},{64,96},{65,33},{96,128},{97,65},{12... | collective-permute-start | bytes 2396168 | tf_op jit(solution)/shard_map/ppermute | solution.py:293
  4.9 25.5 %collective-permute-start.2 = (f32[520,384]{1,0:T(8,128)}, f32[520,384]{1,0:T(8,128)}, u32[]{:S(2)}, u32[]{:S(2)}) collective-permute-start(f32[520,384]{1,0:T(8,128)} %shard_map.122.refs_0_), channel_id=1, source_target_pairs={{0,224},{1,33},{32,0},{33,65},{64,32},{65,97},{96,64},{97,129},{12... | collective-permute-start | bytes 2396168 | tf_op jit(solution)/shard_map/ppermute | solution.py:293
  11.9 25.2 %all-to-all-start = ((f32[8,1,64,384]{3,2,1,0:T(8,128)}), f32[8,1,64,384]{3,2,1,0:T(8,128)}, u32[]{:S(2)}, u32[]{:S(2)}) async-start(f32[8,1,64,384]{3,2,1,0:T(8,128)} %shard_map.123.after), calls=%async_computation | async-start | bytes 1572864 | tf_op jit(solution)/shard_map/all_to_all | solution.py:300
  25.5 47.3 %collective-permute-start.8 = (f32[128,32,128]{2,1,0:T(8,128)}, f32[128,32,128]{2,1,0:T(8,128)}, u32[]{:S(2)}, u32[]{:S(2)}) collective-permute-start(f32[128,32,128]{2,1,0:T(8,128)} %shard_map.128.i0), channel_id=1, source_target_pairs={{0,2},{2,0},{1,3},{3,1},{4,6},{6,4},{5,7},{7,5},{8,10},{10,8},{9,1... | collective-permute-start | bytes 6291464 | tf_op jit(solution)/shard_map/ppermute | solution.py:288
  25.8 71.8 %collective-permute-start.7 = (f32[128,32,128]{2,1,0:T(8,128)}, f32[128,32,128]{2,1,0:T(8,128)}, u32[]{:S(2)}, u32[]{:S(2)}) collective-permute-start(f32[128,32,128]{2,1,0:T(8,128)} %shard_map.128.i0), channel_id=1, source_target_pairs={{0,1},{1,0},{2,3},{3,2},{4,5},{5,4},{6,7},{7,6},{8,9},{9,8},{10,11... | collective-permute-start | bytes 6291464 | tf_op jit(solution)/shard_map/ppermute | solution.py:288
  30.4 21.0 %collective-permute-start.1 = (f32[520,384]{1,0:T(8,128)}, f32[520,384]{1,0:T(8,128)}, u32[]{:S(2)}, u32[]{:S(2)}) collective-permute-start(f32[520,384]{1,0:T(8,128)} %collective-permute-done.refs_0_), channel_id=1, source_target_pairs={{0,32},{1,225},{32,64},{33,1},{64,96},{65,33},{96,128},{97,65},{12... | collective-permute-start | bytes 2396168 | tf_op jit(solution)/shard_map/ppermute | solution.py:293
  30.4 21.0 %collective-permute-start.3 = (f32[520,384]{1,0:T(8,128)}, f32[520,384]{1,0:T(8,128)}, u32[]{:S(2)}, u32[]{:S(2)}) collective-permute-start(f32[520,384]{1,0:T(8,128)} %collective-permute-done.2.refs_1_), channel_id=1, source_target_pairs={{0,224},{1,33},{32,0},{33,65},{64,32},{65,97},{96,64},{97,129},{12... | collective-permute-start | bytes 2396168 | tf_op jit(solution)/shard_map/ppermute | solution.py:293
  37.2 25.8 %all-to-all-start.1 = ((f32[8,2,64,384]{3,2,1,0:T(8,128)}), f32[8,2,64,384]{3,2,1,0:T(8,128)}, u32[]{:S(2)}, u32[]{:S(2)}) async-start(f32[8,2,64,384]{3,2,1,0:T(8,128)} %shard_map.125), calls=%async_computation.1 | async-start | bytes 3145728 | tf_op jit(solution)/shard_map/all_to_all | solution.py:300
  51.4 21.4 %collective-permute-start.4 = (f32[520,384]{1,0:T(8,128)}, f32[520,384]{1,0:T(8,128)}, u32[]{:S(2)}, u32[]{:S(2)}) collective-permute-start(f32[520,384]{1,0:T(8,128)} %get-tuple-element.8.refs_0_), channel_id=1, source_target_pairs={{0,32},{1,225},{32,64},{33,1},{64,96},{65,33},{96,128},{97,65},{12... | collective-permute-start | bytes 2396168 | tf_op jit(solution)/shard_map/ppermute | solution.py:293
  51.4 21.4 %collective-permute-start.5 = (f32[520,384]{1,0:T(8,128)}, f32[520,384]{1,0:T(8,128)}, u32[]{:S(2)}, u32[]{:S(2)}) collective-permute-start(f32[520,384]{1,0:T(8,128)} %get-tuple-element.9.refs_1_), channel_id=1, source_target_pairs={{0,224},{1,33},{32,0},{33,65},{64,32},{65,97},{96,64},{97,129},{12... | collective-permute-start | bytes 2396168 | tf_op jit(solution)/shard_map/ppermute | solution.py:293
  63.0 26.4 %all-to-all-start.4 = ((f32[8,2,64,384]{3,2,1,0:T(8,128)}), f32[8,2,64,384]{3,2,1,0:T(8,128)}, u32[]{:S(2)}, u32[]{:S(2)}) async-start(f32[8,2,64,384]{3,2,1,0:T(8,128)} %shard_map.132), calls=%async_computation.4 | async-start | bytes 3145728 | tf_op jit(solution)/shard_map/all_to_all | solution.py:300
  72.8 13.6 %collective-permute-start.6 = (f32[520,384]{1,0:T(8,128)}, f32[520,384]{1,0:T(8,128)}, u32[]{:S(2)}, u32[]{:S(2)}) collective-permute-start(f32[520,384]{1,0:T(8,128)} %get-tuple-element.10.refs_1_.refs_0_), channel_id=1, source_target_pairs={{0,32},{1,225},{32,64},{33,1},{64,96},{65,33},{96,128},{97,65},{12... | collective-permute-start | bytes 2396168 | tf_op jit(solution)/shard_map/ppermute | solution.py:293
  72.8 24.7 %collective-permute-start.9 = (f32[128,32,128]{2,1,0:T(8,128)}, f32[128,32,128]{2,1,0:T(8,128)}, u32[]{:S(2)}, u32[]{:S(2)}) collective-permute-start(f32[128,32,128]{2,1,0:T(8,128)} %shard_map.129.i2), channel_id=1, source_target_pairs={{0,1},{1,0},{2,3},{3,2},{4,5},{5,4},{6,7},{7,6},{8,9},{9,8},{10,11... | collective-permute-start | bytes 6291464 | tf_op jit(solution)/shard_map/ppermute | solution.py:288
  89.4 32.1 %all-to-all-start.3 = ((f32[8,2,64,384]{3,2,1,0:T(8,128)}), f32[8,2,64,384]{3,2,1,0:T(8,128)}, u32[]{:S(2)}, u32[]{:S(2)}) async-start(f32[8,2,64,384]{3,2,1,0:T(8,128)} %shard_map.131), calls=%async_computation.3 | async-start | bytes 3145728 | tf_op jit(solution)/shard_map/all_to_all | solution.py:298
  116.1 27.7 %collective-permute-start.10 = (f32[512,384]{1,0:T(8,128)}, f32[512,384]{1,0:T(8,128)}, u32[]{:S(2)}, u32[]{:S(2)}) collective-permute-start(f32[512,384]{1,0:T(8,128)} %shard_map.135), channel_id=1, source_target_pairs={{0,2},{2,0},{1,3},{3,1},{4,6},{6,4},{5,7},{7,5},{8,10},{10,8},{9,1... | collective-permute-start | bytes 2359304 | tf_op jit(solution)/shard_map/ppermute | solution.py:288
  121.4 22.3 %all-to-all-start.2 = ((f32[8,1,64,384]{3,2,1,0:T(8,128)}), f32[8,1,64,384]{3,2,1,0:T(8,128)}, u32[]{:S(2)}, u32[]{:S(2)}) async-start(f32[8,1,64,384]{3,2,1,0:T(8,128)} %shard_map.127), calls=%async_computation.2 | async-start | bytes 1572864 | tf_op jit(solution)/shard_map/all_to_all | solution.py:298

commit v7 on v6

v7 whole, which is shorter than its diff:
```python
import functools

import jax
import jax.numpy as jnp
from jax import lax
from jax.experimental import pallas as pl
from jax.experimental.pallas import tpu as pltpu
from jax.sharding import Mesh, PartitionSpec as P

Z, XH, Y, XL, CO = 8, 2, 4, 2, 2
PLANE = XH * Y
OWNERS = Z * PLANE
TILE = 64
ROW_TILES = 8
TERM_SHARE = 16
GROUP = 4
NOTE = 8
SELECT_COST = (3, 40, 40, 15)
PREPARE_COSTS = (10, 10)
MORE_COST = 60
PACK_COST = 40
PREPARE_COST = 10
OTHER_COST = 3
OWN_COST = 60
STEPS = ((0,), (1, -1), (2, -2), (3, -3, 4))
MIRRORED = (True, True, True, False)
ANYWHERE = pl.BlockSpec(memory_space=pl.ANY)
IN_HBM = pl.BlockSpec(memory_space=pltpu.HBM)
INSIDE = pl.BlockSpec(memory_space=pltpu.VMEM)
SCALARS = pl.BlockSpec(memory_space=pltpu.SMEM)
PARAMS = pltpu.CompilerParams(vmem_limit_bytes=65500 * 1024)


def cost(micros):
    return pl.CostEstimate(flops=int(micros * 1e9), bytes_accessed=0, transcendentals=0)


def in_hbm(*xs):
    return [pltpu.with_memory_space_constraint(x, pltpu.HBM) for x in xs]


def split(x):
    hi = x.astype(jnp.bfloat16)
    lo = (x - hi.astype(jnp.float32)).astype(jnp.bfloat16)
    return hi, lo


def first_kernel(amp, send, out, held, sem):
    rows = amp.shape[1]
    held[pl.ds(0, rows)] = amp[...].T
    wide = jnp.pad(send[...].astype(jnp.float32), ((0, 0), (0, amp.shape[0] - OWNERS)))
    held[pl.ds(rows, NOTE)] = jnp.broadcast_to(wide, (NOTE, amp.shape[0]))
    copy = pltpu.make_async_copy(held, out, sem)
    copy.start()
    copy.wait()


def first(amp, send):
    cols, rows = amp.shape
    return pl.pallas_call(
        first_kernel,
        compiler_params=PARAMS,
        out_shape=jax.ShapeDtypeStruct((rows + NOTE, cols), jnp.float32),
        in_specs=[INSIDE, INSIDE],
        out_specs=IN_HBM,
        scratch_shapes=[pltpu.VMEM((rows + NOTE, cols), jnp.float32), pltpu.SemaphoreType.DMA],
    )(amp, send)


def select_kernel(owners, meta, *refs):
    sources, (out, notes, sems) = refs[:owners], refs[-3:]
    rows = ROW_TILES * TILE
    reads = [
        pltpu.make_async_copy(sources[n].at[pl.ds(rows, NOTE), pl.ds(0, 128)], notes.at[n], sems.at[PLANE * owners + n])
        for n in range(owners)
    ]
    for copy in reads:
        copy.start()
    copies = []
    for n in range(owners):
        reads[n].wait()
        for dest in range(PLANE):
            tile = jnp.clip(notes[n, 0, meta[0] * PLANE + dest].astype(jnp.int32), 0, ROW_TILES - 1)
            copy = pltpu.make_async_copy(
                sources[n].at[pl.ds(pl.multiple_of(tile * TILE, TILE), TILE)], out.at[dest, n], sems.at[n * PLANE + dest]
            )
            copy.start()
            copies.append(copy)
    for copy in copies:
        copy.wait()


def select(meta, sources, after, micros):
    owners, cols = len(sources), sources[0].shape[1]
    return pl.pallas_call(
        functools.partial(select_kernel, owners),
        compiler_params=PARAMS,
        out_shape=jax.ShapeDtypeStruct((PLANE, owners, TILE, cols), jnp.float32),
        in_specs=[SCALARS] + [IN_HBM] * owners + [ANYWHERE] * len(after),
        out_specs=INSIDE,
        scratch_shapes=[pltpu.SMEM((owners, NOTE, 128), jnp.float32), pltpu.SemaphoreType.DMA(((PLANE + 1) * owners,))],
        cost_estimate=cost(micros),
    )(meta, *in_hbm(*sources), *after)


def places(offsets, sources, flipped):
    return [(offset, source, flipped) for source in sources for offset in offsets]


OTHERS = places((1, -1), range(4, 8), True) + places((2, -2), range(4, 8), True) + places((0,), range(4, 8), True)
OWNS = (
    places((3, -3, 4), range(8), False)
    + places((1, -1), range(4), True)
    + places((2, -2), range(4), True)
    + places((0,), range(4), True)
)


def prepare_kernel(owners, meta, slots, i0, i1, i2, i3, out_hi, out_lo, held, inverse, order, sems):
    per = ROW_TILES * TERM_SHARE
    g = pl.program_id(0)

    @pl.when(g == 0)
    def _():
        copies = [
            pltpu.make_async_copy(piece, held.at[pl.ds(n * per, per)], sems.at[n])
            for n, piece in enumerate((i0, i1, i2, i3))
        ]
        for copy in copies:
            copy.start()
        z, half, core = meta[0], meta[1], meta[2]
        mine = meta[3] * CO + core
        sign = 1 - 2 * core
        for n, (offset, source, flipped) in enumerate(owners):
            peer = source ^ (half * Y) if flipped else source
            order[n] = ((z - sign * offset) & (Z - 1)) * PLANE + peer

        def fill(k, carry):
            place = ((k >> 4) ^ mine) * per + (k & (TERM_SHARE - 1))
            for x in range(ROW_TILES):
                inverse[x, slots[x, k]] = place + x * TERM_SHARE
            return carry

        lax.fori_loop(0, OWNERS, fill, 0)
        for copy in copies:
            copy.wait()

    low = lax.broadcasted_iota(jnp.int32, (TILE // 2, 2 * TILE), 1) < TILE
    for pair in range(GROUP // 2):
        left, right = order[g * GROUP + 2 * pair], order[g * GROUP + 2 * pair + 1]
        for x in range(ROW_TILES):
            first = held[inverse[x, left]]
            second = held[inverse[x, right]]
            top = jnp.where(low, first, pltpu.roll(second, TILE, 1))
            bottom = jnp.where(low, pltpu.roll(first, TILE, 1), second)
            for half, value in enumerate((top, bottom)):
                hi, lo = split(value)
                rows = pl.ds(x * TILE + half * (TILE // 2), TILE // 2)
                cols = pl.ds(pair * 2 * TILE, 2 * TILE)
                out_hi[rows, cols] = hi
                out_lo[rows, cols] = lo


def prepare(owners, meta, slots, pieces, micros):
    rows, width = ROW_TILES * TILE, GROUP * TILE
    shape = jax.ShapeDtypeStruct((rows, len(owners) * TILE), jnp.bfloat16)
    block = pl.BlockSpec((rows, width), lambda g: (0, g))
    return pl.pallas_call(
        functools.partial(prepare_kernel, owners),
        grid=(len(owners) // GROUP,),
        out_shape=(shape, shape),
        in_specs=[SCALARS, SCALARS] + [ANYWHERE] * 4,
        out_specs=(block, block),
        scratch_shapes=[
            pltpu.VMEM((4 * ROW_TILES * TERM_SHARE, TILE // 2, 2 * TILE), jnp.float32),
            pltpu.SMEM((ROW_TILES, OWNERS), jnp.int32),
            pltpu.SMEM((OWNERS,), jnp.int32),
            pltpu.SemaphoreType.DMA((4,)),
        ],
        compiler_params=PARAMS,
        cost_estimate=cost(micros),
    )(meta, slots, *in_hbm(*pieces))


def product(left_hi, left_lo, right):
    hi, lo = split(right)
    total = jnp.dot(left_hi, lo, preferred_element_type=jnp.float32)
    total += jnp.dot(left_lo, hi, preferred_element_type=jnp.float32)
    return total + jnp.dot(left_hi, hi, preferred_element_type=jnp.float32)


def steps_kernel(count, meta, *refs):
    del meta
    tiles, lefts, out = refs[:count], refs[count : 3 * count], refs[3 * count]
    total = None
    for n in range(count):
        value = tiles[n][...].reshape(-1, tiles[n].shape[-1])
        term = product(lefts[2 * n][...], lefts[2 * n + 1][...], value)
        total = term if total is None else total + term
    out[...] = total


def full(x):
    return pl.BlockSpec(x.shape, lambda g: (0,) * x.ndim)


def steps(meta, tiles, offsets, part, left, micros):
    rows, cols = left[0].shape[0], tiles[0].shape[-1]
    shape = jax.ShapeDtypeStruct((rows, cols), jnp.float32)
    tile_specs, left_specs = [], []
    for t, offset in zip(tiles, offsets):
        depth = Y * t.shape[1] * TILE
        tile_specs.append(pl.BlockSpec((Y,) + t.shape[1:], lambda g, meta: (meta[1] ^ part, 0, 0, 0)))
        left_specs += [pl.BlockSpec((rows, depth), functools.partial(lambda i, g, meta: (0, i), offset // depth))] * 2
    return pl.pallas_call(
        functools.partial(steps_kernel, len(tiles)),
        out_shape=shape,
        grid_spec=pltpu.PrefetchScalarGridSpec(
            num_scalar_prefetch=1,
            grid=(1,),
            in_specs=tile_specs + left_specs,
            out_specs=pl.BlockSpec((rows, cols), lambda g, meta: (0, 0)),
        ),
        compiler_params=PARAMS,
        cost_estimate=cost(micros),
    )(meta, *tiles, *(list(left) * len(tiles)))


def last_kernel(tiles, left_hi, left_lo, total, other, amp, row_gap, col_gap, res, new):
    values = tiles[...].reshape(left_hi.shape[1], tiles.shape[-1])
    cycle = (total[...] + other[...] + product(left_hi[...], left_lo[...], values)).T
    column = jnp.broadcast_to(col_gap[...], (8, col_gap.shape[1])).T[:, :1]
    gap = column + row_gap[...]
    amplitudes = amp[...]
    residual = cycle - gap * amplitudes
    res[...] = residual
    new[...] = amplitudes + residual / gap


def last(offset, tiles, left, total, other, amp, row_gap, col_gap):
    rows, cols = left[0].shape[0], tiles.shape[-1]
    depth = PLANE * tiles.shape[1] * TILE
    block = pl.BlockSpec((rows, depth), lambda g: (0, offset // depth))
    shape = jax.ShapeDtypeStruct((cols, rows), jnp.float32)
    return pl.pallas_call(
        last_kernel,
        grid=(1,),
        out_shape=(shape, shape),
        in_specs=[full(tiles), block, block, full(total), full(other), full(amp), full(row_gap), full(col_gap)],
        out_specs=(full(shape), full(shape)),
        compiler_params=PARAMS,
    )(tiles, *left, total, other, amp, row_gap, col_gap)


def tie_kernel(*refs):
    del refs


def tie(xs, after):
    return pl.pallas_call(
        tie_kernel,
        compiler_params=PARAMS,
        out_shape=[jax.ShapeDtypeStruct(x.shape, x.dtype) for x in xs],
        in_specs=[IN_HBM] * len(xs) + [ANYWHERE] * len(after),
        out_specs=[IN_HBM] * len(xs),
        input_output_aliases={n: n for n in range(len(xs))},
    )(*in_hbm(*xs), *after)


def pack_kernel(integrals, after, out):
    del after
    value = integrals[0]
    out[...] = jnp.concatenate([value[:, : TILE // 2], value[:, TILE // 2 :]], axis=2)


def pack(integrals, after):
    shape = (TERM_SHARE, TILE // 2, 2 * TILE)
    return pl.pallas_call(
        pack_kernel,
        grid=(ROW_TILES,),
        compiler_params=PARAMS,
        out_shape=jax.ShapeDtypeStruct((ROW_TILES * TERM_SHARE,) + shape[1:], jnp.float32),
        in_specs=[pl.BlockSpec((1,) + integrals.shape[1:], lambda x: (x, 0, 0, 0)), IN_HBM],
        out_specs=pl.BlockSpec(shape, lambda x: (x, 0, 0)),
        cost_estimate=cost(PACK_COST),
    )(integrals, *in_hbm(after))


def swap(x, axis):
    return lax.ppermute(x, axis, [(0, 1), (1, 0)])


def shift(x, by):
    turns = [((z * CO + c), ((z + (by if c == 0 else -by)) % Z) * CO + c) for z in range(Z) for c in range(CO)]
    return lax.ppermute(x, ("z", "co"), turns)


def exchange(x, mirrored):
    if not mirrored:
        return lax.all_to_all(x, ("xh", "y"), 0, 0, tiled=True)
    groups = [[(xh * Y + y) * XL + (xh ^ d) for xh in range(XH) for y in range(Y)] for d in range(XL)]
    return lax.all_to_all(x, ("xh", "y", "xl"), 0, 0, axis_index_groups=groups, tiled=True)


def body(amplitudes, integrals, send_tiles, task_slots, row_gap, column_gap):
    meta = jnp.stack([lax.axis_index(n) for n in ("z", "xh", "co", "xl")]).astype(jnp.int32)
    owned = first(amplitudes, send_tiles)
    packed = pack(integrals, owned)
    across, beside = swap(packed, "xl"), swap(packed, "co")
    ring = {0: owned}
    received, chosen = [], []
    for n, (offsets, mirrored) in enumerate(zip(STEPS, MIRRORED)):
        after = [packed] if n == 0 else []
        if n > 0:
            ring[n], ring[-n] = shift(ring[n - 1], 1), shift(ring[1 - n], -1)
        if n > 1:
            ring[n], ring[-n] = tie([ring[n], ring[-n]], [received[n - 2]])
        if n == 3:
            ring[4] = shift(ring[3], 1)
            pieces = (packed, beside, across, swap(across, "co"))
            left = in_hbm(*prepare(OTHERS, meta, task_slots, pieces, PREPARE_COSTS[0]))
            after = left[:1]
        outgoing = select(meta, [ring[o] for o in offsets], after, SELECT_COST[n])
        chosen.append(outgoing)
        received.append(exchange(outgoing, mirrored))

    mirrored = [received[n] for n in (1, 2, 0)]
    other = steps(meta, mirrored, (0, 512, 1024), 1, left, OTHER_COST)
    pieces = (*tie([pieces[0]], [other]), *pieces[1:])
    other = swap(other, "xl")
    left = in_hbm(*prepare(OWNS, meta, task_slots, pieces, PREPARE_COSTS[1]))
    total = steps(meta, mirrored, (1536, 2048, 2560), 0, left, OWN_COST)
    return last(0, received[3], left, total, other, amplitudes, row_gap[None, :], column_gap[None, :])


def solution(mesh):
    fine = Mesh(mesh.devices.reshape(Z, XH, Y, XL, CO), ("z", "xh", "y", "xl", "co"))
    wide, narrow = ("z", "xh", "y"), ("xl", "co")
    return jax.shard_map(
        body,
        mesh=fine,
        in_specs=(P(narrow, wide), P(wide, narrow, None, None), P(wide, None), P(wide, None), P(wide), P(narrow)),
        out_specs=(P(narrow, wide), P(narrow, wide)),
        check_vma=False,
    )
```

time: 151 us -> 157 us (1.040); the launches traced: 148 us -> 156 us
  waiting for transfers between devices: 36.4 us -> 51 us
  starting transfers between devices: 48 us -> 40.1 us
  Pallas kernels: 58.6 us -> 63.2 us
  other arithmetic: 3.02 us -> 0.55 us
    ppermute x7, waiting for transfers between devices: 21.4 us -> 4.23 us  [shift(): return lax.ppermute(x, ('z', 'co'), turns)]
    all_to_all x3, waiting for transfers between devices: 4.86 us -> 17.1 us  [exchange(): lax.all_to_all(x, ('xh', 'y', 'xl'), 0, 0, axis_index_groups=groups, tile...]
    ppermute x4, waiting for transfers between devices: 0.01 us -> 11.1 us  [swap(): return lax.ppermute(x, axis, [(0, 1), (1, 0)])]
    all_to_all x2 -> x1, starting transfers between devices: 15.4 us -> 6.74 us  [exchange(): return lax.all_to_all(x, ('xh', 'y'), 0, 0, tiled=True)]
    all_to_all x2 -> x1, waiting for transfers between devices: 10.1 us -> 18.6 us  [exchange(): return lax.all_to_all(x, ('xh', 'y'), 0, 0, tiled=True)]
    pallas_call x1, Pallas kernels: 4.6 us -> 7.29 us  [last(): pl.pallas_call(last_kernel, grid=(1,), out_shape=(shape, shape), in_specs...]
    pallas_call x9 -> x8, Pallas kernels: 45.2 us -> 47.1 us  [the longest x2 18.3 us: prepare(): pl.pallas_call(functools.partial(prepare_kernel, owners), grid=(len(owner...]
  transfers between devices with their start and end apart: 16 -> 15, of which waited for: 5 -> 5; matrix products, arithmetic and copies ran while one was open for 3% -> 1% of each run, Pallas kernels for 35% -> 34%
where the time goes in v7:
time: 157 us; the launch traced here: 156 us
  Pallas kernels  63.2 us (40%)
  waiting for transfers between devices  51 us (32%)
  starting transfers between devices  40.1 us (26%)
    all_to_all x3, starting transfers between devices, exchange(): lax.all_to_all(x, ('xh', 'y', 'xl'), 0, 0, axis_index_groups=groups, tile...  19.3 us
    all_to_all x1, waiting for transfers between devices, exchange(): return lax.all_to_all(x, ('xh', 'y'), 0, 0, tiled=True)  18.6 us
    pallas_call x2, Pallas kernels, prepare(): pl.pallas_call(functools.partial(prepare_kernel, owners), grid=(len(owner...  18.3 us
    all_to_all x3, waiting for transfers between devices, exchange(): lax.all_to_all(x, ('xh', 'y', 'xl'), 0, 0, axis_index_groups=groups, tile...  17.1 us
    pallas_call x4, Pallas kernels, select(): pl.pallas_call(functools.partial(select_kernel, owners), compiler_params=...  16.8 us
    ppermute x7, starting transfers between devices, shift(): return lax.ppermute(x, ('z', 'co'), turns)  12.5 us
    pallas_call x2, Pallas kernels, steps(): pl.pallas_call(functools.partial(steps_kernel, len(tiles)), out_shape=sha...  12 us
    ppermute x4, waiting for transfers between devices, swap(): return lax.ppermute(x, axis, [(0, 1), (1, 0)])  11.1 us
  transfers between devices with their start and end apart: 15, of which 5 were waited for; matrix products, arithmetic and copies ran while one was open for 1% of the time, Pallas kernels for 34%

profile of v7, /device:TPU:8, one launch (start us, length us, event | category | flops | bytes accessed | tf_op | source)
XLA Modules:
  0.0 156.1 jit_solution(2102259596802725172)
XLA Ops:
  0.6 2.3 %shard_map.77.after.refs_0_ = f32[520,384]{1,0:T(8,128)} custom-call(f32[384,512]{1,0:T(8,128)} %amp.3, s32[1,64]{1,0:T(1,128)} %send.1), custom_call_target="tpu_custom_call" | custom-call | tf_op jit(solution)/shard_map/pallas_call | solution.py:60
  3.0 2.0 %collective-permute-start = (f32[520,384]{1,0:T(8,128)}, f32[520,384]{1,0:T(8,128)}, u32[]{:S(2)}, u32[]{:S(2)}) collective-permute-start(f32[520,384]{1,0:T(8,128)} %shard_map.77.after.refs_0_), channel_id=1, source_target_pairs={{0,32},{1,225},{32,64},{33,1},{64,96},{65,33},{96,128},{97,65},{12... | collective-permute-start | bytes 2396168 | tf_op jit(solution)/shard_map/ppermute | solution.py:295
  5.0 4.0 %collective-permute-start.2 = (f32[520,384]{1,0:T(8,128)}, f32[520,384]{1,0:T(8,128)}, u32[]{:S(2)}, u32[]{:S(2)}) collective-permute-start(f32[520,384]{1,0:T(8,128)} %shard_map.77.after.refs_0_), channel_id=1, source_target_pairs={{0,224},{1,33},{32,0},{33,65},{64,32},{65,97},{96,64},{97,129},{12... | collective-permute-start | bytes 2396168 | tf_op jit(solution)/shard_map/ppermute | solution.py:295
  9.0 6.5 %shard_map.78.refs_1_.i0.refs_0_ = f32[128,32,128]{2,1,0:T(8,128)} custom-call(f32[8,16,64,64]{3,2,1,0:T(8,128)} %integrals.1, f32[520,384]{1,0:T(8,128)} %shard_map.77.after.refs_0_), custom_call_target="tpu_custom_call" | custom-call | flops 40000000000 | tf_op jit(solution)/shard_map/pallas_call | solution.py:278
  15.5 0.0 collective-permute-start.7
  15.5 1.5 collective-permute-start.8
  17.0 0.6 pad_add_fusion.meta
  17.5 3.6 %shard_map.79 = f32[8,1,64,384]{3,2,1,0:T(8,128)} custom-call(s32[4]{0:T(128)} %pad_add_fusion.meta, f32[520,384]{1,0:T(8,128)} %shard_map.77.after.refs_0_, f32[128,32,128]{2,1,0:T(8,128)} %shard_map.78.refs_1_.i0.refs_0_), custom_call_target="tpu_custom_call" | custom-call | flops 3000000000 | tf_op jit(solution)/shard_map/pallas_call | solution.py:95
  21.1 6.5 %all-to-all-start = ((f32[8,1,64,384]{3,2,1,0:T(8,128)}), f32[8,1,64,384]{3,2,1,0:T(8,128)}, u32[]{:S(2)}, u32[]{:S(2)}) async-start(f32[8,1,64,384]{3,2,1,0:T(8,128)} %shard_map.79), calls=%async_computation | async-start | bytes 1572864 | tf_op jit(solution)/shard_map/all_to_all | solution.py:302
  27.6 0.0 collective-permute-done.refs_0_
  27.6 0.0 collective-permute-start.1
  27.6 0.0 collective-permute-done.2.refs_1_
  27.6 3.2 %collective-permute-start.3 = (f32[520,384]{1,0:T(8,128)}, f32[520,384]{1,0:T(8,128)}, u32[]{:S(2)}, u32[]{:S(2)}) collective-permute-start(f32[520,384]{1,0:T(8,128)} %collective-permute-done.2.refs_1_), channel_id=1, source_target_pairs={{0,224},{1,33},{32,0},{33,65},{64,32},{65,97},{96,64},{97,129},{12... | collective-permute-start | bytes 2396168 | tf_op jit(solution)/shard_map/ppermute | solution.py:295
  30.8 4.2 %shard_map.81 = f32[8,2,64,384]{3,2,1,0:T(8,128)} custom-call(s32[4]{0:T(128)} %pad_add_fusion.meta, f32[520,384]{1,0:T(8,128)} %collective-permute-done.refs_0_, f32[520,384]{1,0:T(8,128)} %collective-permute-done.2.refs_1_), custom_call_target="tpu_custom_call" | custom-call | flops 40000000000 | tf_op jit(solution)/shard_map/pallas_call | solution.py:95
  35.1 4.5 %all-to-all-done.refs_2_ = f32[8,1,64,384]{3,2,1,0:T(8,128)} async-done(((f32[8,1,64,384]{3,2,1,0:T(8,128)}), f32[8,1,64,384]{3,2,1,0:T(8,128)}, u32[]{:S(2)}, u32[]{:S(2)}) %all-to-all-start) | async-done | bytes 786464 | tf_op jit(solution)/shard_map/all_to_all | solution.py:302
  39.5 5.8 %all-to-all-start.1 = ((f32[8,2,64,384]{3,2,1,0:T(8,128)}), f32[8,2,64,384]{3,2,1,0:T(8,128)}, u32[]{:S(2)}, u32[]{:S(2)}) async-start(f32[8,2,64,384]{3,2,1,0:T(8,128)} %shard_map.81), calls=%async_computation.1 | async-start | bytes 3145728 | tf_op jit(solution)/shard_map/all_to_all | solution.py:302
  45.3 4.2 %collective-permute-done.1.refs_0_ = f32[520,384]{1,0:T(8,128)} collective-permute-done((f32[520,384]{1,0:T(8,128)}, f32[520,384]{1,0:T(8,128)}, u32[]{:S(2)}, u32[]{:S(2)}) %collective-permute-start.1) | collective-permute-done | bytes 798752 | tf_op jit(solution)/shard_map/ppermute | solution.py:295
  49.5 0.0 collective-permute-done.3.refs_1_
  49.5 0.0 collective-permute-start.4
  49.5 3.2 %collective-permute-start.5 = (f32[520,384]{1,0:T(8,128)}, f32[520,384]{1,0:T(8,128)}, u32[]{:S(2)}, u32[]{:S(2)}) collective-permute-start(f32[520,384]{1,0:T(8,128)} %get-tuple-element.11.refs_1_), channel_id=1, source_target_pairs={{0,224},{1,33},{32,0},{33,65},{64,32},{65,97},{96,64},{97,129},{12... | collective-permute-start | bytes 2396168 | tf_op jit(solution)/shard_map/ppermute | solution.py:295
  52.8 11.1 %collective-permute-done.8.i2 = f32[128,32,128]{2,1,0:T(8,128)} collective-permute-done((f32[128,32,128]{2,1,0:T(8,128)}, f32[128,32,128]{2,1,0:T(8,128)}, u32[]{:S(2)}, u32[]{:S(2)}) %collective-permute-start.8) | collective-permute-done | bytes 2097184 | tf_op jit(solution)/shard_map/ppermute | solution.py:290
  63.8 0.0 collective-permute-start.9
  63.8 4.2 %shard_map.85 = f32[8,2,64,384]{3,2,1,0:T(8,128)} custom-call(s32[4]{0:T(128)} %pad_add_fusion.meta, f32[520,384]{1,0:T(8,128)} %get-tuple-element.10.refs_0_, f32[520,384]{1,0:T(8,128)} %get-tuple-element.11.refs_1_), custom_call_target="tpu_custom_call" | custom-call | flops 40000000000 | tf_op jit(solution)/shard_map/pallas_call | solution.py:95
  68.0 0.0 copy-start
  68.1 0.0 all-to-all-done.1.refs_2_.refs_0_
  68.1 7.1 %all-to-all-start.3 = ((f32[8,2,64,384]{3,2,1,0:T(8,128)}), f32[8,2,64,384]{3,2,1,0:T(8,128)}, u32[]{:S(2)}, u32[]{:S(2)}) async-start(f32[8,2,64,384]{3,2,1,0:T(8,128)} %shard_map.85), calls=%async_computation.3 | async-start | bytes 3145728 | tf_op jit(solution)/shard_map/all_to_all | solution.py:302
  75.2 0.0 copy-done
  75.2 0.6 broadcast_in_dim.7.col_gap
  75.8 0.0 collective-permute-done.4.refs_0_
  75.8 0.0 collective-permute-done.5.refs_1_
  75.8 0.0 collective-permute-start.6
  75.8 0.0 collective-permute-done.7.i1
  75.8 0.0 collective-permute-done.9.i3
  75.8 7.6 %shard_map.83 = (bf16[512,1280]{1,0:T(8,128)(2,1)}, bf16[512,1280]{1,0:T(8,128)(2,1)}) custom-call(s32[4]{0:T(128)} %pad_add_fusion.meta, s32[8,64]{1,0:T(8,128)} %slots.3, f32[128,32,128]{2,1,0:T(8,128)} %shard_map.78.refs_1_.i0.refs_0_, f32[128,32,128]{2,1,0:T(8,128)} %collective-permute-done.7.i1, f32[128,32,128]{2,1,0:T(8,128)} %collective-permute-done.8.i2, ...), custom_call_target="tpu_custom_call" | custom-call | flops 10000000000 | tf_op jit(solution)/shard_map/pallas_call | solution.py:168
  83.4 12.6 %all-to-all-done.3.refs_1_ = f32[8,2,64,384]{3,2,1,0:T(8,128)} async-done(((f32[8,2,64,384]{3,2,1,0:T(8,128)}), f32[8,2,64,384]{3,2,1,0:T(8,128)}, u32[]{:S(2)}, u32[]{:S(2)}) %all-to-all-start.3) | async-done | bytes 1572896 | tf_op jit(solution)/shard_map/all_to_all | solution.py:302
  96.0 6.0 %shard_map.86.refs_1_ = f32[512,384]{1,0:T(8,128)} custom-call(s32[4]{0:T(128)} %pad_add_fusion.meta, f32[8,2,64,384]{3,2,1,0:T(8,128)} %all-to-all-done.1.refs_2_.refs_0_, f32[8,2,64,384]{3,2,1,0:T(8,128)} %all-to-all-done.3.refs_1_, f32[8,1,64,384]{3,2,1,0:T(8,128)} %all-to-all-done.refs_2_, bf16[512,1280]{1,0:T(8,128)(2,1)} %get-tuple-element.14.refs_3_.refs_5_.refs_7_, ...), custom_call_target="tpu_custom_call" | custom-call | flops 3000000000 | tf_op jit(solution)/shard_map/pallas_call | solution.py:215
  102.0 0.0 collective-permute-start.10
  102.0 0.0 collective-permute-done.6.refs_2_
  102.0 4.8 %shard_map.84 = f32[8,3,64,384]{3,2,1,0:T(8,128)} custom-call(s32[4]{0:T(128)} %pad_add_fusion.meta, f32[520,384]{1,0:T(8,128)} %get-tuple-element.12.refs_0_, f32[520,384]{1,0:T(8,128)} %get-tuple-element.13.refs_1_, f32[520,384]{1,0:T(8,128)} %collective-permute-done.6.refs_2_, bf16[512,1280]{1,0:T(8,128)(2,1)} %get-tuple-element.14.refs_3_.refs_5_.refs_7_), custom_call_target="tpu_custom_call" | custom-call | flops 15000000512 | tf_op jit(solution)/shard_map/pallas_call | solution.py:95
  106.8 6.7 %all-to-all-start.2 = ((f32[8,3,64,384]{3,2,1,0:T(8,128)}), f32[8,3,64,384]{3,2,1,0:T(8,128)}, u32[]{:S(2)}, u32[]{:S(2)}) async-start(f32[8,3,64,384]{3,2,1,0:T(8,128)} %shard_map.84), calls=%async_computation.2 | async-start | bytes 4718592 | tf_op jit(solution)/shard_map/all_to_all | solution.py:300
  113.5 10.7 %shard_map.88 = (bf16[512,2816]{1,0:T(8,128)(2,1)}, bf16[512,2816]{1,0:T(8,128)(2,1)}) custom-call(s32[4]{0:T(128)} %pad_add_fusion.meta, s32[8,64]{1,0:T(8,128)} %slots.3, f32[128,32,128]{2,1,0:T(8,128)} %shard_map.87.i0, f32[128,32,128]{2,1,0:T(8,128)} %collective-permute-done.7.i1, f32[128,32,128]{2,1,0:T(8,128)} %collective-permute-done.8.i2, ...), custom_call_target="tpu_custom_call" | custom-call | flops 10000000000 | tf_op jit(solution)/shard_map/pallas_call | solution.py:168
  124.2 6.0 %shard_map.89.total = f32[512,384]{1,0:T(8,128)} custom-call(s32[4]{0:T(128)} %pad_add_fusion.meta, f32[8,2,64,384]{3,2,1,0:T(8,128)} %all-to-all-done.1.refs_2_.refs_0_, f32[8,2,64,384]{3,2,1,0:T(8,128)} %all-to-all-done.3.refs_1_, f32[8,1,64,384]{3,2,1,0:T(8,128)} %all-to-all-done.refs_2_, ...), custom_call_target="tpu_custom_call" | custom-call | flops 60000002048 | tf_op jit(solution)/shard_map/pallas_call | solution.py:215
  130.3 0.0 collective-permute-done.10.other
  130.3 18.6 %all-to-all-done.2.tiles = f32[8,3,64,384]{3,2,1,0:T(8,128)} async-done(((f32[8,3,64,384]{3,2,1,0:T(8,128)}), f32[8,3,64,384]{3,2,1,0:T(8,128)}, u32[]{:S(2)}, u32[]{:S(2)}) %all-to-all-start.2) | async-done | bytes 2359328 | tf_op jit(solution)/shard_map/all_to_all | solution.py:300
  148.9 7.3 %shard_map.90 = (f32[384,512]{1,0:T(8,128)}, f32[384,512]{1,0:T(8,128)}) custom-call(f32[8,3,64,384]{3,2,1,0:T(8,128)} %all-to-all-done.2.tiles, bf16[512,2816]{1,0:T(8,128)(2,1)} %get-tuple-element.16.refs_3_.refs_5_.refs_7_.left_hi, bf16[512,2816]{1,0:T(8,128)(2,1)} %get-tuple-element.17.refs_4_.refs_6_.refs_8_.left_lo, f32[512,384]{1,0:T(8,128)} %shard_map.89.total, ...), custom_call_target="tpu_custom_call" | custom-call | tf_op jit(solution)/shard_map/pallas_call | solution.py:245
  (3 shorter events, 0.0 us)
Async XLA Ops:
  3.0 24.6 %collective-permute-start = (f32[520,384]{1,0:T(8,128)}, f32[520,384]{1,0:T(8,128)}, u32[]{:S(2)}, u32[]{:S(2)}) collective-permute-start(f32[520,384]{1,0:T(8,128)} %shard_map.77.after.refs_0_), channel_id=1, source_target_pairs={{0,32},{1,225},{32,64},{33,1},{64,96},{65,33},{96,128},{97,65},{12... | collective-permute-start | bytes 2396168 | tf_op jit(solution)/shard_map/ppermute | solution.py:295
  5.0 22.6 %collective-permute-start.2 = (f32[520,384]{1,0:T(8,128)}, f32[520,384]{1,0:T(8,128)}, u32[]{:S(2)}, u32[]{:S(2)}) collective-permute-start(f32[520,384]{1,0:T(8,128)} %shard_map.77.after.refs_0_), channel_id=1, source_target_pairs={{0,224},{1,33},{32,0},{33,65},{64,32},{65,97},{96,64},{97,129},{12... | collective-permute-start | bytes 2396168 | tf_op jit(solution)/shard_map/ppermute | solution.py:295
  15.5 60.3 %collective-permute-start.7 = (f32[128,32,128]{2,1,0:T(8,128)}, f32[128,32,128]{2,1,0:T(8,128)}, u32[]{:S(2)}, u32[]{:S(2)}) collective-permute-start(f32[128,32,128]{2,1,0:T(8,128)} %shard_map.78.refs_1_.i0.refs_0_), channel_id=1, source_target_pairs={{0,1},{1,0},{2,3},{3,2},{4,5},{5,4},{6,7},{7,6},{8,9},{9,8},{10,11... | collective-permute-start | bytes 6291464 | tf_op jit(solution)/shard_map/ppermute | solution.py:290
  15.5 48.4 %collective-permute-start.8 = (f32[128,32,128]{2,1,0:T(8,128)}, f32[128,32,128]{2,1,0:T(8,128)}, u32[]{:S(2)}, u32[]{:S(2)}) collective-permute-start(f32[128,32,128]{2,1,0:T(8,128)} %shard_map.78.refs_1_.i0.refs_0_), channel_id=1, source_target_pairs={{0,2},{2,0},{1,3},{3,1},{4,6},{6,4},{5,7},{7,5},{8,10},{10,8},{9,1... | collective-permute-start | bytes 6291464 | tf_op jit(solution)/shard_map/ppermute | solution.py:290
  21.1 18.4 %all-to-all-start = ((f32[8,1,64,384]{3,2,1,0:T(8,128)}), f32[8,1,64,384]{3,2,1,0:T(8,128)}, u32[]{:S(2)}, u32[]{:S(2)}) async-start(f32[8,1,64,384]{3,2,1,0:T(8,128)} %shard_map.79), calls=%async_computation | async-start | bytes 1572864 | tf_op jit(solution)/shard_map/all_to_all | solution.py:302
  27.6 21.9 %collective-permute-start.1 = (f32[520,384]{1,0:T(8,128)}, f32[520,384]{1,0:T(8,128)}, u32[]{:S(2)}, u32[]{:S(2)}) collective-permute-start(f32[520,384]{1,0:T(8,128)} %collective-permute-done.refs_0_), channel_id=1, source_target_pairs={{0,32},{1,225},{32,64},{33,1},{64,96},{65,33},{96,128},{97,65},{12... | collective-permute-start | bytes 2396168 | tf_op jit(solution)/shard_map/ppermute | solution.py:295
  27.6 21.9 %collective-permute-start.3 = (f32[520,384]{1,0:T(8,128)}, f32[520,384]{1,0:T(8,128)}, u32[]{:S(2)}, u32[]{:S(2)}) collective-permute-start(f32[520,384]{1,0:T(8,128)} %collective-permute-done.2.refs_1_), channel_id=1, source_target_pairs={{0,224},{1,33},{32,0},{33,65},{64,32},{65,97},{96,64},{97,129},{12... | collective-permute-start | bytes 2396168 | tf_op jit(solution)/shard_map/ppermute | solution.py:295
  39.5 28.5 %all-to-all-start.1 = ((f32[8,2,64,384]{3,2,1,0:T(8,128)}), f32[8,2,64,384]{3,2,1,0:T(8,128)}, u32[]{:S(2)}, u32[]{:S(2)}) async-start(f32[8,2,64,384]{3,2,1,0:T(8,128)} %shard_map.81), calls=%async_computation.1 | async-start | bytes 3145728 | tf_op jit(solution)/shard_map/all_to_all | solution.py:302
  49.5 26.3 %collective-permute-start.4 = (f32[520,384]{1,0:T(8,128)}, f32[520,384]{1,0:T(8,128)}, u32[]{:S(2)}, u32[]{:S(2)}) collective-permute-start(f32[520,384]{1,0:T(8,128)} %get-tuple-element.10.refs_0_), channel_id=1, source_target_pairs={{0,32},{1,225},{32,64},{33,1},{64,96},{65,33},{96,128},{97,65},{12... | collective-permute-start | bytes 2396168 | tf_op jit(solution)/shard_map/ppermute | solution.py:295
  49.5 26.3 %collective-permute-start.5 = (f32[520,384]{1,0:T(8,128)}, f32[520,384]{1,0:T(8,128)}, u32[]{:S(2)}, u32[]{:S(2)}) collective-permute-start(f32[520,384]{1,0:T(8,128)} %get-tuple-element.11.refs_1_), channel_id=1, source_target_pairs={{0,224},{1,33},{32,0},{33,65},{64,32},{65,97},{96,64},{97,129},{12... | collective-permute-start | bytes 2396168 | tf_op jit(solution)/shard_map/ppermute | solution.py:295
  63.8 12.0 %collective-permute-start.9 = (f32[128,32,128]{2,1,0:T(8,128)}, f32[128,32,128]{2,1,0:T(8,128)}, u32[]{:S(2)}, u32[]{:S(2)}) collective-permute-start(f32[128,32,128]{2,1,0:T(8,128)} %collective-permute-done.8.i2), channel_id=1, source_target_pairs={{0,1},{1,0},{2,3},{3,2},{4,5},{5,4},{6,7},{7,6},{8,9},{9,8},{10,11... | collective-permute-start | bytes 6291464 | tf_op jit(solution)/shard_map/ppermute | solution.py:290
  68.0 7.1 %copy-start = (f32[384]{0:T(512)S(1)}, f32[384]{0:T(512)}, u32[]{:S(2)}) copy-start(f32[384]{0:T(512)} %param.11) | copy-start | bytes 4612
  68.1 27.9 %all-to-all-start.3 = ((f32[8,2,64,384]{3,2,1,0:T(8,128)}), f32[8,2,64,384]{3,2,1,0:T(8,128)}, u32[]{:S(2)}, u32[]{:S(2)}) async-start(f32[8,2,64,384]{3,2,1,0:T(8,128)} %shard_map.85), calls=%async_computation.3 | async-start | bytes 3145728 | tf_op jit(solution)/shard_map/all_to_all | solution.py:302
  75.8 26.2 %collective-permute-start.6 = (f32[520,384]{1,0:T(8,128)}, f32[520,384]{1,0:T(8,128)}, u32[]{:S(2)}, u32[]{:S(2)}) collective-permute-start(f32[520,384]{1,0:T(8,128)} %get-tuple-element.12.refs_0_), channel_id=1, source_target_pairs={{0,32},{1,225},{32,64},{33,1},{64,96},{65,33},{96,128},{97,65},{12... | collective-permute-start | bytes 2396168 | tf_op jit(solution)/shard_map/ppermute | solution.py:295
  102.0 28.3 %collective-permute-start.10 = (f32[512,384]{1,0:T(8,128)}, f32[512,384]{1,0:T(8,128)}, u32[]{:S(2)}, u32[]{:S(2)}) collective-permute-start(f32[512,384]{1,0:T(8,128)} %shard_map.86.refs_1_), channel_id=1, source_target_pairs={{0,2},{2,0},{1,3},{3,1},{4,6},{6,4},{5,7},{7,5},{8,10},{10,8},{9,1... | collective-permute-start | bytes 2359304 | tf_op jit(solution)/shard_map/ppermute | solution.py:290
  106.8 42.1 %all-to-all-start.2 = ((f32[8,3,64,384]{3,2,1,0:T(8,128)}), f32[8,3,64,384]{3,2,1,0:T(8,128)}, u32[]{:S(2)}, u32[]{:S(2)}) async-start(f32[8,3,64,384]{3,2,1,0:T(8,128)} %shard_map.84), calls=%async_computation.2 | async-start | bytes 4718592 | tf_op jit(solution)/shard_map/all_to_all | solution.py:300

commit v8 on v7

--- a/solution.py
+++ b/solution.py
@@ -15,15 +15,15 @@
 TERM_SHARE = 16
 GROUP = 4
 NOTE = 8
-SELECT_COST = (3, 40, 40, 15)
+SELECT_COST = (40, 40, 40, 15, 30)
 PREPARE_COSTS = (10, 10)
 MORE_COST = 60
 PACK_COST = 40
 PREPARE_COST = 10
 OTHER_COST = 3
 OWN_COST = 60
-STEPS = ((0,), (1, -1), (2, -2), (3, -3, 4))
-MIRRORED = (True, True, True, False)
+STEPS = ((0,), (1, -1), (2, -2), (3, -3), (4,))
+MIRRORED = (True, True, True, False, False)
 ANYWHERE = pl.BlockSpec(memory_space=pl.ANY)
 IN_HBM = pl.BlockSpec(memory_space=pltpu.HBM)
 INSIDE = pl.BlockSpec(memory_space=pltpu.VMEM)
@@ -109,9 +109,10 @@
 
 OTHERS = places((1, -1), range(4, 8), True) + places((2, -2), range(4, 8), True) + places((0,), range(4, 8), True)
 OWNS = (
-    places((3, -3, 4), range(8), False)
+    places((3, -3), range(8), False)
     + places((1, -1), range(4), True)
     + places((2, -2), range(4), True)
+    + places((4,), range(8), False)
     + places((0,), range(4), True)
 )
 
@@ -252,6 +253,25 @@
     )(tiles, *left, total, other, amp, row_gap, col_gap)
 
 
+def more_kernel(tiles, left_hi, left_lo, total, out):
+    values = tiles[...].reshape(left_hi.shape[1], tiles.shape[-1])
+    out[...] = total[...] + product(left_hi[...], left_lo[...], values)
+
+
+def more(index, tiles, left, total, micros):
+    rows = left[0].shape[0]
+    block = pl.BlockSpec((rows, PLANE * tiles.shape[1] * TILE), lambda g: (0, index))
+    return pl.pallas_call(
+        more_kernel,
+        grid=(1,),
+        out_shape=jax.ShapeDtypeStruct(total.shape, jnp.float32),
+        in_specs=[full(tiles), block, block, full(total)],
+        out_specs=full(total),
+        compiler_params=PARAMS,
+        cost_estimate=cost(micros),
+    )(tiles, *left, total)
+
+
 def tie_kernel(*refs):
     del refs
 
@@ -264,6 +284,7 @@
         in_specs=[IN_HBM] * len(xs) + [ANYWHERE] * len(after),
         out_specs=[IN_HBM] * len(xs),
         input_output_aliases={n: n for n in range(len(xs))},
+        cost_estimate=cost(20),
     )(*in_hbm(*xs), *after)
 
 
@@ -305,22 +326,27 @@
 def body(amplitudes, integrals, send_tiles, task_slots, row_gap, column_gap):
     meta = jnp.stack([lax.axis_index(n) for n in ("z", "xh", "co", "xl")]).astype(jnp.int32)
     owned = first(amplitudes, send_tiles)
-    packed = pack(integrals, owned)
-    across, beside = swap(packed, "xl"), swap(packed, "co")
     ring = {0: owned}
     received, chosen = [], []
     for n, (offsets, mirrored) in enumerate(zip(STEPS, MIRRORED)):
-        after = [packed] if n == 0 else []
-        if n > 0:
+        after = []
+        if n == Z // 2:
+            ring[n] = shift(ring[n - 1], 1)
+        elif n > 0:
             ring[n], ring[-n] = shift(ring[n - 1], 1), shift(ring[1 - n], -1)
-        if n > 1:
+        if n == 3:
+            (across,) = tie([across], [received[1]])
+        if 1 < n < Z // 2:
             ring[n], ring[-n] = tie([ring[n], ring[-n]], [received[n - 2]])
         if n == 3:
-            ring[4] = shift(ring[3], 1)
             pieces = (packed, beside, across, swap(across, "co"))
             left = in_hbm(*prepare(OTHERS, meta, task_slots, pieces, PREPARE_COSTS[0]))
+        if n == Z // 2:
             after = left[:1]
         outgoing = select(meta, [ring[o] for o in offsets], after, SELECT_COST[n])
+        if n == 0:
+            packed = pack(integrals, outgoing)
+            across, beside = swap(packed, "xl"), swap(packed, "co")
         chosen.append(outgoing)
         received.append(exchange(outgoing, mirrored))
 
@@ -329,8 +355,9 @@
     pieces = (*tie([pieces[0]], [other]), *pieces[1:])
     other = swap(other, "xl")
     left = in_hbm(*prepare(OWNS, meta, task_slots, pieces, PREPARE_COSTS[1]))
-    total = steps(meta, mirrored, (1536, 2048, 2560), 0, left, OWN_COST)
-    return last(0, received[3], left, total, other, amplitudes, row_gap[None, :], column_gap[None, :])
+    total = steps(meta, mirrored, (1024, 1536, 2560), 0, left, OWN_COST)
+    total = more(0, received[3], left, total, MORE_COST)
+    return last(2048, received[4], left, total, other, amplitudes, row_gap[None, :], column_gap[None, :])
 
 
 def solution(mesh):

time: 157 us -> 146 us (0.930)
  waiting for transfers between devices: 51 us -> 28.3 us
  starting transfers between devices: 40.1 us -> 45.9 us
  Pallas kernels: 63.2 us -> 68.3 us
    all_to_all x1 -> x2, waiting for transfers between devices: 18.6 us -> 6.69 us  [exchange(): return lax.all_to_all(x, ('xh', 'y'), 0, 0, tiled=True)]
    all_to_all x3, waiting for transfers between devices: 17.1 us -> 8.06 us  [exchange(): lax.all_to_all(x, ('xh', 'y', 'xl'), 0, 0, axis_index_groups=groups, tile...]
    all_to_all x1 -> x2, starting transfers between devices: 6.74 us -> 12.8 us  [exchange(): return lax.all_to_all(x, ('xh', 'y'), 0, 0, tiled=True)]
    ppermute x4, waiting for transfers between devices: 11.1 us -> 5.62 us  [swap(): return lax.ppermute(x, axis, [(0, 1), (1, 0)])]
    pallas_call x0 -> x1, Pallas kernels: none -> 4.99 us  [more(): pl.pallas_call(more_kernel, grid=(1,), out_shape=jax.ShapeDtypeStruct(tot...]
    ppermute x7, waiting for transfers between devices: 4.23 us -> 7.9 us  [shift(): return lax.ppermute(x, ('z', 'co'), turns)]
    pallas_call x4 -> x5, Pallas kernels: 16.8 us -> 19.7 us  [select(): pl.pallas_call(functools.partial(select_kernel, owners), compiler_params=...]
    pallas_call x1, Pallas kernels: 7.29 us -> 4.6 us  [last(): pl.pallas_call(last_kernel, grid=(1,), out_shape=(shape, shape), in_specs...]
  transfers between devices with their start and end apart: 15 -> 16, of which waited for: 5 -> 7; matrix products, arithmetic and copies ran while one was open for 1% -> 1% of each run, Pallas kernels for 34% -> 42%
where the time goes in v8:
time: 146 us; the launch traced here: 145 us
  Pallas kernels  68.3 us (47%)
  starting transfers between devices  45.9 us (31%)
  waiting for transfers between devices  28.3 us (19%)
    pallas_call x5, Pallas kernels, select(): pl.pallas_call(functools.partial(select_kernel, owners), compiler_params=...  19.7 us
    all_to_all x3, starting transfers between devices, exchange(): lax.all_to_all(x, ('xh', 'y', 'xl'), 0, 0, axis_index_groups=groups, tile...  19.1 us
    pallas_call x2, Pallas kernels, prepare(): pl.pallas_call(functools.partial(prepare_kernel, owners), grid=(len(owner...  18.2 us
    all_to_all x2, starting transfers between devices, exchange(): return lax.all_to_all(x, ('xh', 'y'), 0, 0, tiled=True)  12.8 us
    ppermute x7, starting transfers between devices, shift(): return lax.ppermute(x, ('z', 'co'), turns)  12.5 us
    pallas_call x2, Pallas kernels, steps(): pl.pallas_call(functools.partial(steps_kernel, len(tiles)), out_shape=sha...  12 us
    all_to_all x3, waiting for transfers between devices, exchange(): lax.all_to_all(x, ('xh', 'y', 'xl'), 0, 0, axis_index_groups=groups, tile...  8.06 us
    ppermute x7, waiting for transfers between devices, shift(): return lax.ppermute(x, ('z', 'co'), turns)  7.9 us
  transfers between devices with their start and end apart: 16, of which 7 were waited for; matrix products, arithmetic and copies ran while one was open for 1% of the time, Pallas kernels for 42%

profile of v8, /device:TPU:8, one launch (start us, length us, event | category | flops | bytes accessed | tf_op | source)
XLA Modules:
  0.0 145.1 jit_solution(14577097297960961640)
XLA Ops:
  0.6 2.3 %shard_map.77.refs_0_ = f32[520,384]{1,0:T(8,128)} custom-call(f32[384,512]{1,0:T(8,128)} %amp.3, s32[1,64]{1,0:T(1,128)} %send.1), custom_call_target="tpu_custom_call" | custom-call | tf_op jit(solution)/shard_map/pallas_call | solution.py:60
  3.0 5.9 %collective-permute-start.2 = (f32[520,384]{1,0:T(8,128)}, f32[520,384]{1,0:T(8,128)}, u32[]{:S(2)}, u32[]{:S(2)}) collective-permute-start(f32[520,384]{1,0:T(8,128)} %shard_map.77.refs_0_), channel_id=1, source_target_pairs={{0,224},{1,33},{32,0},{33,65},{64,32},{65,97},{96,64},{97,129},{12... | collective-permute-start | bytes 2396168 | tf_op jit(solution)/shard_map/ppermute | solution.py:316
  8.9 0.0 collective-permute-start
  8.9 0.7 pad_add_fusion.meta
  9.6 3.6 %shard_map.78.after = f32[8,1,64,384]{3,2,1,0:T(8,128)} custom-call(s32[4]{0:T(128)} %pad_add_fusion.meta, f32[520,384]{1,0:T(8,128)} %shard_map.77.refs_0_), custom_call_target="tpu_custom_call" | custom-call | flops 40000000000 | tf_op jit(solution)/shard_map/pallas_call | solution.py:95
  13.1 7.1 %all-to-all-start = ((f32[8,1,64,384]{3,2,1,0:T(8,128)}), f32[8,1,64,384]{3,2,1,0:T(8,128)}, u32[]{:S(2)}, u32[]{:S(2)}) async-start(f32[8,1,64,384]{3,2,1,0:T(8,128)} %shard_map.78.after), calls=%async_computation | async-start | bytes 1572864 | tf_op jit(solution)/shard_map/all_to_all | solution.py:323
  20.3 6.5 %shard_map.82.i0.refs_0_ = f32[128,32,128]{2,1,0:T(8,128)} custom-call(f32[8,16,64,64]{3,2,1,0:T(8,128)} %integrals.1, f32[8,1,64,384]{3,2,1,0:T(8,128)} %shard_map.78.after), custom_call_target="tpu_custom_call" | custom-call | flops 40000000000 | tf_op jit(solution)/shard_map/pallas_call | solution.py:299
  26.8 0.2 collective-permute-start.8
  27.0 0.0 collective-permute-start.7
  27.0 1.3 broadcast_in_dim.7.col_gap
  28.3 0.0 collective-permute-done.2.refs_1_
  28.3 3.2 %collective-permute-start.3 = (f32[520,384]{1,0:T(8,128)}, f32[520,384]{1,0:T(8,128)}, u32[]{:S(2)}, u32[]{:S(2)}) collective-permute-start(f32[520,384]{1,0:T(8,128)} %collective-permute-done.2.refs_1_), channel_id=1, source_target_pairs={{0,224},{1,33},{32,0},{33,65},{64,32},{65,97},{96,64},{97,129},{12... | collective-permute-start | bytes 2396168 | tf_op jit(solution)/shard_map/ppermute | solution.py:316
  31.5 0.0 collective-permute-done.refs_0_
  31.5 0.0 collective-permute-start.1
  31.5 4.2 %shard_map.80 = f32[8,2,64,384]{3,2,1,0:T(8,128)} custom-call(s32[4]{0:T(128)} %pad_add_fusion.meta, f32[520,384]{1,0:T(8,128)} %collective-permute-done.refs_0_, f32[520,384]{1,0:T(8,128)} %collective-permute-done.2.refs_1_), custom_call_target="tpu_custom_call" | custom-call | flops 40000000000 | tf_op jit(solution)/shard_map/pallas_call | solution.py:95
  35.7 0.0 all-to-all-done.refs_2_
  35.7 6.7 %all-to-all-start.1 = ((f32[8,2,64,384]{3,2,1,0:T(8,128)}), f32[8,2,64,384]{3,2,1,0:T(8,128)}, u32[]{:S(2)}, u32[]{:S(2)}) async-start(f32[8,2,64,384]{3,2,1,0:T(8,128)} %shard_map.80), calls=%async_computation.1 | async-start | bytes 3145728 | tf_op jit(solution)/shard_map/all_to_all | solution.py:323
  42.4 7.2 %collective-permute-done.3.refs_1_ = f32[520,384]{1,0:T(8,128)} collective-permute-done((f32[520,384]{1,0:T(8,128)}, f32[520,384]{1,0:T(8,128)}, u32[]{:S(2)}, u32[]{:S(2)}) %collective-permute-start.3) | collective-permute-done | bytes 798752 | tf_op jit(solution)/shard_map/ppermute | solution.py:316
  49.6 0.7 collective-permute-done.1.refs_0_
  50.3 0.0 collective-permute-start.4
  50.3 3.2 %collective-permute-start.5 = (f32[520,384]{1,0:T(8,128)}, f32[520,384]{1,0:T(8,128)}, u32[]{:S(2)}, u32[]{:S(2)}) collective-permute-start(f32[520,384]{1,0:T(8,128)} %get-tuple-element.11.refs_1_), channel_id=1, source_target_pairs={{0,224},{1,33},{32,0},{33,65},{64,32},{65,97},{96,64},{97,129},{12... | collective-permute-start | bytes 2396168 | tf_op jit(solution)/shard_map/ppermute | solution.py:316
  53.5 4.2 %shard_map.86 = f32[8,2,64,384]{3,2,1,0:T(8,128)} custom-call(s32[4]{0:T(128)} %pad_add_fusion.meta, f32[520,384]{1,0:T(8,128)} %get-tuple-element.10.refs_0_, f32[520,384]{1,0:T(8,128)} %get-tuple-element.11.refs_1_), custom_call_target="tpu_custom_call" | custom-call | flops 40000000000 | tf_op jit(solution)/shard_map/pallas_call | solution.py:95
  57.7 5.3 %all-to-all-done.1.refs_2_.refs_1_.refs_0_ = f32[8,2,64,384]{3,2,1,0:T(8,128)} async-done(((f32[8,2,64,384]{3,2,1,0:T(8,128)}), f32[8,2,64,384]{3,2,1,0:T(8,128)}, u32[]{:S(2)}, u32[]{:S(2)}) %all-to-all-start.1) | async-done | bytes 1572896 | tf_op jit(solution)/shard_map/all_to_all | solution.py:323
  63.0 5.3 %all-to-all-start.3 = ((f32[8,2,64,384]{3,2,1,0:T(8,128)}), f32[8,2,64,384]{3,2,1,0:T(8,128)}, u32[]{:S(2)}, u32[]{:S(2)}) async-start(f32[8,2,64,384]{3,2,1,0:T(8,128)} %shard_map.86), calls=%async_computation.3 | async-start | bytes 3145728 | tf_op jit(solution)/shard_map/all_to_all | solution.py:323
  68.2 5.5 %collective-permute-done.8.refs_0_ = f32[128,32,128]{2,1,0:T(8,128)} collective-permute-done((f32[128,32,128]{2,1,0:T(8,128)}, f32[128,32,128]{2,1,0:T(8,128)}, u32[]{:S(2)}, u32[]{:S(2)}) %collective-permute-start.8) | collective-permute-done | bytes 2097184 | tf_op jit(solution)/shard_map/ppermute | solution.py:311
  73.7 0.0 collective-permute-start.9
  73.7 0.0 collective-permute-done.4.refs_0_
  73.7 0.0 collective-permute-done.5.refs_1_
  73.7 0.1 collective-permute-start.6
  73.8 4.2 %shard_map.90 = f32[8,2,64,384]{3,2,1,0:T(8,128)} custom-call(s32[4]{0:T(128)} %pad_add_fusion.meta, f32[520,384]{1,0:T(8,128)} %get-tuple-element.12.refs_0_, f32[520,384]{1,0:T(8,128)} %get-tuple-element.17.refs_1_), custom_call_target="tpu_custom_call" | custom-call | flops 15000000512 | tf_op jit(solution)/shard_map/pallas_call | solution.py:95
  78.0 0.0 collective-permute-done.7.i1
  78.0 0.2 collective-permute-done.9.i3
  78.2 7.4 %shard_map.84 = (bf16[512,1280]{1,0:T(8,128)(2,1)}, bf16[512,1280]{1,0:T(8,128)(2,1)}) custom-call(s32[4]{0:T(128)} %pad_add_fusion.meta, s32[8,64]{1,0:T(8,128)} %slots.3, f32[128,32,128]{2,1,0:T(8,128)} %shard_map.82.i0.refs_0_, f32[128,32,128]{2,1,0:T(8,128)} %collective-permute-done.7.i1, f32[128,32,128]{2,1,0:T(8,128)} %shard_map.83.i2, ...), custom_call_target="tpu_custom_call" | custom-call | flops 10000000000 | tf_op jit(solution)/shard_map/pallas_call | solution.py:169
  85.6 2.8 %all-to-all-done.3.refs_1_ = f32[8,2,64,384]{3,2,1,0:T(8,128)} async-done(((f32[8,2,64,384]{3,2,1,0:T(8,128)}), f32[8,2,64,384]{3,2,1,0:T(8,128)}, u32[]{:S(2)}, u32[]{:S(2)}) %all-to-all-start.3) | async-done | bytes 1572896 | tf_op jit(solution)/shard_map/all_to_all | solution.py:323
  88.4 4.9 %all-to-all-start.4 = ((f32[8,2,64,384]{3,2,1,0:T(8,128)}), f32[8,2,64,384]{3,2,1,0:T(8,128)}, u32[]{:S(2)}, u32[]{:S(2)}) async-start(f32[8,2,64,384]{3,2,1,0:T(8,128)} %shard_map.90), calls=%async_computation.4 | async-start | bytes 3145728 | tf_op jit(solution)/shard_map/all_to_all | solution.py:321
  93.4 6.0 %shard_map.87.refs_1_ = f32[512,384]{1,0:T(8,128)} custom-call(s32[4]{0:T(128)} %pad_add_fusion.meta, f32[8,2,64,384]{3,2,1,0:T(8,128)} %all-to-all-done.1.refs_2_.refs_1_.refs_0_, f32[8,2,64,384]{3,2,1,0:T(8,128)} %all-to-all-done.3.refs_1_, f32[8,1,64,384]{3,2,1,0:T(8,128)} %all-to-all-done.refs_2_, ...), custom_call_target="tpu_custom_call" | custom-call | flops 3000000000 | tf_op jit(solution)/shard_map/pallas_call | solution.py:216
  99.4 1.3 collective-permute-start.10
  100.7 10.7 %shard_map.89 = (bf16[512,2816]{1,0:T(8,128)(2,1)}, bf16[512,2816]{1,0:T(8,128)(2,1)}) custom-call(s32[4]{0:T(128)} %pad_add_fusion.meta, s32[8,64]{1,0:T(8,128)} %slots.3, f32[128,32,128]{2,1,0:T(8,128)} %shard_map.88.i0, f32[128,32,128]{2,1,0:T(8,128)} %collective-permute-done.7.i1, f32[128,32,128]{2,1,0:T(8,128)} %shard_map.83.i2, ...), custom_call_target="tpu_custom_call" | custom-call | flops 10000000000 | tf_op jit(solution)/shard_map/pallas_call | solution.py:169
  111.4 6.0 %shard_map.91.total = f32[512,384]{1,0:T(8,128)} custom-call(s32[4]{0:T(128)} %pad_add_fusion.meta, f32[8,2,64,384]{3,2,1,0:T(8,128)} %all-to-all-done.1.refs_2_.refs_1_.refs_0_, f32[8,2,64,384]{3,2,1,0:T(8,128)} %all-to-all-done.3.refs_1_, f32[8,1,64,384]{3,2,1,0:T(8,128)} %all-to-all-done.refs_2_, ...), custom_call_target="tpu_custom_call" | custom-call | flops 60000002048 | tf_op jit(solution)/shard_map/pallas_call | solution.py:216
  117.4 0.0 collective-permute-done.6.refs_0_
  117.4 3.6 %shard_map.85 = f32[8,1,64,384]{3,2,1,0:T(8,128)} custom-call(s32[4]{0:T(128)} %pad_add_fusion.meta, f32[520,384]{1,0:T(8,128)} %collective-permute-done.6.refs_0_, bf16[512,1280]{1,0:T(8,128)(2,1)} %get-tuple-element.13.refs_1_.refs_3_.refs_5_.refs_7_), custom_call_target="tpu_custom_call" | custom-call | flops 30000001024 | tf_op jit(solution)/shard_map/pallas_call | solution.py:95
  121.0 0.0 all-to-all-done.4.tiles
  121.0 7.8 %all-to-all-start.2 = ((f32[8,1,64,384]{3,2,1,0:T(8,128)}), f32[8,1,64,384]{3,2,1,0:T(8,128)}, u32[]{:S(2)}, u32[]{:S(2)}) async-start(f32[8,1,64,384]{3,2,1,0:T(8,128)} %shard_map.85), calls=%async_computation.2 | async-start | bytes 1572864 | tf_op jit(solution)/shard_map/all_to_all | solution.py:321
  128.8 5.0 %shard_map.92.total = f32[512,384]{1,0:T(8,128)} custom-call(f32[8,2,64,384]{3,2,1,0:T(8,128)} %all-to-all-done.4.tiles, bf16[512,2816]{1,0:T(8,128)(2,1)} %get-tuple-element.15.refs_3_.refs_5_.refs_7_.left_hi, bf16[512,2816]{1,0:T(8,128)(2,1)} %get-tuple-element.16.refs_4_.refs_6_.refs_8_.left_lo, f32[512,384]{1,0:T(8,128)} %shard_map.91.total), custom_call_target="tpu_custom_call" | custom-call | flops 60000002048 | tf_op jit(solution)/shard_map/pallas_call | solution.py:264
  133.8 6.7 %all-to-all-done.2.tiles = f32[8,1,64,384]{3,2,1,0:T(8,128)} async-done(((f32[8,1,64,384]{3,2,1,0:T(8,128)}), f32[8,1,64,384]{3,2,1,0:T(8,128)}, u32[]{:S(2)}, u32[]{:S(2)}) %all-to-all-start.2) | async-done | bytes 786464 | tf_op jit(solution)/shard_map/all_to_all | solution.py:321
  140.5 0.0 collective-permute-done.10.other
  140.5 4.6 %shard_map.93 = (f32[384,512]{1,0:T(8,128)}, f32[384,512]{1,0:T(8,128)}) custom-call(f32[8,1,64,384]{3,2,1,0:T(8,128)} %all-to-all-done.2.tiles, bf16[512,2816]{1,0:T(8,128)(2,1)} %get-tuple-element.15.refs_3_.refs_5_.refs_7_.left_hi, bf16[512,2816]{1,0:T(8,128)(2,1)} %get-tuple-element.16.refs_4_.refs_6_.refs_8_.left_lo, f32[512,384]{1,0:T(8,128)} %shard_map.92.total, ...), custom_call_target="tpu_custom_call" | custom-call | tf_op jit(solution)/shard_map/pallas_call | solution.py:246
  (4 shorter events, 0.0 us)
Async XLA Ops:
  3.0 25.3 %collective-permute-start.2 = (f32[520,384]{1,0:T(8,128)}, f32[520,384]{1,0:T(8,128)}, u32[]{:S(2)}, u32[]{:S(2)}) collective-permute-start(f32[520,384]{1,0:T(8,128)} %shard_map.77.refs_0_), channel_id=1, source_target_pairs={{0,224},{1,33},{32,0},{33,65},{64,32},{65,97},{96,64},{97,129},{12... | collective-permute-start | bytes 2396168 | tf_op jit(solution)/shard_map/ppermute | solution.py:316
  8.9 22.6 %collective-permute-start = (f32[520,384]{1,0:T(8,128)}, f32[520,384]{1,0:T(8,128)}, u32[]{:S(2)}, u32[]{:S(2)}) collective-permute-start(f32[520,384]{1,0:T(8,128)} %shard_map.77.refs_0_), channel_id=1, source_target_pairs={{0,32},{1,225},{32,64},{33,1},{64,96},{65,33},{96,128},{97,65},{12... | collective-permute-start | bytes 2396168 | tf_op jit(solution)/shard_map/ppermute | solution.py:316
  13.1 22.5 %all-to-all-start = ((f32[8,1,64,384]{3,2,1,0:T(8,128)}), f32[8,1,64,384]{3,2,1,0:T(8,128)}, u32[]{:S(2)}, u32[]{:S(2)}) async-start(f32[8,1,64,384]{3,2,1,0:T(8,128)} %shard_map.78.after), calls=%async_computation | async-start | bytes 1572864 | tf_op jit(solution)/shard_map/all_to_all | solution.py:323
  26.8 46.9 %collective-permute-start.8 = (f32[128,32,128]{2,1,0:T(8,128)}, f32[128,32,128]{2,1,0:T(8,128)}, u32[]{:S(2)}, u32[]{:S(2)}) collective-permute-start(f32[128,32,128]{2,1,0:T(8,128)} %shard_map.82.i0.refs_0_), channel_id=1, source_target_pairs={{0,2},{2,0},{1,3},{3,1},{4,6},{6,4},{5,7},{7,5},{8,10},{10,8},{9,1... | collective-permute-start | bytes 6291464 | tf_op jit(solution)/shard_map/ppermute | solution.py:311
  27.0 51.0 %collective-permute-start.7 = (f32[128,32,128]{2,1,0:T(8,128)}, f32[128,32,128]{2,1,0:T(8,128)}, u32[]{:S(2)}, u32[]{:S(2)}) collective-permute-start(f32[128,32,128]{2,1,0:T(8,128)} %shard_map.82.i0.refs_0_), channel_id=1, source_target_pairs={{0,1},{1,0},{2,3},{3,2},{4,5},{5,4},{6,7},{7,6},{8,9},{9,8},{10,11... | collective-permute-start | bytes 6291464 | tf_op jit(solution)/shard_map/ppermute | solution.py:311
  28.3 21.4 %collective-permute-start.3 = (f32[520,384]{1,0:T(8,128)}, f32[520,384]{1,0:T(8,128)}, u32[]{:S(2)}, u32[]{:S(2)}) collective-permute-start(f32[520,384]{1,0:T(8,128)} %collective-permute-done.2.refs_1_), channel_id=1, source_target_pairs={{0,224},{1,33},{32,0},{33,65},{64,32},{65,97},{96,64},{97,129},{12... | collective-permute-start | bytes 2396168 | tf_op jit(solution)/shard_map/ppermute | solution.py:316
  31.5 18.8 %collective-permute-start.1 = (f32[520,384]{1,0:T(8,128)}, f32[520,384]{1,0:T(8,128)}, u32[]{:S(2)}, u32[]{:S(2)}) collective-permute-start(f32[520,384]{1,0:T(8,128)} %collective-permute-done.refs_0_), channel_id=1, source_target_pairs={{0,32},{1,225},{32,64},{33,1},{64,96},{65,33},{96,128},{97,65},{12... | collective-permute-start | bytes 2396168 | tf_op jit(solution)/shard_map/ppermute | solution.py:316
  35.7 27.3 %all-to-all-start.1 = ((f32[8,2,64,384]{3,2,1,0:T(8,128)}), f32[8,2,64,384]{3,2,1,0:T(8,128)}, u32[]{:S(2)}, u32[]{:S(2)}) async-start(f32[8,2,64,384]{3,2,1,0:T(8,128)} %shard_map.80), calls=%async_computation.1 | async-start | bytes 3145728 | tf_op jit(solution)/shard_map/all_to_all | solution.py:323
  50.3 23.4 %collective-permute-start.4 = (f32[520,384]{1,0:T(8,128)}, f32[520,384]{1,0:T(8,128)}, u32[]{:S(2)}, u32[]{:S(2)}) collective-permute-start(f32[520,384]{1,0:T(8,128)} %get-tuple-element.10.refs_0_), channel_id=1, source_target_pairs={{0,32},{1,225},{32,64},{33,1},{64,96},{65,33},{96,128},{97,65},{12... | collective-permute-start | bytes 2396168 | tf_op jit(solution)/shard_map/ppermute | solution.py:316
  50.3 23.4 %collective-permute-start.5 = (f32[520,384]{1,0:T(8,128)}, f32[520,384]{1,0:T(8,128)}, u32[]{:S(2)}, u32[]{:S(2)}) collective-permute-start(f32[520,384]{1,0:T(8,128)} %get-tuple-element.11.refs_1_), channel_id=1, source_target_pairs={{0,224},{1,33},{32,0},{33,65},{64,32},{65,97},{96,64},{97,129},{12... | collective-permute-start | bytes 2396168 | tf_op jit(solution)/shard_map/ppermute | solution.py:316
  63.0 25.5 %all-to-all-start.3 = ((f32[8,2,64,384]{3,2,1,0:T(8,128)}), f32[8,2,64,384]{3,2,1,0:T(8,128)}, u32[]{:S(2)}, u32[]{:S(2)}) async-start(f32[8,2,64,384]{3,2,1,0:T(8,128)} %shard_map.86), calls=%async_computation.3 | async-start | bytes 3145728 | tf_op jit(solution)/shard_map/all_to_all | solution.py:323
  73.7 4.5 %collective-permute-start.9 = (f32[128,32,128]{2,1,0:T(8,128)}, f32[128,32,128]{2,1,0:T(8,128)}, u32[]{:S(2)}, u32[]{:S(2)}) collective-permute-start(f32[128,32,128]{2,1,0:T(8,128)} %shard_map.83.i2), channel_id=1, source_target_pairs={{0,1},{1,0},{2,3},{3,2},{4,5},{5,4},{6,7},{7,6},{8,9},{9,8},{10,11... | collective-permute-start | bytes 6291464 | tf_op jit(solution)/shard_map/ppermute | solution.py:311
  73.7 43.7 %collective-permute-start.6 = (f32[520,384]{1,0:T(8,128)}, f32[520,384]{1,0:T(8,128)}, u32[]{:S(2)}, u32[]{:S(2)}) collective-permute-start(f32[520,384]{1,0:T(8,128)} %get-tuple-element.12.refs_0_), channel_id=1, source_target_pairs={{0,32},{1,225},{32,64},{33,1},{64,96},{65,33},{96,128},{97,65},{12... | collective-permute-start | bytes 2396168 | tf_op jit(solution)/shard_map/ppermute | solution.py:316
  88.4 32.6 %all-to-all-start.4 = ((f32[8,2,64,384]{3,2,1,0:T(8,128)}), f32[8,2,64,384]{3,2,1,0:T(8,128)}, u32[]{:S(2)}, u32[]{:S(2)}) async-start(f32[8,2,64,384]{3,2,1,0:T(8,128)} %shard_map.90), calls=%async_computation.4 | async-start | bytes 3145728 | tf_op jit(solution)/shard_map/all_to_all | solution.py:321
  99.4 41.1 %collective-permute-start.10 = (f32[512,384]{1,0:T(8,128)}, f32[512,384]{1,0:T(8,128)}, u32[]{:S(2)}, u32[]{:S(2)}) collective-permute-start(f32[512,384]{1,0:T(8,128)} %shard_map.87.refs_1_), channel_id=1, source_target_pairs={{0,2},{2,0},{1,3},{3,1},{4,6},{6,4},{5,7},{7,5},{8,10},{10,8},{9,1... | collective-permute-start | bytes 2359304 | tf_op jit(solution)/shard_map/ppermute | solution.py:311
  121.0 19.5 %all-to-all-start.2 = ((f32[8,1,64,384]{3,2,1,0:T(8,128)}), f32[8,1,64,384]{3,2,1,0:T(8,128)}, u32[]{:S(2)}, u32[]{:S(2)}) async-start(f32[8,1,64,384]{3,2,1,0:T(8,128)} %shard_map.85), calls=%async_computation.2 | async-start | bytes 1572864 | tf_op jit(solution)/shard_map/all_to_all | solution.py:321

commit v9 on v8

--- a/solution.py
+++ b/solution.py
@@ -103,6 +103,36 @@
     )(meta, *in_hbm(*sources), *after)
 
 
+def scatter_kernel(meta, source, *refs):
+    outs, notes, sems = refs[-PLANE - 2 : -2], refs[-2], refs[-1]
+    rows = ROW_TILES * TILE
+    read = pltpu.make_async_copy(source.at[pl.ds(rows, NOTE), pl.ds(0, 128)], notes, sems.at[PLANE])
+    read.start()
+    read.wait()
+    copies = []
+    for n, out in enumerate(outs):
+        reader = meta[0] * PLANE + (meta[1] ^ (n // Y)) * Y + ((meta[4] + n % Y) & (Y - 1))
+        tile = jnp.clip(notes[0, reader].astype(jnp.int32), 0, ROW_TILES - 1)
+        copy = pltpu.make_async_copy(source.at[pl.ds(pl.multiple_of(tile * TILE, TILE), TILE)], out, sems.at[n])
+        copy.start()
+        copies.append(copy)
+    for copy in copies:
+        copy.wait()
+
+
+def scatter(meta, source, after, micros):
+    shape = jax.ShapeDtypeStruct((TILE, source.shape[1]), jnp.float32)
+    return pl.pallas_call(
+        scatter_kernel,
+        compiler_params=PARAMS,
+        out_shape=[shape] * PLANE,
+        in_specs=[SCALARS, IN_HBM] + [ANYWHERE] * len(after),
+        out_specs=[INSIDE] * PLANE,
+        scratch_shapes=[pltpu.SMEM((NOTE, 128), jnp.float32), pltpu.SemaphoreType.DMA((PLANE + 1,))],
+        cost_estimate=cost(micros),
+    )(meta, *in_hbm(source), *after)
+
+
 def places(offsets, sources, flipped):
     return [(offset, source, flipped) for source in sources for offset in offsets]
 
@@ -112,7 +142,7 @@
     places((3, -3), range(8), False)
     + places((1, -1), range(4), True)
     + places((2, -2), range(4), True)
-    + places((4,), range(8), False)
+    + places((4,), range(8), None)
     + places((0,), range(4), True)
 )
 
@@ -133,7 +163,10 @@
         mine = meta[3] * CO + core
         sign = 1 - 2 * core
         for n, (offset, source, flipped) in enumerate(owners):
-            peer = source ^ (half * Y) if flipped else source
+            if flipped is None:
+                peer = (half ^ (source // Y)) * Y + ((meta[4] - source % Y) & (Y - 1))
+            else:
+                peer = source ^ (half * Y) if flipped else source
             order[n] = ((z - sign * offset) & (Z - 1)) * PLANE + peer
 
         def fill(k, carry):
@@ -227,8 +260,10 @@
     )(meta, *tiles, *(list(left) * len(tiles)))
 
 
-def last_kernel(tiles, left_hi, left_lo, total, other, amp, row_gap, col_gap, res, new):
-    values = tiles[...].reshape(left_hi.shape[1], tiles.shape[-1])
+def last_kernel(*refs):
+    tiles, refs = refs[:PLANE], refs[PLANE:]
+    left_hi, left_lo, total, other, amp, row_gap, col_gap, res, new = refs
+    values = jnp.concatenate([tile[...] for tile in tiles], axis=0)
     cycle = (total[...] + other[...] + product(left_hi[...], left_lo[...], values)).T
     column = jnp.broadcast_to(col_gap[...], (8, col_gap.shape[1])).T[:, :1]
     gap = column + row_gap[...]
@@ -239,18 +274,19 @@
 
 
 def last(offset, tiles, left, total, other, amp, row_gap, col_gap):
-    rows, cols = left[0].shape[0], tiles.shape[-1]
-    depth = PLANE * tiles.shape[1] * TILE
+    cols, rows = amp.shape
+    depth = PLANE * TILE
     block = pl.BlockSpec((rows, depth), lambda g: (0, offset // depth))
     shape = jax.ShapeDtypeStruct((cols, rows), jnp.float32)
+    rest = (total, other, amp, row_gap, col_gap)
     return pl.pallas_call(
         last_kernel,
         grid=(1,),
         out_shape=(shape, shape),
-        in_specs=[full(tiles), block, block, full(total), full(other), full(amp), full(row_gap), full(col_gap)],
+        in_specs=[full(t) for t in tiles] + [block, block] + [full(x) for x in rest],
         out_specs=(full(shape), full(shape)),
         compiler_params=PARAMS,
-    )(tiles, *left, total, other, amp, row_gap, col_gap)
+    )(*tiles, *left, *rest)
 
 
 def more_kernel(tiles, left_hi, left_lo, total, out):
@@ -316,6 +352,13 @@
     return lax.ppermute(x, ("z", "co"), turns)
 
 
+def send(x, n):
+    if n == 0:
+        return x
+    turns = [(xh * Y + y, (xh ^ (n // Y)) * Y + (y + n % Y) % Y) for xh in range(XH) for y in range(Y)]
+    return lax.ppermute(x, ("xh", "y"), turns)
+
+
 def exchange(x, mirrored):
     if not mirrored:
         return lax.all_to_all(x, ("xh", "y"), 0, 0, tiled=True)
@@ -324,7 +367,7 @@
 
 
 def body(amplitudes, integrals, send_tiles, task_slots, row_gap, column_gap):
-    meta = jnp.stack([lax.axis_index(n) for n in ("z", "xh", "co", "xl")]).astype(jnp.int32)
+    meta = jnp.stack([lax.axis_index(n) for n in ("z", "xh", "co", "xl", "y")]).astype(jnp.int32)
     owned = first(amplitudes, send_tiles)
     ring = {0: owned}
     received, chosen = [], []
@@ -343,6 +386,9 @@
             left = in_hbm(*prepare(OTHERS, meta, task_slots, pieces, PREPARE_COSTS[0]))
         if n == Z // 2:
             after = left[:1]
+            apart = scatter(meta, ring[n], after, SELECT_COST[n])
+            received.append([send(x, r) for r, x in enumerate(apart)])
+            break
         outgoing = select(meta, [ring[o] for o in offsets], after, SELECT_COST[n])
         if n == 0:
             packed = pack(integrals, outgoing)

time: 146 us -> 148 us (1.014)
  starting transfers between devices: 45.9 us -> 52.4 us
  waiting for transfers between devices: 28.3 us -> 24 us
    ppermute x0 -> x7, starting transfers between devices: none -> 14.3 us  [send(): return lax.ppermute(x, ('xh', 'y'), turns)]
    all_to_all x2 -> x1, starting transfers between devices: 12.8 us -> 4.94 us  [exchange(): return lax.all_to_all(x, ('xh', 'y'), 0, 0, tiled=True)]
    all_to_all x2 -> x1, waiting for transfers between devices: 6.69 us -> 0.01 us  [exchange(): return lax.all_to_all(x, ('xh', 'y'), 0, 0, tiled=True)]
    pallas_call x0 -> x1, Pallas kernels: none -> 3.62 us  [scatter(): pl.pallas_call(scatter_kernel, compiler_params=PARAMS, out_shape=[shape]...]
    pallas_call x5 -> x4, Pallas kernels: 19.7 us -> 16.2 us  [select(): pl.pallas_call(functools.partial(select_kernel, owners), compiler_params=...]
    ppermute x0 -> x7, waiting for transfers between devices: none -> 2.36 us  [send(): return lax.ppermute(x, ('xh', 'y'), turns)]
  transfers between devices with their start and end apart: 16 -> 22, of which waited for: 7 -> 8; matrix products, arithmetic and copies ran while one was open for 1% -> 1% of each run, Pallas kernels for 42% -> 42%
where the time goes in v9:
time: 148 us; the launch traced here: 147 us
  Pallas kernels  68.3 us (46%)
  starting transfers between devices  52.4 us (35%)
  waiting for transfers between devices  24 us (16%)
  local copies, waits for them, and re-layouts  1.91 us (1%)
    all_to_all x3, starting transfers between devices, exchange(): lax.all_to_all(x, ('xh', 'y', 'xl'), 0, 0, axis_index_groups=groups, tile...  19.1 us
    pallas_call x2, Pallas kernels, prepare(): pl.pallas_call(functools.partial(prepare_kernel, owners), grid=(len(owner...  17.9 us
    pallas_call x4, Pallas kernels, select(): pl.pallas_call(functools.partial(select_kernel, owners), compiler_params=...  16.2 us
    ppermute x7, starting transfers between devices, send(): return lax.ppermute(x, ('xh', 'y'), turns)  14.3 us
    ppermute x7, starting transfers between devices, shift(): return lax.ppermute(x, ('z', 'co'), turns)  12.5 us
    pallas_call x2, Pallas kernels, steps(): pl.pallas_call(functools.partial(steps_kernel, len(tiles)), out_shape=sha...  12 us
    all_to_all x3, waiting for transfers between devices, exchange(): lax.all_to_all(x, ('xh', 'y', 'xl'), 0, 0, axis_index_groups=groups, tile...  7.99 us
    ppermute x7, waiting for transfers between devices, shift(): return lax.ppermute(x, ('z', 'co'), turns)  7.89 us
  transfers between devices with their start and end apart: 22, of which 8 were waited for; matrix products, arithmetic and copies ran while one was open for 1% of the time, Pallas kernels for 42%

profile of v9, /device:TPU:8, one launch (start us, length us, event | category | flops | bytes accessed | tf_op | source)
XLA Modules:
  0.0 147.3 jit_solution(9461992750745935689)
XLA Ops:
  0.6 2.3 %shard_map.77.refs_0_ = f32[520,384]{1,0:T(8,128)} custom-call(f32[384,512]{1,0:T(8,128)} %refs_12_.1, s32[1,64]{1,0:T(1,128)} %send.1), custom_call_target="tpu_custom_call" | custom-call | tf_op jit(solution)/shard_map/pallas_call | solution.py:60
  3.0 5.9 %collective-permute-start.2 = (f32[520,384]{1,0:T(8,128)}, f32[520,384]{1,0:T(8,128)}, u32[]{:S(2)}, u32[]{:S(2)}) collective-permute-start(f32[520,384]{1,0:T(8,128)} %shard_map.77.refs_0_), channel_id=1, source_target_pairs={{0,224},{1,33},{32,0},{33,65},{64,32},{65,97},{96,64},{97,129},{12... | collective-permute-start | bytes 2396168 | tf_op jit(solution)/shard_map/ppermute | solution.py:352
  8.9 0.0 collective-permute-start
  8.9 0.7 stack.23.meta
  9.6 3.6 %shard_map.78.after = f32[8,1,64,384]{3,2,1,0:T(8,128)} custom-call(s32[5]{0:T(128)} %stack.23.meta, f32[520,384]{1,0:T(8,128)} %shard_map.77.refs_0_), custom_call_target="tpu_custom_call" | custom-call | flops 40000000000 | tf_op jit(solution)/shard_map/pallas_call | solution.py:95
  13.1 7.1 %all-to-all-start = ((f32[8,1,64,384]{3,2,1,0:T(8,128)}), f32[8,1,64,384]{3,2,1,0:T(8,128)}, u32[]{:S(2)}, u32[]{:S(2)}) async-start(f32[8,1,64,384]{3,2,1,0:T(8,128)} %shard_map.78.after), calls=%async_computation | async-start | bytes 1572864 | tf_op jit(solution)/shard_map/all_to_all | solution.py:366
  20.3 6.5 %shard_map.82.i0.refs_0_ = f32[128,32,128]{2,1,0:T(8,128)} custom-call(f32[8,16,64,64]{3,2,1,0:T(8,128)} %integrals.1, f32[8,1,64,384]{3,2,1,0:T(8,128)} %shard_map.78.after), custom_call_target="tpu_custom_call" | custom-call | flops 40000000000 | tf_op jit(solution)/shard_map/pallas_call | solution.py:335
  26.8 0.2 collective-permute-start.8
  27.0 0.0 collective-permute-start.7
  27.0 1.2 broadcast_in_dim.7.refs_14_
  28.2 0.0 collective-permute-done.2.refs_1_
  28.2 3.2 %collective-permute-start.3 = (f32[520,384]{1,0:T(8,128)}, f32[520,384]{1,0:T(8,128)}, u32[]{:S(2)}, u32[]{:S(2)}) collective-permute-start(f32[520,384]{1,0:T(8,128)} %collective-permute-done.2.refs_1_), channel_id=1, source_target_pairs={{0,224},{1,33},{32,0},{33,65},{64,32},{65,97},{96,64},{97,129},{12... | collective-permute-start | bytes 2396168 | tf_op jit(solution)/shard_map/ppermute | solution.py:352
  31.5 0.0 collective-permute-done.refs_0_
  31.5 0.0 collective-permute-start.1
  31.5 4.2 %shard_map.80 = f32[8,2,64,384]{3,2,1,0:T(8,128)} custom-call(s32[5]{0:T(128)} %stack.23.meta, f32[520,384]{1,0:T(8,128)} %collective-permute-done.refs_0_, f32[520,384]{1,0:T(8,128)} %collective-permute-done.2.refs_1_), custom_call_target="tpu_custom_call" | custom-call | flops 40000000000 | tf_op jit(solution)/shard_map/pallas_call | solution.py:95
  35.7 0.0 all-to-all-done.refs_2_
  35.7 6.7 %all-to-all-start.1 = ((f32[8,2,64,384]{3,2,1,0:T(8,128)}), f32[8,2,64,384]{3,2,1,0:T(8,128)}, u32[]{:S(2)}, u32[]{:S(2)}) async-start(f32[8,2,64,384]{3,2,1,0:T(8,128)} %shard_map.80), calls=%async_computation.1 | async-start | bytes 3145728 | tf_op jit(solution)/shard_map/all_to_all | solution.py:366
  42.4 7.2 %collective-permute-done.3.refs_1_ = f32[520,384]{1,0:T(8,128)} collective-permute-done((f32[520,384]{1,0:T(8,128)}, f32[520,384]{1,0:T(8,128)}, u32[]{:S(2)}, u32[]{:S(2)}) %collective-permute-start.3) | collective-permute-done | bytes 798752 | tf_op jit(solution)/shard_map/ppermute | solution.py:352
  49.6 0.7 collective-permute-done.1.refs_0_
  50.3 0.0 collective-permute-start.4
  50.3 3.2 %collective-permute-start.5 = (f32[520,384]{1,0:T(8,128)}, f32[520,384]{1,0:T(8,128)}, u32[]{:S(2)}, u32[]{:S(2)}) collective-permute-start(f32[520,384]{1,0:T(8,128)} %get-tuple-element.19.refs_1_), channel_id=1, source_target_pairs={{0,224},{1,33},{32,0},{33,65},{64,32},{65,97},{96,64},{97,129},{12... | collective-permute-start | bytes 2396168 | tf_op jit(solution)/shard_map/ppermute | solution.py:352
  53.5 4.3 %shard_map.86 = f32[8,2,64,384]{3,2,1,0:T(8,128)} custom-call(s32[5]{0:T(128)} %stack.23.meta, f32[520,384]{1,0:T(8,128)} %get-tuple-element.18.refs_0_, f32[520,384]{1,0:T(8,128)} %get-tuple-element.19.refs_1_), custom_call_target="tpu_custom_call" | custom-call | flops 40000000000 | tf_op jit(solution)/shard_map/pallas_call | solution.py:95
  57.8 5.2 %all-to-all-done.1.refs_2_.refs_1_.refs_0_ = f32[8,2,64,384]{3,2,1,0:T(8,128)} async-done(((f32[8,2,64,384]{3,2,1,0:T(8,128)}), f32[8,2,64,384]{3,2,1,0:T(8,128)}, u32[]{:S(2)}, u32[]{:S(2)}) %all-to-all-start.1) | async-done | bytes 1572896 | tf_op jit(solution)/shard_map/all_to_all | solution.py:366
  62.9 5.3 %all-to-all-start.2 = ((f32[8,2,64,384]{3,2,1,0:T(8,128)}), f32[8,2,64,384]{3,2,1,0:T(8,128)}, u32[]{:S(2)}, u32[]{:S(2)}) async-start(f32[8,2,64,384]{3,2,1,0:T(8,128)} %shard_map.86), calls=%async_computation.2 | async-start | bytes 3145728 | tf_op jit(solution)/shard_map/all_to_all | solution.py:366
  68.2 5.5 %collective-permute-done.8.refs_0_ = f32[128,32,128]{2,1,0:T(8,128)} collective-permute-done((f32[128,32,128]{2,1,0:T(8,128)}, f32[128,32,128]{2,1,0:T(8,128)}, u32[]{:S(2)}, u32[]{:S(2)}) %collective-permute-start.8) | collective-permute-done | bytes 2097184 | tf_op jit(solution)/shard_map/ppermute | solution.py:347
  73.7 0.0 collective-permute-start.9
  73.7 0.0 collective-permute-done.4.refs_0_
  73.7 0.0 collective-permute-done.5.refs_1_
  73.7 0.1 collective-permute-start.6
  73.8 4.2 %shard_map.90 = f32[8,2,64,384]{3,2,1,0:T(8,128)} custom-call(s32[5]{0:T(128)} %stack.23.meta, f32[520,384]{1,0:T(8,128)} %get-tuple-element.20.refs_0_, f32[520,384]{1,0:T(8,128)} %get-tuple-element.33.refs_1_), custom_call_target="tpu_custom_call" | custom-call | flops 15000000512 | tf_op jit(solution)/shard_map/pallas_call | solution.py:95
  78.0 0.0 collective-permute-done.7.i1
  78.0 0.2 collective-permute-done.9.i3
  78.2 7.4 %shard_map.84 = (bf16[512,1280]{1,0:T(8,128)(2,1)}, bf16[512,1280]{1,0:T(8,128)(2,1)}) custom-call(s32[5]{0:T(128)} %stack.23.meta, s32[8,64]{1,0:T(8,128)} %slots.3, f32[128,32,128]{2,1,0:T(8,128)} %shard_map.82.i0.refs_0_, f32[128,32,128]{2,1,0:T(8,128)} %collective-permute-done.7.i1, f32[128,32,128]{2,1,0:T(8,128)} %shard_map.83.i2, ...), custom_call_target="tpu_custom_call" | custom-call | flops 10000000000 | tf_op jit(solution)/shard_map/pallas_call | solution.py:202
  85.6 2.8 %all-to-all-done.2.refs_1_ = f32[8,2,64,384]{3,2,1,0:T(8,128)} async-done(((f32[8,2,64,384]{3,2,1,0:T(8,128)}), f32[8,2,64,384]{3,2,1,0:T(8,128)}, u32[]{:S(2)}, u32[]{:S(2)}) %all-to-all-start.2) | async-done | bytes 1572896 | tf_op jit(solution)/shard_map/all_to_all | solution.py:366
  88.4 4.9 %all-to-all-start.3 = ((f32[8,2,64,384]{3,2,1,0:T(8,128)}), f32[8,2,64,384]{3,2,1,0:T(8,128)}, u32[]{:S(2)}, u32[]{:S(2)}) async-start(f32[8,2,64,384]{3,2,1,0:T(8,128)} %shard_map.90), calls=%async_computation.3 | async-start | bytes 3145728 | tf_op jit(solution)/shard_map/all_to_all | solution.py:364
  93.3 6.0 %shard_map.87.refs_1_ = f32[512,384]{1,0:T(8,128)} custom-call(s32[5]{0:T(128)} %stack.23.meta, f32[8,2,64,384]{3,2,1,0:T(8,128)} %all-to-all-done.1.refs_2_.refs_1_.refs_0_, f32[8,2,64,384]{3,2,1,0:T(8,128)} %all-to-all-done.2.refs_1_, f32[8,1,64,384]{3,2,1,0:T(8,128)} %all-to-all-done.refs_2_, ...), custom_call_target="tpu_custom_call" | custom-call | flops 3000000000 | tf_op jit(solution)/shard_map/pallas_call | solution.py:249
  99.3 1.3 collective-permute-start.17
  100.6 0.0 collective-permute-done.6.source
  100.6 3.6 %shard_map.85 = (f32[64,384]{1,0:T(8,128)}, f32[64,384]{1,0:T(8,128)}, f32[64,384]{1,0:T(8,128)}, f32[64,384]{1,0:T(8,128)}, f32[64,384]{1,0:T(8,128)}, /*index=...) custom-call(s32[5]{0:T(128)} %stack.23.meta, f32[520,384]{1,0:T(8,128)} %collective-permute-done.6.source, ...), custom_call_target="tpu_custom_call" | custom-call | flops 30000001024 | tf_op jit(solution)/shard_map/pallas_call | solution.py:125
  104.3 1.5 %collective-permute-start.10 = (f32[64,384]{1,0:T(8,128)}, f32[64,384]{1,0:T(8,128)}, u32[]{:S(2)}, u32[]{:S(2)}) collective-permute-start(f32[64,384]{1,0:T(8,128)} %get-tuple-element.23), channel_id=1, source_target_pairs={{0,4},{4,8},{8,12},{12,0},{16,20},{20,24},{24,28},{28,16},{1,5},{5... | collective-permute-start | bytes 294920 | tf_op jit(solution)/shard_map/ppermute | solution.py:359
  105.8 0.9 collective-permute-start.11
  106.7 2.4 %collective-permute-start.12 = (f32[64,384]{1,0:T(8,128)}, f32[64,384]{1,0:T(8,128)}, u32[]{:S(2)}, u32[]{:S(2)}) collective-permute-start(f32[64,384]{1,0:T(8,128)} %get-tuple-element.25), channel_id=1, source_target_pairs={{0,12},{4,0},{8,4},{12,8},{16,28},{20,16},{24,20},{28,24},{1,13},{... | collective-permute-start | bytes 294920 | tf_op jit(solution)/shard_map/ppermute | solution.py:359
  109.0 3.6 %collective-permute-start.13 = (f32[64,384]{1,0:T(8,128)}, f32[64,384]{1,0:T(8,128)}, u32[]{:S(2)}, u32[]{:S(2)}) collective-permute-start(f32[64,384]{1,0:T(8,128)} %get-tuple-element.26), channel_id=1, source_target_pairs={{0,16},{4,20},{8,24},{12,28},{16,0},{20,4},{24,8},{28,12},{1,17},{... | collective-permute-start | bytes 294920 | tf_op jit(solution)/shard_map/ppermute | solution.py:359
  112.6 10.6 %shard_map.89 = (bf16[512,2816]{1,0:T(8,128)(2,1)}, bf16[512,2816]{1,0:T(8,128)(2,1)}) custom-call(s32[5]{0:T(128)} %stack.23.meta, s32[8,64]{1,0:T(8,128)} %slots.3, f32[128,32,128]{2,1,0:T(8,128)} %shard_map.88.i0, f32[128,32,128]{2,1,0:T(8,128)} %collective-permute-done.7.i1, f32[128,32,128]{2,1,0:T(8,128)} %shard_map.83.i2, ...), custom_call_target="tpu_custom_call" | custom-call | flops 10000000000 | tf_op jit(solution)/shard_map/pallas_call | solution.py:202
  123.2 6.0 %shard_map.91.total = f32[512,384]{1,0:T(8,128)} custom-call(s32[5]{0:T(128)} %stack.23.meta, f32[8,2,64,384]{3,2,1,0:T(8,128)} %all-to-all-done.1.refs_2_.refs_1_.refs_0_, f32[8,2,64,384]{3,2,1,0:T(8,128)} %all-to-all-done.2.refs_1_, f32[8,1,64,384]{3,2,1,0:T(8,128)} %all-to-all-done.refs_2_, ...), custom_call_target="tpu_custom_call" | custom-call | flops 60000002048 | tf_op jit(solution)/shard_map/pallas_call | solution.py:249
  129.2 0.0 collective-permute-done.10.refs_1_
  129.2 0.0 collective-permute-start.14
  129.2 0.0 collective-permute-done.11.refs_2_
  129.2 6.0 %collective-permute-start.15 = (f32[64,384]{1,0:T(8,128)}, f32[64,384]{1,0:T(8,128)}, u32[]{:S(2)}, u32[]{:S(2)}) collective-permute-start(f32[64,384]{1,0:T(8,128)} %get-tuple-element.28), channel_id=1, source_target_pairs={{0,24},{4,28},{8,16},{12,20},{16,8},{20,12},{24,0},{28,4},{1,25},{... | collective-permute-start | bytes 294920 | tf_op jit(solution)/shard_map/ppermute | solution.py:359
  135.2 0.0 collective-permute-done.12.refs_3_
  135.2 0.0 collective-permute-start.16
  135.2 0.0 all-to-all-done.3.tiles
  135.2 5.0 %shard_map.92.refs_10_ = f32[512,384]{1,0:T(8,128)} custom-call(f32[8,2,64,384]{3,2,1,0:T(8,128)} %all-to-all-done.3.tiles, bf16[512,2816]{1,0:T(8,128)(2,1)} %get-tuple-element.31.refs_3_.refs_5_.refs_7_.left_hi.refs_8_, bf16[512,2816]{1,0:T(8,128)(2,1)} %get-tuple-element.32.refs_4_.refs_6_.refs_8_.left_lo.refs_9_, f32[512,384]{1,0:T(8,128)} %shard_map.91.total), custom_call_target="tpu_custom_call" | custom-call | flops 60000002048 | tf_op jit(solution)/shard_map/pallas_call | solution.py:300
  140.2 0.0 collective-permute-done.13.refs_4_
  140.2 0.0 collective-permute-done.14.refs_5_
  140.2 0.3 collective-permute-done.15.refs_6_
  140.5 2.1 %collective-permute-done.16.refs_7_ = f32[64,384]{1,0:T(8,128)} collective-permute-done((f32[64,384]{1,0:T(8,128)}, f32[64,384]{1,0:T(8,128)}, u32[]{:S(2)}, u32[]{:S(2)}) %collective-permute-start.16) | collective-permute-done | bytes 98336 | tf_op jit(solution)/shard_map/ppermute | solution.py:359
  142.6 0.0 collective-permute-done.17.refs_11_
  142.6 4.7 %shard_map.93 = (f32[384,512]{1,0:T(8,128)}, f32[384,512]{1,0:T(8,128)}) custom-call(f32[64,384]{1,0:T(8,128)} %get-tuple-element.22.refs_0_, f32[64,384]{1,0:T(8,128)} %collective-permute-done.10.refs_1_, f32[64,384]{1,0:T(8,128)} %collective-permute-done.11.refs_2_, f32[64,384]{1,0:T(8,128)} %collective-permute-done.12.refs_3_, ...), custom_call_target="tpu_custom_call" | custom-call | tf_op jit(solution)/shard_map/pallas_call | solution.py:282
  (4 shorter events, 0.0 us)
Async XLA Ops:
  3.0 25.3 %collective-permute-start.2 = (f32[520,384]{1,0:T(8,128)}, f32[520,384]{1,0:T(8,128)}, u32[]{:S(2)}, u32[]{:S(2)}) collective-permute-start(f32[520,384]{1,0:T(8,128)} %shard_map.77.refs_0_), channel_id=1, source_target_pairs={{0,224},{1,33},{32,0},{33,65},{64,32},{65,97},{96,64},{97,129},{12... | collective-permute-start | bytes 2396168 | tf_op jit(solution)/shard_map/ppermute | solution.py:352
  8.9 22.6 %collective-permute-start = (f32[520,384]{1,0:T(8,128)}, f32[520,384]{1,0:T(8,128)}, u32[]{:S(2)}, u32[]{:S(2)}) collective-permute-start(f32[520,384]{1,0:T(8,128)} %shard_map.77.refs_0_), channel_id=1, source_target_pairs={{0,32},{1,225},{32,64},{33,1},{64,96},{65,33},{96,128},{97,65},{12... | collective-permute-start | bytes 2396168 | tf_op jit(solution)/shard_map/ppermute | solution.py:352
  13.1 22.5 %all-to-all-start = ((f32[8,1,64,384]{3,2,1,0:T(8,128)}), f32[8,1,64,384]{3,2,1,0:T(8,128)}, u32[]{:S(2)}, u32[]{:S(2)}) async-start(f32[8,1,64,384]{3,2,1,0:T(8,128)} %shard_map.78.after), calls=%async_computation | async-start | bytes 1572864 | tf_op jit(solution)/shard_map/all_to_all | solution.py:366
  26.8 46.9 %collective-permute-start.8 = (f32[128,32,128]{2,1,0:T(8,128)}, f32[128,32,128]{2,1,0:T(8,128)}, u32[]{:S(2)}, u32[]{:S(2)}) collective-permute-start(f32[128,32,128]{2,1,0:T(8,128)} %shard_map.82.i0.refs_0_), channel_id=1, source_target_pairs={{0,2},{2,0},{1,3},{3,1},{4,6},{6,4},{5,7},{7,5},{8,10},{10,8},{9,1... | collective-permute-start | bytes 6291464 | tf_op jit(solution)/shard_map/ppermute | solution.py:347
  27.0 51.0 %collective-permute-start.7 = (f32[128,32,128]{2,1,0:T(8,128)}, f32[128,32,128]{2,1,0:T(8,128)}, u32[]{:S(2)}, u32[]{:S(2)}) collective-permute-start(f32[128,32,128]{2,1,0:T(8,128)} %shard_map.82.i0.refs_0_), channel_id=1, source_target_pairs={{0,1},{1,0},{2,3},{3,2},{4,5},{5,4},{6,7},{7,6},{8,9},{9,8},{10,11... | collective-permute-start | bytes 6291464 | tf_op jit(solution)/shard_map/ppermute | solution.py:347
  28.2 21.4 %collective-permute-start.3 = (f32[520,384]{1,0:T(8,128)}, f32[520,384]{1,0:T(8,128)}, u32[]{:S(2)}, u32[]{:S(2)}) collective-permute-start(f32[520,384]{1,0:T(8,128)} %collective-permute-done.2.refs_1_), channel_id=1, source_target_pairs={{0,224},{1,33},{32,0},{33,65},{64,32},{65,97},{96,64},{97,129},{12... | collective-permute-start | bytes 2396168 | tf_op jit(solution)/shard_map/ppermute | solution.py:352
  31.5 18.8 %collective-permute-start.1 = (f32[520,384]{1,0:T(8,128)}, f32[520,384]{1,0:T(8,128)}, u32[]{:S(2)}, u32[]{:S(2)}) collective-permute-start(f32[520,384]{1,0:T(8,128)} %collective-permute-done.refs_0_), channel_id=1, source_target_pairs={{0,32},{1,225},{32,64},{33,1},{64,96},{65,33},{96,128},{97,65},{12... | collective-permute-start | bytes 2396168 | tf_op jit(solution)/shard_map/ppermute | solution.py:352
  35.7 27.3 %all-to-all-start.1 = ((f32[8,2,64,384]{3,2,1,0:T(8,128)}), f32[8,2,64,384]{3,2,1,0:T(8,128)}, u32[]{:S(2)}, u32[]{:S(2)}) async-start(f32[8,2,64,384]{3,2,1,0:T(8,128)} %shard_map.80), calls=%async_computation.1 | async-start | bytes 3145728 | tf_op jit(solution)/shard_map/all_to_all | solution.py:366
  50.3 23.5 %collective-permute-start.4 = (f32[520,384]{1,0:T(8,128)}, f32[520,384]{1,0:T(8,128)}, u32[]{:S(2)}, u32[]{:S(2)}) collective-permute-start(f32[520,384]{1,0:T(8,128)} %get-tuple-element.18.refs_0_), channel_id=1, source_target_pairs={{0,32},{1,225},{32,64},{33,1},{64,96},{65,33},{96,128},{97,65},{12... | collective-permute-start | bytes 2396168 | tf_op jit(solution)/shard_map/ppermute | solution.py:352
  50.3 23.5 %collective-permute-start.5 = (f32[520,384]{1,0:T(8,128)}, f32[520,384]{1,0:T(8,128)}, u32[]{:S(2)}, u32[]{:S(2)}) collective-permute-start(f32[520,384]{1,0:T(8,128)} %get-tuple-element.19.refs_1_), channel_id=1, source_target_pairs={{0,224},{1,33},{32,0},{33,65},{64,32},{65,97},{96,64},{97,129},{12... | collective-permute-start | bytes 2396168 | tf_op jit(solution)/shard_map/ppermute | solution.py:352
  62.9 25.5 %all-to-all-start.2 = ((f32[8,2,64,384]{3,2,1,0:T(8,128)}), f32[8,2,64,384]{3,2,1,0:T(8,128)}, u32[]{:S(2)}, u32[]{:S(2)}) async-start(f32[8,2,64,384]{3,2,1,0:T(8,128)} %shard_map.86), calls=%async_computation.2 | async-start | bytes 3145728 | tf_op jit(solution)/shard_map/all_to_all | solution.py:366
  73.7 4.5 %collective-permute-start.9 = (f32[128,32,128]{2,1,0:T(8,128)}, f32[128,32,128]{2,1,0:T(8,128)}, u32[]{:S(2)}, u32[]{:S(2)}) collective-permute-start(f32[128,32,128]{2,1,0:T(8,128)} %shard_map.83.i2), channel_id=1, source_target_pairs={{0,1},{1,0},{2,3},{3,2},{4,5},{5,4},{6,7},{7,6},{8,9},{9,8},{10,11... | collective-permute-start | bytes 6291464 | tf_op jit(solution)/shard_map/ppermute | solution.py:347
  73.7 26.9 %collective-permute-start.6 = (f32[520,384]{1,0:T(8,128)}, f32[520,384]{1,0:T(8,128)}, u32[]{:S(2)}, u32[]{:S(2)}) collective-permute-start(f32[520,384]{1,0:T(8,128)} %get-tuple-element.20.refs_0_), channel_id=1, source_target_pairs={{0,32},{1,225},{32,64},{33,1},{64,96},{65,33},{96,128},{97,65},{12... | collective-permute-start | bytes 2396168 | tf_op jit(solution)/shard_map/ppermute | solution.py:352
  88.4 46.8 %all-to-all-start.3 = ((f32[8,2,64,384]{3,2,1,0:T(8,128)}), f32[8,2,64,384]{3,2,1,0:T(8,128)}, u32[]{:S(2)}, u32[]{:S(2)}) async-start(f32[8,2,64,384]{3,2,1,0:T(8,128)} %shard_map.90), calls=%async_computation.3 | async-start | bytes 3145728 | tf_op jit(solution)/shard_map/all_to_all | solution.py:364
  99.3 43.2 %collective-permute-start.17 = (f32[512,384]{1,0:T(8,128)}, f32[512,384]{1,0:T(8,128)}, u32[]{:S(2)}, u32[]{:S(2)}) collective-permute-start(f32[512,384]{1,0:T(8,128)} %shard_map.87.refs_1_), channel_id=1, source_target_pairs={{0,2},{2,0},{1,3},{3,1},{4,6},{6,4},{5,7},{7,5},{8,10},{10,8},{9,1... | collective-permute-start | bytes 2359304 | tf_op jit(solution)/shard_map/ppermute | solution.py:347
  104.3 25.0 %collective-permute-start.10 = (f32[64,384]{1,0:T(8,128)}, f32[64,384]{1,0:T(8,128)}, u32[]{:S(2)}, u32[]{:S(2)}) collective-permute-start(f32[64,384]{1,0:T(8,128)} %get-tuple-element.23), channel_id=1, source_target_pairs={{0,4},{4,8},{8,12},{12,0},{16,20},{20,24},{24,28},{28,16},{1,5},{5... | collective-permute-start | bytes 294920 | tf_op jit(solution)/shard_map/ppermute | solution.py:359
  105.8 23.4 %collective-permute-start.11 = (f32[64,384]{1,0:T(8,128)}, f32[64,384]{1,0:T(8,128)}, u32[]{:S(2)}, u32[]{:S(2)}) collective-permute-start(f32[64,384]{1,0:T(8,128)} %get-tuple-element.24), channel_id=1, source_target_pairs={{0,8},{4,12},{8,0},{12,4},{16,24},{20,28},{24,16},{28,20},{1,9},{5... | collective-permute-start | bytes 294920 | tf_op jit(solution)/shard_map/ppermute | solution.py:359
  106.7 28.5 %collective-permute-start.12 = (f32[64,384]{1,0:T(8,128)}, f32[64,384]{1,0:T(8,128)}, u32[]{:S(2)}, u32[]{:S(2)}) collective-permute-start(f32[64,384]{1,0:T(8,128)} %get-tuple-element.25), channel_id=1, source_target_pairs={{0,12},{4,0},{8,4},{12,8},{16,28},{20,16},{24,20},{28,24},{1,13},{... | collective-permute-start | bytes 294920 | tf_op jit(solution)/shard_map/ppermute | solution.py:359
  109.0 31.2 %collective-permute-start.13 = (f32[64,384]{1,0:T(8,128)}, f32[64,384]{1,0:T(8,128)}, u32[]{:S(2)}, u32[]{:S(2)}) collective-permute-start(f32[64,384]{1,0:T(8,128)} %get-tuple-element.26), channel_id=1, source_target_pairs={{0,16},{4,20},{8,24},{12,28},{16,0},{20,4},{24,8},{28,12},{1,17},{... | collective-permute-start | bytes 294920 | tf_op jit(solution)/shard_map/ppermute | solution.py:359
  129.2 11.0 %collective-permute-start.14 = (f32[64,384]{1,0:T(8,128)}, f32[64,384]{1,0:T(8,128)}, u32[]{:S(2)}, u32[]{:S(2)}) collective-permute-start(f32[64,384]{1,0:T(8,128)} %get-tuple-element.27), channel_id=1, source_target_pairs={{0,20},{4,24},{8,28},{12,16},{16,4},{20,8},{24,12},{28,0},{1,21},{... | collective-permute-start | bytes 294920 | tf_op jit(solution)/shard_map/ppermute | solution.py:359
  129.2 11.3 %collective-permute-start.15 = (f32[64,384]{1,0:T(8,128)}, f32[64,384]{1,0:T(8,128)}, u32[]{:S(2)}, u32[]{:S(2)}) collective-permute-start(f32[64,384]{1,0:T(8,128)} %get-tuple-element.28), channel_id=1, source_target_pairs={{0,24},{4,28},{8,16},{12,20},{16,8},{20,12},{24,0},{28,4},{1,25},{... | collective-permute-start | bytes 294920 | tf_op jit(solution)/shard_map/ppermute | solution.py:359
  135.2 7.3 %collective-permute-start.16 = (f32[64,384]{1,0:T(8,128)}, f32[64,384]{1,0:T(8,128)}, u32[]{:S(2)}, u32[]{:S(2)}) collective-permute-start(f32[64,384]{1,0:T(8,128)} %get-tuple-element.29), channel_id=1, source_target_pairs={{0,28},{4,16},{8,20},{12,24},{16,12},{20,0},{24,4},{28,8},{1,29},{... | collective-permute-start | bytes 294920 | tf_op jit(solution)/shard_map/ppermute | solution.py:359

commit v10 on v9

--- a/solution.py
+++ b/solution.py
@@ -260,11 +260,19 @@
     )(meta, *tiles, *(list(left) * len(tiles)))
 
 
-def last_kernel(*refs):
-    tiles, refs = refs[:PLANE], refs[PLANE:]
-    left_hi, left_lo, total, other, amp, row_gap, col_gap, res, new = refs
-    values = jnp.concatenate([tile[...] for tile in tiles], axis=0)
-    cycle = (total[...] + other[...] + product(left_hi[...], left_lo[...], values)).T
+def last_kernel(meta, *refs):
+    del meta
+    far, third, near, refs = refs[:PLANE], refs[PLANE], refs[PLANE + 1 : PLANE + 4], refs[PLANE + 4 :]
+    left_hi, left_lo, other, amp, row_gap, col_gap, res, new = refs
+    cols = amp.shape[0]
+    blocks = [third[...].reshape(-1, cols), near[0][...].reshape(-1, cols), near[1][...].reshape(-1, cols)]
+    blocks += [jnp.concatenate([tile[...] for tile in far], axis=0), near[2][...].reshape(-1, cols)]
+    total, start = other[...], 0
+    for block in blocks:
+        part = pl.ds(start, block.shape[0])
+        total = total + product(left_hi[:, part], left_lo[:, part], block)
+        start += block.shape[0]
+    cycle = total.T
     column = jnp.broadcast_to(col_gap[...], (8, col_gap.shape[1])).T[:, :1]
     gap = column + row_gap[...]
     amplitudes = amp[...]
@@ -273,39 +281,25 @@
     new[...] = amplitudes + residual / gap
 
 
-def last(offset, tiles, left, total, other, amp, row_gap, col_gap):
-    cols, rows = amp.shape
-    depth = PLANE * TILE
-    block = pl.BlockSpec((rows, depth), lambda g: (0, offset // depth))
-    shape = jax.ShapeDtypeStruct((cols, rows), jnp.float32)
-    rest = (total, other, amp, row_gap, col_gap)
+def last(meta, far, third, near, left, other, amp, row_gap, col_gap):
+    shape = jax.ShapeDtypeStruct(amp.shape, jnp.float32)
+    rest = (*left, other, amp, row_gap, col_gap)
+
+    def whole(x):
+        return pl.BlockSpec(x.shape, lambda g, meta: (0,) * x.ndim)
+
+    halves = [pl.BlockSpec((Y,) + t.shape[1:], lambda g, meta: (meta[1], 0, 0, 0)) for t in near]
     return pl.pallas_call(
         last_kernel,
-        grid=(1,),
         out_shape=(shape, shape),
-        in_specs=[full(t) for t in tiles] + [block, block] + [full(x) for x in rest],
-        out_specs=(full(shape), full(shape)),
-        compiler_params=PARAMS,
-    )(*tiles, *left, *rest)
-
-
-def more_kernel(tiles, left_hi, left_lo, total, out):
-    values = tiles[...].reshape(left_hi.shape[1], tiles.shape[-1])
-    out[...] = total[...] + product(left_hi[...], left_lo[...], values)
-
-
-def more(index, tiles, left, total, micros):
-    rows = left[0].shape[0]
-    block = pl.BlockSpec((rows, PLANE * tiles.shape[1] * TILE), lambda g: (0, index))
-    return pl.pallas_call(
-        more_kernel,
-        grid=(1,),
-        out_shape=jax.ShapeDtypeStruct(total.shape, jnp.float32),
-        in_specs=[full(tiles), block, block, full(total)],
-        out_specs=full(total),
-        compiler_params=PARAMS,
-        cost_estimate=cost(micros),
-    )(tiles, *left, total)
+        grid_spec=pltpu.PrefetchScalarGridSpec(
+            num_scalar_prefetch=1,
+            grid=(1,),
+            in_specs=[whole(x) for x in (*far, third)] + halves + [whole(x) for x in rest],
+            out_specs=(whole(amp), whole(amp)),
+        ),
+        compiler_params=PARAMS,
+    )(meta, *far, third, *near, *rest)
 
 
 def tie_kernel(*refs):
@@ -401,9 +395,7 @@
     pieces = (*tie([pieces[0]], [other]), *pieces[1:])
     other = swap(other, "xl")
     left = in_hbm(*prepare(OWNS, meta, task_slots, pieces, PREPARE_COSTS[1]))
-    total = steps(meta, mirrored, (1024, 1536, 2560), 0, left, OWN_COST)
-    total = more(0, received[3], left, total, MORE_COST)
-    return last(2048, received[4], left, total, other, amplitudes, row_gap[None, :], column_gap[None, :])
+    return last(meta, received[4], received[3], mirrored, left, other, amplitudes, row_gap[None, :], column_gap[None, :])
 
 
 def solution(mesh):

time: 148 us -> 162 us (1.095)
  waiting for transfers between devices: 24 us -> 41.2 us
  Pallas kernels: 68.3 us -> 63.9 us
    ppermute x7, waiting for transfers between devices: 2.36 us -> 19.2 us  [send(): return lax.ppermute(x, ('xh', 'y'), turns)]
    pallas_call x2 -> x1, Pallas kernels: 12 us -> 6.01 us  [steps(): pl.pallas_call(functools.partial(steps_kernel, len(tiles)), out_shape=sha...]
    all_to_all x3, waiting for transfers between devices: 7.99 us -> 4.54 us  [exchange(): lax.all_to_all(x, ('xh', 'y', 'xl'), 0, 0, axis_index_groups=groups, tile...]
    ppermute x4, waiting for transfers between devices: 5.71 us -> 8.43 us  [swap(): return lax.ppermute(x, axis, [(0, 1), (1, 0)])]
    pallas_call x2 -> x1, Pallas kernels: 9.68 us -> 11.2 us  [last(): pl.pallas_call(last_kernel, out_shape=(shape, shape), grid_spec=pltpu.Pre...]
  transfers between devices with their start and end apart: 22 -> 22, of which waited for: 8 -> 9; matrix products, arithmetic and copies ran while one was open for 1% -> 1% of each run, Pallas kernels for 42% -> 31%
where the time goes in v10:
time: 162 us; the launch traced here: 161 us
  Pallas kernels  63.9 us (39%)
  starting transfers between devices  53.2 us (33%)
  waiting for transfers between devices  41.2 us (25%)
  local copies, waits for them, and re-layouts  1.91 us (1%)
    ppermute x7, waiting for transfers between devices, send(): return lax.ppermute(x, ('xh', 'y'), turns)  19.2 us
    all_to_all x3, starting transfers between devices, exchange(): lax.all_to_all(x, ('xh', 'y', 'xl'), 0, 0, axis_index_groups=groups, tile...  19.2 us
    pallas_call x2, Pallas kernels, prepare(): pl.pallas_call(functools.partial(prepare_kernel, owners), grid=(len(owner...  18.1 us
    pallas_call x4, Pallas kernels, select(): pl.pallas_call(functools.partial(select_kernel, owners), compiler_params=...  16.2 us
    ppermute x7, starting transfers between devices, send(): return lax.ppermute(x, ('xh', 'y'), turns)  14.9 us
    ppermute x7, starting transfers between devices, shift(): return lax.ppermute(x, ('z', 'co'), turns)  12.6 us
    pallas_call x1, Pallas kernels, last(): pl.pallas_call(last_kernel, out_shape=(shape, shape), grid_spec=pltpu.Pre...  11.2 us
    ppermute x7, waiting for transfers between devices, shift(): return lax.ppermute(x, ('z', 'co'), turns)  9 us
  transfers between devices with their start and end apart: 22, of which 9 were waited for; matrix products, arithmetic and copies ran while one was open for 1% of the time, Pallas kernels for 31%

profile of v10, /device:TPU:8, one launch (start us, length us, event | category | flops | bytes accessed | tf_op | source)
XLA Modules:
  0.0 160.9 jit_solution(14248743856690365492)
XLA Ops:
  0.6 2.3 %shard_map.77.refs_0_ = f32[520,384]{1,0:T(8,128)} custom-call(f32[384,512]{1,0:T(8,128)} %refs_15_.1, s32[1,64]{1,0:T(1,128)} %send.1), custom_call_target="tpu_custom_call" | custom-call | tf_op jit(solution)/shard_map/pallas_call | solution.py:60
  2.9 2.0 %collective-permute-start = (f32[520,384]{1,0:T(8,128)}, f32[520,384]{1,0:T(8,128)}, u32[]{:S(2)}, u32[]{:S(2)}) collective-permute-start(f32[520,384]{1,0:T(8,128)} %shard_map.77.refs_0_), channel_id=1, source_target_pairs={{0,32},{1,225},{32,64},{33,1},{64,96},{65,33},{96,128},{97,65},{12... | collective-permute-start | bytes 2396168 | tf_op jit(solution)/shard_map/ppermute | solution.py:346
  4.9 4.0 %collective-permute-start.2 = (f32[520,384]{1,0:T(8,128)}, f32[520,384]{1,0:T(8,128)}, u32[]{:S(2)}, u32[]{:S(2)}) collective-permute-start(f32[520,384]{1,0:T(8,128)} %shard_map.77.refs_0_), channel_id=1, source_target_pairs={{0,224},{1,33},{32,0},{33,65},{64,32},{65,97},{96,64},{97,129},{12... | collective-permute-start | bytes 2396168 | tf_op jit(solution)/shard_map/ppermute | solution.py:346
  9.0 0.7 stack.23.meta
  9.6 3.6 %shard_map.78.after = f32[8,1,64,384]{3,2,1,0:T(8,128)} custom-call(s32[5]{0:T(128)} %stack.23.meta, f32[520,384]{1,0:T(8,128)} %shard_map.77.refs_0_), custom_call_target="tpu_custom_call" | custom-call | flops 40000000000 | tf_op jit(solution)/shard_map/pallas_call | solution.py:95
  13.2 7.1 %all-to-all-start = ((f32[8,1,64,384]{3,2,1,0:T(8,128)}), f32[8,1,64,384]{3,2,1,0:T(8,128)}, u32[]{:S(2)}, u32[]{:S(2)}) async-start(f32[8,1,64,384]{3,2,1,0:T(8,128)} %shard_map.78.after), calls=%async_computation | async-start | bytes 1572864 | tf_op jit(solution)/shard_map/all_to_all | solution.py:360
  20.3 6.5 %shard_map.82.i0.refs_0_ = f32[128,32,128]{2,1,0:T(8,128)} custom-call(f32[8,16,64,64]{3,2,1,0:T(8,128)} %integrals.1, f32[8,1,64,384]{3,2,1,0:T(8,128)} %shard_map.78.after), custom_call_target="tpu_custom_call" | custom-call | flops 40000000000 | tf_op jit(solution)/shard_map/pallas_call | solution.py:329
  26.8 0.0 collective-permute-start.7
  26.8 0.2 collective-permute-start.8
  27.1 1.3 broadcast_in_dim.7.refs_17_
  28.3 0.0 collective-permute-done.refs_0_
  28.3 0.0 collective-permute-start.1
  28.3 0.0 collective-permute-done.2.refs_1_
  28.3 3.2 %collective-permute-start.3 = (f32[520,384]{1,0:T(8,128)}, f32[520,384]{1,0:T(8,128)}, u32[]{:S(2)}, u32[]{:S(2)}) collective-permute-start(f32[520,384]{1,0:T(8,128)} %collective-permute-done.2.refs_1_), channel_id=1, source_target_pairs={{0,224},{1,33},{32,0},{33,65},{64,32},{65,97},{96,64},{97,129},{12... | collective-permute-start | bytes 2396168 | tf_op jit(solution)/shard_map/ppermute | solution.py:346
  31.6 4.2 %shard_map.80 = f32[8,2,64,384]{3,2,1,0:T(8,128)} custom-call(s32[5]{0:T(128)} %stack.23.meta, f32[520,384]{1,0:T(8,128)} %collective-permute-done.refs_0_, f32[520,384]{1,0:T(8,128)} %collective-permute-done.2.refs_1_), custom_call_target="tpu_custom_call" | custom-call | flops 40000000000 | tf_op jit(solution)/shard_map/pallas_call | solution.py:95
  35.7 0.0 all-to-all-done.refs_2_.refs_11_
  35.8 6.7 %all-to-all-start.1 = ((f32[8,2,64,384]{3,2,1,0:T(8,128)}), f32[8,2,64,384]{3,2,1,0:T(8,128)}, u32[]{:S(2)}, u32[]{:S(2)}) async-start(f32[8,2,64,384]{3,2,1,0:T(8,128)} %shard_map.80), calls=%async_computation.1 | async-start | bytes 3145728 | tf_op jit(solution)/shard_map/all_to_all | solution.py:360
  42.5 7.1 %collective-permute-done.1.refs_0_ = f32[520,384]{1,0:T(8,128)} collective-permute-done((f32[520,384]{1,0:T(8,128)}, f32[520,384]{1,0:T(8,128)}, u32[]{:S(2)}, u32[]{:S(2)}) %collective-permute-start.1) | collective-permute-done | bytes 798752 | tf_op jit(solution)/shard_map/ppermute | solution.py:346
  49.6 0.0 collective-permute-done.3.refs_1_
  49.6 0.0 collective-permute-start.4
  49.6 3.2 %collective-permute-start.5 = (f32[520,384]{1,0:T(8,128)}, f32[520,384]{1,0:T(8,128)}, u32[]{:S(2)}, u32[]{:S(2)}) collective-permute-start(f32[520,384]{1,0:T(8,128)} %get-tuple-element.19.refs_1_), channel_id=1, source_target_pairs={{0,224},{1,33},{32,0},{33,65},{64,32},{65,97},{96,64},{97,129},{12... | collective-permute-start | bytes 2396168 | tf_op jit(solution)/shard_map/ppermute | solution.py:346
  52.8 4.2 %shard_map.87 = f32[8,2,64,384]{3,2,1,0:T(8,128)} custom-call(s32[5]{0:T(128)} %stack.23.meta, f32[520,384]{1,0:T(8,128)} %get-tuple-element.18.refs_0_, f32[520,384]{1,0:T(8,128)} %get-tuple-element.19.refs_1_), custom_call_target="tpu_custom_call" | custom-call | flops 40000000000 | tf_op jit(solution)/shard_map/pallas_call | solution.py:95
  57.0 4.5 %all-to-all-done.1.refs_2_.refs_1_.refs_0_.refs_9_ = f32[8,2,64,384]{3,2,1,0:T(8,128)} async-done(((f32[8,2,64,384]{3,2,1,0:T(8,128)}), f32[8,2,64,384]{3,2,1,0:T(8,128)}, u32[]{:S(2)}, u32[]{:S(2)}) %all-to-all-start.1) | async-done | bytes 1572896 | tf_op jit(solution)/shard_map/all_to_all | solution.py:360
  61.6 5.4 %all-to-all-start.3 = ((f32[8,2,64,384]{3,2,1,0:T(8,128)}), f32[8,2,64,384]{3,2,1,0:T(8,128)}, u32[]{:S(2)}, u32[]{:S(2)}) async-start(f32[8,2,64,384]{3,2,1,0:T(8,128)} %shard_map.87), calls=%async_computation.3 | async-start | bytes 3145728 | tf_op jit(solution)/shard_map/all_to_all | solution.py:360
  66.9 8.3 %collective-permute-done.8.refs_0_ = f32[128,32,128]{2,1,0:T(8,128)} collective-permute-done((f32[128,32,128]{2,1,0:T(8,128)}, f32[128,32,128]{2,1,0:T(8,128)}, u32[]{:S(2)}, u32[]{:S(2)}) %collective-permute-start.8) | collective-permute-done | bytes 2097184 | tf_op jit(solution)/shard_map/ppermute | solution.py:341
  75.2 0.0 collective-permute-start.9
  75.2 0.0 collective-permute-done.4.refs_0_
  75.2 0.0 collective-permute-done.5.refs_1_
  75.2 0.1 collective-permute-start.6
  75.3 4.2 %shard_map.86 = f32[8,2,64,384]{3,2,1,0:T(8,128)} custom-call(s32[5]{0:T(128)} %stack.23.meta, f32[520,384]{1,0:T(8,128)} %get-tuple-element.20.refs_0_, f32[520,384]{1,0:T(8,128)} %get-tuple-element.30.refs_1_), custom_call_target="tpu_custom_call" | custom-call | flops 15000000512 | tf_op jit(solution)/shard_map/pallas_call | solution.py:95
  79.5 0.0 collective-permute-done.7.i1
  79.5 0.2 collective-permute-done.9.i3
  79.7 7.3 %shard_map.84 = (bf16[512,1280]{1,0:T(8,128)(2,1)}, bf16[512,1280]{1,0:T(8,128)(2,1)}) custom-call(s32[5]{0:T(128)} %stack.23.meta, s32[8,64]{1,0:T(8,128)} %slots.3, f32[128,32,128]{2,1,0:T(8,128)} %shard_map.82.i0.refs_0_, f32[128,32,128]{2,1,0:T(8,128)} %collective-permute-done.7.i1, f32[128,32,128]{2,1,0:T(8,128)} %shard_map.83.i2, ...), custom_call_target="tpu_custom_call" | custom-call | flops 10000000000 | tf_op jit(solution)/shard_map/pallas_call | solution.py:202
  87.1 1.9 %collective-permute-done.6.source = f32[520,384]{1,0:T(8,128)} collective-permute-done((f32[520,384]{1,0:T(8,128)}, f32[520,384]{1,0:T(8,128)}, u32[]{:S(2)}, u32[]{:S(2)}) %collective-permute-start.6) | collective-permute-done | bytes 798752 | tf_op jit(solution)/shard_map/ppermute | solution.py:346
  88.9 3.6 %shard_map.85 = (f32[64,384]{1,0:T(8,128)}, f32[64,384]{1,0:T(8,128)}, f32[64,384]{1,0:T(8,128)}, f32[64,384]{1,0:T(8,128)}, f32[64,384]{1,0:T(8,128)}, /*index=...) custom-call(s32[5]{0:T(128)} %stack.23.meta, f32[520,384]{1,0:T(8,128)} %collective-permute-done.6.source, ...), custom_call_target="tpu_custom_call" | custom-call | flops 30000001024 | tf_op jit(solution)/shard_map/pallas_call | solution.py:125
  92.5 1.5 collective-permute-start.10
  94.1 0.7 collective-permute-start.11
  94.8 2.5 %collective-permute-start.12 = (f32[64,384]{1,0:T(8,128)}, f32[64,384]{1,0:T(8,128)}, u32[]{:S(2)}, u32[]{:S(2)}) collective-permute-start(f32[64,384]{1,0:T(8,128)} %get-tuple-element.25), channel_id=1, source_target_pairs={{0,12},{4,0},{8,4},{12,8},{16,28},{20,16},{24,20},{28,24},{1,13},{... | collective-permute-start | bytes 294920 | tf_op jit(solution)/shard_map/ppermute | solution.py:353
  97.3 0.0 all-to-all-done.3.refs_1_.refs_10_
  97.3 5.6 %all-to-all-start.2 = ((f32[8,2,64,384]{3,2,1,0:T(8,128)}), f32[8,2,64,384]{3,2,1,0:T(8,128)}, u32[]{:S(2)}, u32[]{:S(2)}) async-start(f32[8,2,64,384]{3,2,1,0:T(8,128)} %shard_map.86), calls=%async_computation.2 | async-start | bytes 3145728 | tf_op jit(solution)/shard_map/all_to_all | solution.py:358
  102.9 6.0 %shard_map.88.refs_1_ = f32[512,384]{1,0:T(8,128)} custom-call(s32[5]{0:T(128)} %stack.23.meta, f32[8,2,64,384]{3,2,1,0:T(8,128)} %all-to-all-done.1.refs_2_.refs_1_.refs_0_.refs_9_, f32[8,2,64,384]{3,2,1,0:T(8,128)} %all-to-all-done.3.refs_1_.refs_10_, f32[8,1,64,384]{3,2,1,0:T(8,128)} %all-to-all-done.refs_2_.refs_11_, ...), custom_call_target="tpu_custom_call" | custom-call | flops 3000000000 | tf_op jit(solution)/shard_map/pallas_call | solution.py:249
  108.9 0.6 collective-permute-start.17
  109.6 3.6 %collective-permute-start.13 = (f32[64,384]{1,0:T(8,128)}, f32[64,384]{1,0:T(8,128)}, u32[]{:S(2)}, u32[]{:S(2)}) collective-permute-start(f32[64,384]{1,0:T(8,128)} %get-tuple-element.26), channel_id=1, source_target_pairs={{0,16},{4,20},{8,24},{12,28},{16,0},{20,4},{24,8},{28,12},{1,17},{... | collective-permute-start | bytes 294920 | tf_op jit(solution)/shard_map/ppermute | solution.py:353
  113.2 0.0 collective-permute-done.10.refs_1_
  113.2 0.9 collective-permute-start.14
  114.1 0.0 collective-permute-done.11.refs_2_
  114.1 4.1 %collective-permute-start.15 = (f32[64,384]{1,0:T(8,128)}, f32[64,384]{1,0:T(8,128)}, u32[]{:S(2)}, u32[]{:S(2)}) collective-permute-start(f32[64,384]{1,0:T(8,128)} %get-tuple-element.28), channel_id=1, source_target_pairs={{0,24},{4,28},{8,16},{12,20},{16,8},{20,12},{24,0},{28,4},{1,25},{... | collective-permute-start | bytes 294920 | tf_op jit(solution)/shard_map/ppermute | solution.py:353
  118.2 0.0 collective-permute-done.12.refs_3_
  118.2 1.5 collective-permute-start.16
  119.7 10.8 %shard_map.90 = (bf16[512,2816]{1,0:T(8,128)(2,1)}, bf16[512,2816]{1,0:T(8,128)(2,1)}) custom-call(s32[5]{0:T(128)} %stack.23.meta, s32[8,64]{1,0:T(8,128)} %slots.3, f32[128,32,128]{2,1,0:T(8,128)} %shard_map.89.i0, f32[128,32,128]{2,1,0:T(8,128)} %collective-permute-done.7.i1, f32[128,32,128]{2,1,0:T(8,128)} %shard_map.83.i2, ...), custom_call_target="tpu_custom_call" | custom-call | flops 10000000000 | tf_op jit(solution)/shard_map/pallas_call | solution.py:202
  130.5 0.0 all-to-all-done.2.refs_8_
  130.5 13.2 %collective-permute-done.13.refs_4_ = f32[64,384]{1,0:T(8,128)} collective-permute-done((f32[64,384]{1,0:T(8,128)}, f32[64,384]{1,0:T(8,128)}, u32[]{:S(2)}, u32[]{:S(2)}) %collective-permute-start.13) | collective-permute-done | bytes 98336 | tf_op jit(solution)/shard_map/ppermute | solution.py:353
  143.6 2.1 %collective-permute-done.14.refs_5_ = f32[64,384]{1,0:T(8,128)} collective-permute-done((f32[64,384]{1,0:T(8,128)}, f32[64,384]{1,0:T(8,128)}, u32[]{:S(2)}, u32[]{:S(2)}) %collective-permute-start.14) | collective-permute-done | bytes 98336 | tf_op jit(solution)/shard_map/ppermute | solution.py:353
  145.8 3.4 %collective-permute-done.15.refs_6_ = f32[64,384]{1,0:T(8,128)} collective-permute-done((f32[64,384]{1,0:T(8,128)}, f32[64,384]{1,0:T(8,128)}, u32[]{:S(2)}, u32[]{:S(2)}) %collective-permute-start.15) | collective-permute-done | bytes 98336 | tf_op jit(solution)/shard_map/ppermute | solution.py:353
  149.2 0.5 collective-permute-done.16.refs_7_
  149.7 0.0 collective-permute-done.17.refs_14_
  149.7 11.2 %shard_map.91 = (f32[384,512]{1,0:T(8,128)}, f32[384,512]{1,0:T(8,128)}) custom-call(s32[5]{0:T(128)} %stack.23.meta, f32[64,384]{1,0:T(8,128)} %get-tuple-element.22.refs_0_, f32[64,384]{1,0:T(8,128)} %collective-permute-done.10.refs_1_, f32[64,384]{1,0:T(8,128)} %collective-permute-done.11.refs_2_, f32[64,384]{1,0:T(8,128)} %collective-permute-done.12.refs_3_, ...), custom_call_target="tpu_custom_call" | custom-call | tf_op jit(solution)/shard_map/pallas_call | solution.py:292
  (4 shorter events, 0.0 us)
Async XLA Ops:
  2.9 25.4 %collective-permute-start = (f32[520,384]{1,0:T(8,128)}, f32[520,384]{1,0:T(8,128)}, u32[]{:S(2)}, u32[]{:S(2)}) collective-permute-start(f32[520,384]{1,0:T(8,128)} %shard_map.77.refs_0_), channel_id=1, source_target_pairs={{0,32},{1,225},{32,64},{33,1},{64,96},{65,33},{96,128},{97,65},{12... | collective-permute-start | bytes 2396168 | tf_op jit(solution)/shard_map/ppermute | solution.py:346
  4.9 23.4 %collective-permute-start.2 = (f32[520,384]{1,0:T(8,128)}, f32[520,384]{1,0:T(8,128)}, u32[]{:S(2)}, u32[]{:S(2)}) collective-permute-start(f32[520,384]{1,0:T(8,128)} %shard_map.77.refs_0_), channel_id=1, source_target_pairs={{0,224},{1,33},{32,0},{33,65},{64,32},{65,97},{96,64},{97,129},{12... | collective-permute-start | bytes 2396168 | tf_op jit(solution)/shard_map/ppermute | solution.py:346
  13.2 22.6 %all-to-all-start = ((f32[8,1,64,384]{3,2,1,0:T(8,128)}), f32[8,1,64,384]{3,2,1,0:T(8,128)}, u32[]{:S(2)}, u32[]{:S(2)}) async-start(f32[8,1,64,384]{3,2,1,0:T(8,128)} %shard_map.78.after), calls=%async_computation | async-start | bytes 1572864 | tf_op jit(solution)/shard_map/all_to_all | solution.py:360
  26.8 52.7 %collective-permute-start.7 = (f32[128,32,128]{2,1,0:T(8,128)}, f32[128,32,128]{2,1,0:T(8,128)}, u32[]{:S(2)}, u32[]{:S(2)}) collective-permute-start(f32[128,32,128]{2,1,0:T(8,128)} %shard_map.82.i0.refs_0_), channel_id=1, source_target_pairs={{0,1},{1,0},{2,3},{3,2},{4,5},{5,4},{6,7},{7,6},{8,9},{9,8},{10,11... | collective-permute-start | bytes 6291464 | tf_op jit(solution)/shard_map/ppermute | solution.py:341
  26.8 48.4 %collective-permute-start.8 = (f32[128,32,128]{2,1,0:T(8,128)}, f32[128,32,128]{2,1,0:T(8,128)}, u32[]{:S(2)}, u32[]{:S(2)}) collective-permute-start(f32[128,32,128]{2,1,0:T(8,128)} %shard_map.82.i0.refs_0_), channel_id=1, source_target_pairs={{0,2},{2,0},{1,3},{3,1},{4,6},{6,4},{5,7},{7,5},{8,10},{10,8},{9,1... | collective-permute-start | bytes 6291464 | tf_op jit(solution)/shard_map/ppermute | solution.py:341
  28.3 21.2 %collective-permute-start.1 = (f32[520,384]{1,0:T(8,128)}, f32[520,384]{1,0:T(8,128)}, u32[]{:S(2)}, u32[]{:S(2)}) collective-permute-start(f32[520,384]{1,0:T(8,128)} %collective-permute-done.refs_0_), channel_id=1, source_target_pairs={{0,32},{1,225},{32,64},{33,1},{64,96},{65,33},{96,128},{97,65},{12... | collective-permute-start | bytes 2396168 | tf_op jit(solution)/shard_map/ppermute | solution.py:346
  28.3 21.2 %collective-permute-start.3 = (f32[520,384]{1,0:T(8,128)}, f32[520,384]{1,0:T(8,128)}, u32[]{:S(2)}, u32[]{:S(2)}) collective-permute-start(f32[520,384]{1,0:T(8,128)} %collective-permute-done.2.refs_1_), channel_id=1, source_target_pairs={{0,224},{1,33},{32,0},{33,65},{64,32},{65,97},{96,64},{97,129},{12... | collective-permute-start | bytes 2396168 | tf_op jit(solution)/shard_map/ppermute | solution.py:346
  35.8 25.8 %all-to-all-start.1 = ((f32[8,2,64,384]{3,2,1,0:T(8,128)}), f32[8,2,64,384]{3,2,1,0:T(8,128)}, u32[]{:S(2)}, u32[]{:S(2)}) async-start(f32[8,2,64,384]{3,2,1,0:T(8,128)} %shard_map.80), calls=%async_computation.1 | async-start | bytes 3145728 | tf_op jit(solution)/shard_map/all_to_all | solution.py:360
  49.6 25.6 %collective-permute-start.4 = (f32[520,384]{1,0:T(8,128)}, f32[520,384]{1,0:T(8,128)}, u32[]{:S(2)}, u32[]{:S(2)}) collective-permute-start(f32[520,384]{1,0:T(8,128)} %get-tuple-element.18.refs_0_), channel_id=1, source_target_pairs={{0,32},{1,225},{32,64},{33,1},{64,96},{65,33},{96,128},{97,65},{12... | collective-permute-start | bytes 2396168 | tf_op jit(solution)/shard_map/ppermute | solution.py:346
  49.6 25.6 %collective-permute-start.5 = (f32[520,384]{1,0:T(8,128)}, f32[520,384]{1,0:T(8,128)}, u32[]{:S(2)}, u32[]{:S(2)}) collective-permute-start(f32[520,384]{1,0:T(8,128)} %get-tuple-element.19.refs_1_), channel_id=1, source_target_pairs={{0,224},{1,33},{32,0},{33,65},{64,32},{65,97},{96,64},{97,129},{12... | collective-permute-start | bytes 2396168 | tf_op jit(solution)/shard_map/ppermute | solution.py:346
  61.6 35.7 %all-to-all-start.3 = ((f32[8,2,64,384]{3,2,1,0:T(8,128)}), f32[8,2,64,384]{3,2,1,0:T(8,128)}, u32[]{:S(2)}, u32[]{:S(2)}) async-start(f32[8,2,64,384]{3,2,1,0:T(8,128)} %shard_map.87), calls=%async_computation.3 | async-start | bytes 3145728 | tf_op jit(solution)/shard_map/all_to_all | solution.py:360
  75.2 4.5 %collective-permute-start.9 = (f32[128,32,128]{2,1,0:T(8,128)}, f32[128,32,128]{2,1,0:T(8,128)}, u32[]{:S(2)}, u32[]{:S(2)}) collective-permute-start(f32[128,32,128]{2,1,0:T(8,128)} %shard_map.83.i2), channel_id=1, source_target_pairs={{0,1},{1,0},{2,3},{3,2},{4,5},{5,4},{6,7},{7,6},{8,9},{9,8},{10,11... | collective-permute-start | bytes 6291464 | tf_op jit(solution)/shard_map/ppermute | solution.py:341
  75.2 13.7 %collective-permute-start.6 = (f32[520,384]{1,0:T(8,128)}, f32[520,384]{1,0:T(8,128)}, u32[]{:S(2)}, u32[]{:S(2)}) collective-permute-start(f32[520,384]{1,0:T(8,128)} %get-tuple-element.20.refs_0_), channel_id=1, source_target_pairs={{0,32},{1,225},{32,64},{33,1},{64,96},{65,33},{96,128},{97,65},{12... | collective-permute-start | bytes 2396168 | tf_op jit(solution)/shard_map/ppermute | solution.py:346
  92.5 20.6 %collective-permute-start.10 = (f32[64,384]{1,0:T(8,128)}, f32[64,384]{1,0:T(8,128)}, u32[]{:S(2)}, u32[]{:S(2)}) collective-permute-start(f32[64,384]{1,0:T(8,128)} %get-tuple-element.23), channel_id=1, source_target_pairs={{0,4},{4,8},{8,12},{12,0},{16,20},{20,24},{24,28},{28,16},{1,5},{5... | collective-permute-start | bytes 294920 | tf_op jit(solution)/shard_map/ppermute | solution.py:353
  94.1 20.0 %collective-permute-start.11 = (f32[64,384]{1,0:T(8,128)}, f32[64,384]{1,0:T(8,128)}, u32[]{:S(2)}, u32[]{:S(2)}) collective-permute-start(f32[64,384]{1,0:T(8,128)} %get-tuple-element.24), channel_id=1, source_target_pairs={{0,8},{4,12},{8,0},{12,4},{16,24},{20,28},{24,16},{28,20},{1,9},{5... | collective-permute-start | bytes 294920 | tf_op jit(solution)/shard_map/ppermute | solution.py:353
  94.8 23.4 %collective-permute-start.12 = (f32[64,384]{1,0:T(8,128)}, f32[64,384]{1,0:T(8,128)}, u32[]{:S(2)}, u32[]{:S(2)}) collective-permute-start(f32[64,384]{1,0:T(8,128)} %get-tuple-element.25), channel_id=1, source_target_pairs={{0,12},{4,0},{8,4},{12,8},{16,28},{20,16},{24,20},{28,24},{1,13},{... | collective-permute-start | bytes 294920 | tf_op jit(solution)/shard_map/ppermute | solution.py:353
  97.3 33.2 %all-to-all-start.2 = ((f32[8,2,64,384]{3,2,1,0:T(8,128)}), f32[8,2,64,384]{3,2,1,0:T(8,128)}, u32[]{:S(2)}, u32[]{:S(2)}) async-start(f32[8,2,64,384]{3,2,1,0:T(8,128)} %shard_map.86), calls=%async_computation.2 | async-start | bytes 3145728 | tf_op jit(solution)/shard_map/all_to_all | solution.py:358
  108.9 40.8 %collective-permute-start.17 = (f32[512,384]{1,0:T(8,128)}, f32[512,384]{1,0:T(8,128)}, u32[]{:S(2)}, u32[]{:S(2)}) collective-permute-start(f32[512,384]{1,0:T(8,128)} %shard_map.88.refs_1_), channel_id=1, source_target_pairs={{0,2},{2,0},{1,3},{3,1},{4,6},{6,4},{5,7},{7,5},{8,10},{10,8},{9,1... | collective-permute-start | bytes 2359304 | tf_op jit(solution)/shard_map/ppermute | solution.py:341
  109.6 34.1 %collective-permute-start.13 = (f32[64,384]{1,0:T(8,128)}, f32[64,384]{1,0:T(8,128)}, u32[]{:S(2)}, u32[]{:S(2)}) collective-permute-start(f32[64,384]{1,0:T(8,128)} %get-tuple-element.26), channel_id=1, source_target_pairs={{0,16},{4,20},{8,24},{12,28},{16,0},{20,4},{24,8},{28,12},{1,17},{... | collective-permute-start | bytes 294920 | tf_op jit(solution)/shard_map/ppermute | solution.py:353
  113.2 32.6 %collective-permute-start.14 = (f32[64,384]{1,0:T(8,128)}, f32[64,384]{1,0:T(8,128)}, u32[]{:S(2)}, u32[]{:S(2)}) collective-permute-start(f32[64,384]{1,0:T(8,128)} %get-tuple-element.27), channel_id=1, source_target_pairs={{0,20},{4,24},{8,28},{12,16},{16,4},{20,8},{24,12},{28,0},{1,21},{... | collective-permute-start | bytes 294920 | tf_op jit(solution)/shard_map/ppermute | solution.py:353
  114.1 35.2 %collective-permute-start.15 = (f32[64,384]{1,0:T(8,128)}, f32[64,384]{1,0:T(8,128)}, u32[]{:S(2)}, u32[]{:S(2)}) collective-permute-start(f32[64,384]{1,0:T(8,128)} %get-tuple-element.28), channel_id=1, source_target_pairs={{0,24},{4,28},{8,16},{12,20},{16,8},{20,12},{24,0},{28,4},{1,25},{... | collective-permute-start | bytes 294920 | tf_op jit(solution)/shard_map/ppermute | solution.py:353
  118.2 31.5 %collective-permute-start.16 = (f32[64,384]{1,0:T(8,128)}, f32[64,384]{1,0:T(8,128)}, u32[]{:S(2)}, u32[]{:S(2)}) collective-permute-start(f32[64,384]{1,0:T(8,128)} %get-tuple-element.29), channel_id=1, source_target_pairs={{0,28},{4,16},{8,20},{12,24},{16,12},{20,0},{24,4},{28,8},{1,29},{... | collective-permute-start | bytes 294920 | tf_op jit(solution)/shard_map/ppermute | solution.py:353
